TPU v7x, 32 devices: a whole 2x2x4 slice. The times are simulated.
32 devices in a mesh: seq: 8 (over z, y), batch: 4 (over x, core).
Axes of the slice: x: 2, y: 2, z: 4, core: 2. Of those that a mesh axis runs over, the one named last changes fastest.
Arguments:
- token_ids: int32 [32768], P(('batch', 'seq')), parts along dimension 0, may hold values from 0 to 4
- embed_table: bfloat16 [5, 256], replicated, may hold values from -6 to 6
- input_weight_matrix: bfloat16 [256, 1064], replicated, may hold values from -0.375 to 0.375
- output_weight_matrix: bfloat16 [512, 256], replicated, may hold values from -0.25 to 0.25
- conv_weight: float32 [2, 4, 512], replicated, may hold values from -3 to 3
- dt_bias: float32 [2, 8], replicated, may hold values from -1 to 1
- decay_rate: float32 [2, 8], replicated, may hold values from 0 to 0.05
- skip_gain: float32 [2, 8], replicated, may hold values from -4 to 4
- norm_gain: float32 [2, 512], replicated, may hold values from 0.1 to 1.9
Outputs:
- hidden: bfloat16 [32768, 256], P(('batch', 'seq')), parts along dimension 0
There are 4 independent parts, one for each index of `batch`. A program takes and returns all parts, laid end to end along the dimension named above; an argument that names none is the same for every part. Nothing has to cross between parts.
All inputs are finite; a program needn't handle non-finite values.
Results may differ from a plain program's by a relative error of at most 0.0029.
The roundings to bfloat16 on the way count: a program that leaves them out, or rounds other values in their place, can miss the bound.
Values may be sent and summed in bfloat16 or wider, within the bound.
No kernel may reach another device: no remote copies, remote signals or barrier semaphores. Data moves between devices by JAX's collectives and lax.ppermute only.
A program may use at most 128 MiB of HBM per device.

v0:
```python
import jax
import jax.numpy as jnp
from jax import lax
from jax.sharding import PartitionSpec as P

E = 512
NS = 16
P_SIZE = 64
KW = 4
BLK = 128
H = 8


EPSILON = 1e-05


def carried_in(value, axis, join, neutral, backward):
    count, mine = (lax.axis_size(axis), lax.axis_index(axis))
    pieces = jax.tree.map(lambda part: lax.all_gather(part, axis), value)
    if backward:
        pieces = jax.tree.map(lambda part: part[::-1], pieces)
        mine = count - 1 - mine
    running = jax.tree.map(
        lambda part, zero: jnp.full_like(part, 0) + jnp.asarray(zero, part.dtype), value, neutral
    )

    def hop(position, running):
        longer = join(running, jax.tree.map(lambda part: part[position], pieces))
        return jax.tree.map(lambda new, old: jnp.where(position < mine, new, old), longer, running)

    return lax.fori_loop(0, count - 1, hop, running)


def swapped(block, axis, bit):
    count = lax.axis_size(axis)
    route = []
    for low in range(count):
        high = low | 1 << bit
        if high != low and high < count:
            route += [(low, high), (high, low)]
    return lax.ppermute(block, axis, route)


def padded(cells, sides, width):
    for axis, dim in sides:
        count = lax.axis_size(axis)
        ends = count - 1
        head = lax.slice_in_dim(cells, 0, width, axis=dim)
        tail = lax.slice_in_dim(cells, cells.shape[dim] - width, cells.shape[dim], axis=dim)
        cells = jnp.concatenate(
            [
                lax.ppermute(tail, axis, [(i, (i + 1) % count) for i in range(ends)]),
                cells,
                lax.ppermute(head, axis, [((i + 1) % count, i) for i in range(ends)]),
            ],
            axis=dim,
        )
    return cells


def complement(ids):
    return jnp.where(ids < 4, 3 - ids, ids)


def embed_rows(ids, embed_table):
    onehot = (ids[:, None] == jnp.arange(5, dtype=jnp.int32)[None, :]).astype(jnp.bfloat16)
    return jnp.dot(onehot, embed_table, preferred_element_type=jnp.float32).astype(jnp.bfloat16)


def block_step(state, pieces):
    highest = lax.Precision.HIGHEST
    inner_x, log_decay, step, b_part, c_part = pieces
    count = log_decay.shape[0]
    cumul = jnp.cumsum(log_decay, axis=0)
    index = jnp.arange(count)
    lower = index[:, None] >= index[None, :]
    spread = cumul[:, None, :] - cumul[None, :, :]
    decay = jnp.exp(jnp.where(lower[:, :, None], spread, -1e30))
    scores = jnp.dot(c_part, b_part.T, precision=highest)
    weighted = inner_x * step[:, :, None]
    inner = jnp.einsum("trh,rhp->thp", scores[:, :, None] * decay, weighted, precision=highest)
    carried = jnp.exp(cumul)[:, :, None] * jnp.einsum(
        "tn,hpn->thp", c_part, state, precision=highest
    )
    tail = jnp.exp(cumul[-1][None, :] - cumul)
    new_state = jnp.exp(cumul[-1])[:, None, None] * state + jnp.einsum(
        "rh,rhp,rn->hpn", tail, weighted, b_part, precision=highest
    )
    return (new_state, inner + carried)


def join_carry(earlier, later):
    return (earlier[0] * later[0], earlier[1] * later[0][:, :, None, None] + later[1])


def processor_sequence(inner_x, log_decay, step, b_part, c_part, backward):
    if backward:
        inner_x = jnp.flip(inner_x, axis=1)
        log_decay = jnp.flip(log_decay, axis=1)
        step = jnp.flip(step, axis=1)
        b_part = jnp.flip(b_part, axis=1)
        c_part = jnp.flip(c_part, axis=1)
    strands = log_decay.shape[0]
    rows = log_decay.shape[1]
    blocks = rows // BLK

    def split(value):
        return jnp.swapaxes(value.reshape((strands, blocks, BLK) + value.shape[2:]), 0, 1)

    init = jnp.zeros((strands, H, P_SIZE, NS), jnp.float32)
    pieces = (split(inner_x), split(log_decay), split(step), split(b_part), split(c_part))
    end_state, outputs = lax.scan(jax.vmap(block_step), init, pieces)
    outputs = jnp.swapaxes(outputs, 0, 1).reshape(strands, rows, H, P_SIZE)
    total = jnp.exp(jnp.sum(log_decay, axis=1))
    identity = (jnp.ones_like(total), jnp.zeros_like(end_state))
    if backward:
        incoming = carried_in((total, end_state), "seq", join_carry, identity, True)[1]
    else:
        incoming = carried_in((total, end_state), "seq", join_carry, identity, False)[1]
    reach = jnp.exp(jnp.cumsum(log_decay, axis=1))
    outputs = outputs + reach[..., None] * jnp.einsum(
        "sln,shpn->slhp", c_part, incoming, precision=lax.Precision.HIGHEST
    )
    if backward:
        outputs = jnp.flip(outputs, axis=1)
    return outputs


def per_device(
    token_ids,
    embed_table,
    input_weight_matrix,
    output_weight_matrix,
    conv_weight,
    dt_bias,
    decay_rate,
    skip_gain,
    norm_gain,
):
    rows = token_ids.shape[0]
    paired_strand = token_ids
    for bit in range(lax.axis_size("seq").bit_length() - 1):
        paired_strand = swapped(paired_strand, "seq", bit)
    second_ids = complement(paired_strand[::-1])
    forward_direction_params = (0, 0)
    behind_params = (1, 1)
    feature_vectors = jnp.stack(
        [embed_rows(token_ids, embed_table), embed_rows(second_ids, embed_table)]
    )
    projected = jnp.einsum(
        "zmx,xf->zmf", feature_vectors, input_weight_matrix, preferred_element_type=jnp.float32
    ).astype(jnp.bfloat16)
    values = projected[:, :, E : 2 * E]
    rim = KW - 1
    edges = jnp.concatenate([values[:, :rim], values[:, rows - rim :]], axis=1)
    extended = padded(edges, (("seq", 1),), rim)
    padded_input = jnp.concatenate(
        [extended[:, :rim], values, extended[:, 3 * rim :]], axis=1
    ).astype(jnp.float32)
    gate = projected[:, :, :E].astype(jnp.float32)
    b_part = projected[:, :, 2 * E : 2 * E + NS].astype(jnp.float32)
    c_part = projected[:, :, 2 * E + NS : 2 * E + 2 * NS].astype(jnp.float32)
    raw = projected[:, :, 2 * E + 2 * NS :].astype(jnp.float32)
    mixer_output = None
    for backward, params in ((False, forward_direction_params), (True, behind_params)):
        taps = jnp.stack([conv_weight[k] for k in params])
        bias = jnp.stack([dt_bias[k] for k in params])
        rate = jnp.stack([decay_rate[k] for k in params])
        skip = jnp.stack([skip_gain[k] for k in params])
        gain = jnp.stack([norm_gain[k] for k in params])
        acc = None
        for j in range(KW):
            begin = 2 * (KW - 1) - j if backward else j
            term = taps[:, j][:, None, :] * padded_input[:, begin : begin + rows]
            acc = term if acc is None else acc + term
        inner_x = jax.nn.silu(acc).reshape(2, rows, H, P_SIZE)
        step = jax.nn.softplus(raw + bias[:, None, :])
        log_decay = -rate[:, None, :] * step
        outputs = (
            processor_sequence(inner_x, log_decay, step, b_part, c_part, backward)
            + skip[:, None, :, None] * inner_x
        )
        gated = outputs * jax.nn.silu(gate).reshape(2, rows, H, P_SIZE)
        meansq = jnp.mean(gated * gated, axis=-1, keepdims=True)
        normed = (gated * lax.rsqrt(meansq + EPSILON) * gain.reshape(2, 1, H, P_SIZE)).reshape(
            2, rows, E
        )
        mixer_output = normed if mixer_output is None else mixer_output + normed
    mixer_output = mixer_output.astype(jnp.bfloat16)
    strand_out = jnp.einsum(
        "qtf,fg->qtg", mixer_output, output_weight_matrix, preferred_element_type=jnp.float32
    ).astype(jnp.bfloat16)
    mirrored = strand_out[1]
    for bit in range(lax.axis_size("seq").bit_length() - 1):
        mirrored = swapped(mirrored, "seq", bit)
    other = mirrored[::-1, ::-1]
    hidden = (
        feature_vectors[0].astype(jnp.float32)
        + strand_out[0].astype(jnp.float32)
        + other.astype(jnp.float32)
    )
    return hidden.astype(jnp.bfloat16)


def solution(mesh):
    placed = (P(("batch", "seq")), P(), P(), P(), P(), P(), P(), P(), P())
    return jax.shard_map(
        per_device, mesh=mesh, in_specs=placed, out_specs=P(("batch", "seq"), None), check_vma=False
    )
```

profile of v0, /device:TPU:0, one launch (start us, length us, event | category | flops | bytes accessed | tf_op | source)
XLA Modules:
  0.0 440.7 jit_solution(5854677234308266844)
XLA Ops:
  0.0 3.0 collective-permute-start
  10.1 2.0 collective-permute-done.1
  12.1 2.6 collective-permute-start.2
  22.1 4.5 %reduce-window.14 = f32[2,8,8,128]{3,2,1,0:T(8,128)S(1)} reduce-window(f32[2,8,8,128]{3,2,1,0:T(8,128)S(1)} %copy.70, f32[]{:T(128)} %constant.108.clone.1), window={size=1x1x1x128 pad=0_0x0_0x0_0x127_0}, to_apply=%region_3.4 | reduce-window | flops 2080768 | bytes 131076 | tf_op jit(solution)/shard_map/reduce-window
  27.9 2.8 collective-permute-start.3
  34.4 4.5 %reduce-window.16 = f32[2,8,8,128]{3,2,1,0:T(8,128)S(1)} reduce-window(f32[2,8,8,128]{3,2,1,0:T(8,128)S(1)} %copy.77, f32[]{:T(128)} %constant.108.clone.1), window={size=1x1x1x128 pad=0_0x0_0x0_0x127_0}, to_apply=%region_12.13 | reduce-window | flops 2080768 | bytes 131076 | tf_op jit(solution)/shard_map/reduce-window.2
  42.6 22.2 %all-gather.5 = f32[8,2,8]{2,1,0:T(2,128)S(1)} all-gather(f32[1,2,8]{2,1,0:T(2,128)S(1)} %exponential_bitcast_fusion), channel_id=4, replica_groups=mesh['seq'=8,'batch'=4] {'seq'}, dimensions={0}, use_global_device_ids=true | all-gather | bytes 576 | tf_op jit(solution)/shard_map/all_gather | solution.py:19
  68.2 16.3 %all-gather.4 = f32[8,2,8]{2,1,0:T(2,128)S(1)} all-gather(f32[1,2,8]{2,1,0:T(2,128)S(1)} %exponential_bitcast_fusion.1), channel_id=2, replica_groups=mesh['seq'=8,'batch'=4] {'seq'}, dimensions={0}, use_global_device_ids=true | all-gather | bytes 576 | tf_op jit(solution)/shard_map/all_gather | solution.py:19
  84.5 4.8 %concatenate.11 = bf16[2,1030,512]{1,2,0:T(8,128)(2,1)} concatenate(bf16[2,3,512]{1,2,0:T(8,128)(2,1)} %collective-permute-done.3, bf16[2,1024,512]{1,2,0:T(8,128)(2,1)S(1)} %slice-done, bf16[2,3,512]{1,2,0:T(8,128)(2,1)} %collective-permute-done.4), dimensions={1} | concatenate | bytes 4218880 | tf_op jit(solution)/shard_map/concatenate | solution.py:157
  89.3 2.0 convert_element_type.55
  91.3 9.9 %divide_multiply_fusion.1 = (f32[2,1024,512]{1,2,0:T(8,128)}, f32[2,1024,512]{1,2,0:T(8,128)}) fusion(f32[2,1030,512]{1,2,0:T(8,128)S(1)} %convert_element_type.55, f32[2,512]{1,0:T(2,128)S(1)} %bitcast.310, f32[2,512]{1,0:T(2,128)S(1)} %bitcast.311, f32[2,512]{1,0:T(2,128)S(1)} %bitcast.312, f32[2,512]{1,0:T(2,128)S(1)} %bitcast.313, ...), kind=kLoop, calls=%fused_computation.115 | loop fusion | flops 23068672 | bytes 37781504 | tf_op jit(solution)/shard_map/jit(silu)/mul | solution.py:176
  101.2 7.3 %rev.35 = f32[2,1024,8,64]{1,3,2,0:T(8,128)} reverse(f32[2,1024,8,64]{1,3,2,0:T(8,128)} %bitcast.291), dimensions={1} | reverse | bytes 8388608 | tf_op jit(solution)/shard_map/jit(_flip)/rev | solution.py:98
  108.5 4.7 %bitcast_bitcast_fusion = f32[8,2,128,8,64]{2,4,3,1,0:T(8,128)} fusion(f32[2,1024,8,64]{1,3,2,0:T(8,128)} %rev.35), kind=kLoop, calls=%fused_computation.96 | loop fusion | bytes 8388608 | tf_op jit(solution)/shard_map/transpose | solution.py:108
  113.2 2.5 broadcast.72.clone
  115.7 93.7 %while.56 = (s32[]{:T(128)}, f32[2,8,64,16]{2,3,1,0:T(8,128)S(1)}, f32[8,2,128,8,64]{2,4,3,1,0:T(8,128)}, f32[8,2,128,8]{3,2,1,0:T(8,128)}, f32[8,2,128,8,64]{2,...) while((s32[]{:T(128)}, f32[2,8,64,16]{2,3,1,0:T(8,128)S(1)}, ...), condition=%wide.region_11.12_spmd.clone, body=%wide.region_9.11_spmd.clone.sunk | while | flops 259637248 | bytes 3385880 | solution.py:112
  116.9 1.7 convolution_multiply_fusion.5
  120.2 2.0 convolution_add_fusion.5
  123.4 4.0 fusion.169
  128.7 1.7 convolution_multiply_fusion.5
  131.9 2.0 convolution_add_fusion.5
  135.1 4.0 fusion.169
  143.6 2.0 convolution_add_fusion.5
  146.8 4.0 fusion.169
  152.1 1.7 convolution_multiply_fusion.5
  155.3 2.0 convolution_add_fusion.5
  158.5 4.0 fusion.169
  167.1 2.0 convolution_add_fusion.5
  170.3 4.0 fusion.169
  175.5 1.7 convolution_multiply_fusion.5
  178.8 2.0 convolution_add_fusion.5
  182.0 4.0 fusion.169
  190.5 2.0 convolution_add_fusion.5
  193.7 4.0 fusion.169
  202.2 2.0 convolution_add_fusion.5
  205.4 4.0 fusion.169
  209.4 33.1 %all-gather.3 = f32[16,8,64,16]{2,3,1,0:T(8,128)S(1)} all-gather(f32[2,8,64,16]{2,3,1,0:T(8,128)S(1)} %get-tuple-element.283), channel_id=5, replica_groups=mesh['seq'=8,'batch'=4] {'seq'}, dimensions={0}, use_global_device_ids=true | all-gather | bytes 589824 | tf_op jit(solution)/shard_map/all_gather | solution.py:19
  243.6 6.8 %bitcast_add_fusion.2 = f32[2,1024,8,64]{1,3,2,0:T(8,128)} fusion(f32[2,8,64,16]{2,3,1,0:T(8,128)S(1)} %get-tuple-element.284, f32[2,1024,8]{1,2,0:T(8,128)S(1)} %bitcast.301, f32[2,1024,16]{1,2,0:T(8,128)S(1)} %copy-done.8, f32[8,2,128,8,64]{2,4,3,1,0:T(8,128)} %get-tuple-element.282), kind=kOutput, calls=%fused_computation.92 | convolution fusion | flops 203423744 | bytes 8650752 | tf_op jit(solution)/shard_map/sln,shpn->slhp/dot_general | solution.py:121
  250.4 7.3 %rev.41 = f32[2,1024,8,64]{1,3,2,0:T(8,128)} reverse(f32[2,1024,8,64]{1,3,2,0:T(8,128)} %bitcast_add_fusion.2), dimensions={1} | reverse | bytes 8388608 | tf_op jit(solution)/shard_map/jit(_flip)/rev | solution.py:125
  257.7 3.2 copy.99
  260.9 2.7 copy.119
  263.6 2.5 broadcast.72.clone.1
  266.2 93.8 %while.54 = (s32[]{:T(128)}, f32[2,8,64,16]{2,3,1,0:T(8,128)S(1)}, f32[8,2,128,8,64]{2,4,3,1,0:T(8,128)}, f32[8,2,128,8]{3,2,1,0:T(8,128)}, f32[8,2,128,8,64]{2,...) while((s32[]{:T(128)}, f32[2,8,64,16]{2,3,1,0:T(8,128)S(1)}, ...), condition=%wide.region_2.3_spmd.clone, body=%wide.region_0.2_spmd.clone.sunk | while | flops 259637248 | bytes 3385880 | solution.py:112
  270.7 2.0 convolution_add_fusion.4
  273.9 4.0 fusion.160
  282.4 2.0 convolution_add_fusion.4
  285.6 4.0 fusion.160
  294.1 2.0 convolution_add_fusion.4
  297.3 4.0 fusion.160
  305.8 2.0 convolution_add_fusion.4
  309.0 4.1 fusion.160
  317.6 2.0 convolution_add_fusion.4
  320.8 4.0 fusion.160
  329.3 2.0 convolution_add_fusion.4
  332.5 4.0 fusion.160
  341.0 2.0 convolution_add_fusion.4
  344.2 4.0 fusion.160
  352.7 2.0 convolution_add_fusion.4
  355.9 4.1 fusion.160
  360.0 32.3 %all-gather.1 = f32[16,8,64,16]{2,3,1,0:T(8,128)S(1)} all-gather(f32[2,8,64,16]{2,3,1,0:T(8,128)S(1)} %get-tuple-element.280), channel_id=3, replica_groups=mesh['seq'=8,'batch'=4] {'seq'}, dimensions={0}, use_global_device_ids=true | all-gather | bytes 589824 | tf_op jit(solution)/shard_map/all_gather | solution.py:19
  393.2 9.0 %multiply_reduce_fusion.1 = (f32[2,1024,8]{1,2,0:T(8,128)S(1)}, f32[2,1024,8,64]{1,3,2,0:T(8,128)S(1)}, f32[2,1024,8]{1,2,0:T(8,128)S(1)}, f32[2,1024,8,64]{1,3,2,0:T(8,128)S(1)}) fusion(f32[2,8]{1,0:T(2,128)S(1)} %copy-done.12, f32[2,1024,8]{1,2,0:T(8,128)S(1)} %bitcast.307, f32[2,1024,8,64]{1,3,2,0:T(8,128)} %rev.41, f32[2,8]{1,0:T(2,128)S(1)} %copy-done.13, ...), kind=kOutput, calls=%fused_computation.114 | convolution fusion | flops 219119616 | bytes 27590784 | tf_op jit(solution)/shard_map/sln,shpn->slhp/dot_general | solution.py:121
  404.5 9.1 %collective-permute-done.5 = bf16[1024,256]{1,0:T(8,128)(2,1)S(1)} collective-permute-done((bf16[1024,256]{1,0:T(8,128)(2,1)S(1)}, bf16[1024,256]{1,0:T(8,128)(2,1)S(1)}, u32[]{:S(2)}, u32[]{:S(2)}) %collective-permute-start.5) | collective-permute-done | bytes 524320 | tf_op jit(solution)/shard_map/ppermute | solution.py:41
  413.6 9.2 %collective-permute-done.6 = bf16[1024,256]{1,0:T(8,128)(2,1)S(1)} collective-permute-done((bf16[1024,256]{1,0:T(8,128)(2,1)S(1)}, bf16[1024,256]{1,0:T(8,128)(2,1)S(1)}, u32[]{:S(2)}, u32[]{:S(2)}) %collective-permute-start.6) | collective-permute-done | bytes 524320 | tf_op jit(solution)/shard_map/ppermute | solution.py:41
  422.8 15.1 %collective-permute-done.7 = bf16[1024,256]{1,0:T(8,128)(2,1)S(1)} collective-permute-done((bf16[1024,256]{1,0:T(8,128)(2,1)S(1)}, bf16[1024,256]{1,0:T(8,128)(2,1)S(1)}, u32[]{:S(2)}, u32[]{:S(2)}) %collective-permute-start.7) | collective-permute-done | bytes 524320 | tf_op jit(solution)/shard_map/ppermute | solution.py:41
  437.9 1.8 rev.42
  (338 shorter events, 116.7 us)
Async XLA Ops:
  0.0 17.8 %copy-start = (bf16[256,1064]{0,1:T(8,128)(2,1)S(1)}, bf16[256,1064]{0,1:T(8,128)(2,1)}, u32[]{:S(2)}) copy-start(bf16[256,1064]{0,1:T(8,128)(2,1)} %param.19) | copy-start | bytes 1634308
  0.0 8.5 %collective-permute-start = (s32[1024]{0:T(1024)}, s32[1024]{0:T(1024)S(1)}, u32[]{:S(2)}, u32[]{:S(2)}) collective-permute-start(s32[1024]{0:T(1024)} %param.17), channel_id=1, source_target_pairs={{0,4},{4,0},{8,12},{12,8},{16,20},{20,16},{24,28},{28,24},{1,5},{5... | collective-permute-start | bytes 12296 | tf_op jit(solution)/shard_map/ppermute | solution.py:41
  6.3 15.0 %copy-start.4 = (bf16[1024,256]{1,0:T(8,128)(2,1)}, bf16[1024,256]{1,0:T(8,128)(2,1)S(1)}, u32[]{:S(2)}) copy-start(bf16[1024,256]{1,0:T(8,128)(2,1)S(1)} %convolution_convert_fusion.3) | copy-start | bytes 1572868
  8.5 3.6 collective-permute-start.1
  12.1 4.5 %collective-permute-start.2 = (s32[1024]{0:T(1024)S(1)}, s32[1024]{0:T(1024)S(1)}, u32[]{:S(2)}, u32[]{:S(2)}) collective-permute-start(s32[1024]{0:T(1024)S(1)} %collective-permute-done.1), channel_id=1, source_target_pairs={{0,16},{16,0},{4,20},{20,4},{8,24},{24,8},{12,28},{28,12},{1,17},{... | collective-permute-start | bytes 12296 | tf_op jit(solution)/shard_map/ppermute | solution.py:41
  19.1 2.2 copy-start.2
  27.9 56.6 %collective-permute-start.3 = (bf16[2,3,512]{1,2,0:T(8,128)(2,1)}, bf16[2,3,512]{1,2,0:T(8,128)(2,1)}, u32[]{:S(2)}, u32[]{:S(2)}) collective-permute-start(bf16[2,3,512]{1,2,0:T(8,128)(2,1)} %get-tuple-element.450), channel_id=1, source_target_pairs={{0,4},{4,8},{8,12},{12,16},{16,20},{20,24},{24,28},{1,5},{5,9},{9,... | collective-permute-start | bytes 18440 | tf_op jit(solution)/shard_map/ppermute | solution.py:52
  30.7 53.8 %collective-permute-start.4 = (bf16[2,3,512]{1,2,0:T(8,128)(2,1)}, bf16[2,3,512]{1,2,0:T(8,128)(2,1)}, u32[]{:S(2)}, u32[]{:S(2)}) collective-permute-start(bf16[2,3,512]{1,2,0:T(8,128)(2,1)} %get-tuple-element.449), channel_id=1, source_target_pairs={{4,0},{8,4},{12,8},{16,12},{20,16},{24,20},{28,24},{5,1},{9,5},{13... | collective-permute-start | bytes 18440 | tf_op jit(solution)/shard_map/ppermute | solution.py:54
  34.4 33.8 %copy-start.7 = (f32[2,1024,16]{1,2,0:T(8,128)}, f32[2,1024,16]{1,2,0:T(8,128)S(1)}, u32[]{:S(2)}) copy-start(f32[2,1024,16]{1,2,0:T(8,128)S(1)} %rev.38) | copy-start | bytes 393220
  34.4 33.2 %copy-start.9 = (f32[2,8,128,8]{2,3,1,0:T(8,128)S(1)}, f32[2,8,128,8]{2,3,1,0:T(8,128)}, u32[]{:S(2)}) copy-start(f32[2,8,128,8]{2,3,1,0:T(8,128)} %get-tuple-element.440) | copy-start | bytes 196612
  34.4 50.1 %slice-start = ((bf16[2,1024,1064]{1,2,0:T(8,128)(2,1)}), bf16[2,1024,512]{1,2,0:T(8,128)(2,1)S(1)}, s32[]{:S(2)}) async-start(bf16[2,1024,1064]{1,2,0:T(8,128)(2,1)} %copy-done.2), calls=%async_computation | async-start | bytes 4194304 | tf_op jit(solution)/shard_map/slice | solution.py:153
  89.3 2.0 copy-start.11
  115.7 126.9 %copy-start.3 = (f32[2,8,64,16]{2,3,1,0:T(8,128)S(1)}, f32[2,8,64,16]{2,3,1,0:T(8,128)}, u32[]{:S(2)}) copy-start(f32[2,8,64,16]{2,3,1,0:T(8,128)} %custom-call.3) | copy-start | bytes 196612
  209.4 34.2 %copy-start.8 = (f32[2,1024,16]{1,2,0:T(8,128)S(1)}, f32[2,1024,16]{1,2,0:T(8,128)}, u32[]{:S(2)}) copy-start(f32[2,1024,16]{1,2,0:T(8,128)} %copy-done.7) | copy-start | bytes 393220
  266.2 126.1 %copy-start.6 = (f32[2,8,64,16]{2,3,1,0:T(8,128)S(1)}, f32[2,8,64,16]{2,3,1,0:T(8,128)}, u32[]{:S(2)}) copy-start(f32[2,8,64,16]{2,3,1,0:T(8,128)} %custom-call.1) | copy-start | bytes 196612
  266.2 127.0 %copy-start.10 = (f32[2,8,1024]{2,1,0:T(8,128)S(1)}, f32[2,8,1024]{2,1,0:T(8,128)}, u32[]{:S(2)}) copy-start(f32[2,8,1024]{2,1,0:T(8,128)} %exp.105) | copy-start | bytes 196612
  266.2 127.0 %copy-start.12 = (f32[2,8]{1,0:T(2,128)S(1)}, f32[2,8]{1,0:T(2,128)}, u32[]{:S(2)}) copy-start(f32[2,8]{1,0:T(2,128)} %get-tuple-element.475) | copy-start | bytes 196
  266.2 127.0 %copy-start.13 = (f32[2,8]{1,0:T(2,128)S(1)}, f32[2,8]{1,0:T(2,128)}, u32[]{:S(2)}) copy-start(f32[2,8]{1,0:T(2,128)} %get-tuple-element.476) | copy-start | bytes 196
  402.3 1.2 copy-start.14
  403.5 36.2 %copy-start.5 = (bf16[1024,256]{1,0:T(8,128)(2,1)S(1)}, bf16[1024,256]{1,0:T(8,128)(2,1)}, u32[]{:S(2)}) copy-start(bf16[1024,256]{1,0:T(8,128)(2,1)} %copy-done.4) | copy-start | bytes 1572868
  403.5 37.2 %copy-start.1 = (bf16[256,1064]{0,1:T(8,128)(2,1)S(1)}, bf16[256,1064]{0,1:T(8,128)(2,1)}, u32[]{:S(2)}) copy-start(bf16[256,1064]{0,1:T(8,128)(2,1)} %param.19) | copy-start | bytes 1634308
  404.4 9.2 %collective-permute-start.5 = (bf16[1024,256]{1,0:T(8,128)(2,1)S(1)}, bf16[1024,256]{1,0:T(8,128)(2,1)S(1)}, u32[]{:S(2)}, u32[]{:S(2)}) collective-permute-start(bf16[1024,256]{1,0:T(8,128)(2,1)S(1)} %slice_bitcast_fusion), channel_id=1, source_target_pairs={{0,4},{4,0},{8,12},{12,8},{16,20},{20,16},{24,28},{28,24},{1,5},{5... | collective-permute-start | bytes 1572872 | tf_op jit(solution)/shard_map/ppermute | solution.py:41
  413.6 9.2 %collective-permute-start.6 = (bf16[1024,256]{1,0:T(8,128)(2,1)S(1)}, bf16[1024,256]{1,0:T(8,128)(2,1)S(1)}, u32[]{:S(2)}, u32[]{:S(2)}) collective-permute-start(bf16[1024,256]{1,0:T(8,128)(2,1)S(1)} %collective-permute-done.5), channel_id=1, source_target_pairs={{0,8},{8,0},{4,12},{12,4},{16,24},{24,16},{20,28},{28,20},{1,9},{9... | collective-permute-start | bytes 1572872 | tf_op jit(solution)/shard_map/ppermute | solution.py:41
  422.8 15.1 %collective-permute-start.7 = (bf16[1024,256]{1,0:T(8,128)(2,1)S(1)}, bf16[1024,256]{1,0:T(8,128)(2,1)S(1)}, u32[]{:S(2)}, u32[]{:S(2)}) collective-permute-start(bf16[1024,256]{1,0:T(8,128)(2,1)S(1)} %collective-permute-done.6), channel_id=1, source_target_pairs={{0,16},{16,0},{4,20},{20,4},{8,24},{24,8},{12,28},{28,12},{1,17},{... | collective-permute-start | bytes 1572872 | tf_op jit(solution)/shard_map/ppermute | solution.py:41
where the time goes:
time: 448 us; the launch traced here: 441 us
  matrix products  162 us (36%)
  blocking collectives  104 us (23%)
  local copies, waits for them, and re-layouts  93.3 us (21%)
  waiting for transfers between devices  36.5 us (8%)
  other arithmetic  31.9 us (7%)
  starting transfers between devices  11.3 us (3%)
    all_gather x4, blocking collectives, carried_in(): pieces = jax.tree.map(lambda part: lax.all_gather(part, axis), value)  104 us
    dot_general x16, matrix products, block_step(): jnp.einsum('trh,rhp->thp', scores[:, :, None] * decay, weighted, precisio...  64.6 us
    ppermute x6, waiting for transfers between devices, swapped(): return lax.ppermute(block, axis, route)  36.5 us
    dot_general x16, matrix products, block_step(): jnp.einsum('rh,rhp,rn->hpn', tail, weighted, b_part, precision=highest)  31.6 us
    dot_general x16, matrix products, block_step(): jnp.einsum('tn,hpn->thp', c_part, state, precision=highest)  27.9 us
    squeeze x32, local copies, waits for them, and re-layouts, processor_sequence(): end_state, outputs = lax.scan(jax.vmap(block_step), init, pieces)  26.4 us
    dot_general x16, matrix products, block_step(): scores = jnp.dot(c_part, b_part.T, precision=highest)  18.1 us
    dot_general x2, matrix products, processor_sequence(): jnp.einsum('sln,shpn->slhp', c_part, incoming, precision=lax.Precision.HI...  15.8 us
  transfers between devices with their start and end apart: 8, of which 5 were waited for; matrix products, arithmetic and copies ran while one was open for 5% of the time, Pallas kernels for 0%

commit v1 on v0

v1 whole, which is shorter than its diff:
```python
import jax
import jax.numpy as jnp
from jax import lax
from jax.experimental import pallas as pl
from jax.experimental.pallas import tpu as pltpu
from jax.sharding import PartitionSpec as P

D = 256
E = 512
NS = 16
H = 8
KW = 4
SYM = 5
LOG2E = 1.4426950408889634
EPSILON = 1e-05
CH = 128

F32 = jnp.float32
BF16 = jnp.bfloat16

CHAINS = ((0, 0, 0), (0, 1, 1), (1, 0, 1), (1, 1, 0))


def iota(shape, dim):
    return lax.broadcasted_iota(jnp.int32, shape, dim)


def nn(a, b, **kw):
    return lax.dot_general(a, b, (((1,), (0,)), ((), ())), preferred_element_type=F32, **kw)


def nt(a, b, **kw):
    return lax.dot_general(a, b, (((1,), (1,)), ((), ())), preferred_element_type=F32, **kw)


def split(value):
    high = value.astype(BF16)
    low = (value - high.astype(F32)).astype(BF16)
    return high, low


def softplus(x):
    return jnp.maximum(x, 0.0) + jnp.log1p(jnp.exp(-jnp.abs(x)))


def silu_half(half):
    return half + half * jnp.tanh(half)


def tap_row(direction, j):
    return j if direction == 0 else 2 * (KW - 1) - j


def window_onehot(rows):
    sub = iota((8, CH), 0).astype(F32)
    blocks = [jnp.where(row == sub, 1.0, 0.0) for row in rows]
    blocks.append(jnp.zeros((8, CH), F32))
    stacked = jnp.concatenate(blocks + blocks, axis=0)
    return stacked.T.astype(BF16)


def shifted(tok, offset, rows):
    if offset == 0:
        return tok
    lane = iota((rows, CH), 1)
    row = iota((rows, CH), 0)
    moved = pltpu.roll(tok, (-offset) % CH, 1)
    if offset < 0:
        other = pltpu.roll(moved, 1, 0)
        crossing = lane < -offset
        outside = crossing & (row == 0)
    else:
        other = pltpu.roll(moved, rows - 1, 0)
        crossing = lane >= CH - offset
        outside = crossing & (row == rows - 1)
    return jnp.where(outside, 5.0, jnp.where(crossing, other, moved))


def pick(values, u):
    out = values[0]
    for k in range(1, SYM):
        out = jnp.where(u == k, values[k], out)
    return out


def tile_at(ref, row):
    return ref[pl.ds(pl.multiple_of(row, 8), 8), :]


def local_kernel(
    tok_s, tok_v, emb, w_in, w_out, cw, bias, rate, skip, gain,
    yad, ybc, feat, atab, gtab, zg, cst, lac, tw, xch, xcl, pst, wflip,
    emb16,
):
    nchunk = tok_v.shape[0]
    highest = lax.Precision.HIGHEST
    emb16[...] = jnp.zeros_like(emb16)
    e32 = emb[...].astype(F32)
    emb16[0:SYM, :] = e32
    for v in range(4):
        emb16[8 + v : 9 + v, :] = e32[3 - v : 4 - v, :]
    emb16[12:13, :] = e32[4:5, :]
    embs = emb16[...].astype(BF16)
    z16 = nn(embs, w_in[:, 0:E]).astype(BF16).astype(F32)
    x16 = nn(embs, w_in[:, E : 2 * E]).astype(BF16).astype(F32)
    rest = nn(embs, w_in[:, 2 * E :]).astype(BF16)
    nrest = 2 * NS + H
    expand = jnp.where(
        iota((nrest, E), 0) == (iota((nrest, E), 1) >> 6) + 2 * NS, 1.0, 0.0
    ).astype(BF16)
    heads = jnp.where(iota((H, E), 0) == (iota((H, E), 1) >> 6), 1.0, 0.0)
    r_exp = nn(rest, expand)
    bias_e = nn(bias[...], heads, precision=highest)
    rate_e = nn(rate[...], heads, precision=highest)
    skip_e = nn(skip[...], heads, precision=highest)
    shift = jnp.where(
        iota((nrest, nrest), 0) + NS == iota((nrest, nrest), 1),
        jnp.where(iota((nrest, nrest), 0) < NS, 1.0, 0.0),
        0.0,
    ).astype(BF16)
    rest_b = nn(rest, shift).astype(BF16)
    cb = nt(rest_b, rest)
    sz = z16 * (0.5 + 0.5 * jnp.tanh(0.5 * z16))
    for s in range(2):
        for i in range(4):
            zg[pl.ds(s * 4 + i, 8, stride=8), :] = sz[8 * s : 8 * s + 8, 128 * i : 128 * i + 128]
    pick_r = jnp.where(
        iota((H, nrest), 0) + 2 * NS == iota((H, nrest), 1), 1.0, 0.0
    ).astype(BF16)
    r_t = nt(pick_r, rest)
    eye = jnp.where(iota((H, H), 0) == iota((H, H), 1), 1.0, 0.0)
    bias_t = nt(eye, bias[...], precision=highest)
    rate_t = nt(eye, rate[...], precision=highest)
    for q, (d, s, k) in enumerate(CHAINS):
        dt = softplus(r_exp[8 * s : 8 * s + 8, :] + bias_e[k : k + 1, :])
        a = jnp.exp(-rate_e[k : k + 1, :] * dt)
        for i in range(4):
            lanes = slice(128 * i, 128 * i + 128)
            atab[pl.ds(d * 64 + s * 4 + i, 8, stride=8), :] = a[:, lanes]
            cst[d * 8 + s * 4 + i : d * 8 + s * 4 + i + 1, :] = skip_e[k : k + 1, lanes]
            cst[16 + d * 8 + s * 4 + i : 17 + d * 8 + s * 4 + i, :] = gain[k : k + 1, lanes]
        for u in range(SYM):
            g = cb[8 * s : 8 * s + 8, 8 * s + u : 8 * s + u + 1] * dt
            for i in range(4):
                gtab[pl.ds((d * SYM + u) * 64 + s * 4 + i, 8, stride=8), :] = g[
                    :, 128 * i : 128 * i + 128
                ]
        la = (
            -rate_t[:, k : k + 1] * softplus(r_t[:, 8 * s : 8 * s + 8] + bias_t[:, k : k + 1])
        ) * LOG2E
        for v in range(SYM):
            lac[(d * SYM + v) * 16 + s * 8 : (d * SYM + v) * 16 + s * 8 + 8, :] = jnp.broadcast_to(
                la[:, v : v + 1], (8, CH)
            )
        xs = x16[8 * s : 8 * s + 8, :]
        blocks = [jnp.zeros((8, E), F32)] * 8
        for j in range(KW):
            blocks[tap_row(d, j)] = (0.5 * cw[k, j : j + 1, :]) * xs
        high, low = split(jnp.concatenate(blocks, axis=0))
        tw[q, 0:64, :] = high
        tw[q, 64:128, :] = low
        code = iota((CH, CH), 0).astype(F32)
        lane = iota((CH, CH), 1) & 63
        slot = lane >> 3
        sym = (lane & 7).astype(F32)
        d0 = jnp.floor((code + 0.5) * (1.0 / 25.0))
        d01 = jnp.floor((code + 0.5) * (1.0 / 5.0))
        digits = (d0, d01 - 5.0 * d0, code - 5.0 * d01)
        hot = jnp.zeros((CH, CH), F32)
        for j in range(KW - 1):
            hot = jnp.where(
                slot == tap_row(d, j), jnp.where(sym == digits[j], 1.0, 0.0), hot
            )
        partial = nn(hot.astype(BF16), tw[q])
        last = blocks[tap_row(d, KW - 1)]
        for v in range(SYM):
            high, low = split(silu_half(partial + last[v : v + 1, :]))
            xch[(q * SYM + v) * CH : (q * SYM + v + 1) * CH, :] = high
            xcl[(q * SYM + v) * CH : (q * SYM + v + 1) * CH, :] = low
    flip = jnp.where(iota((D, D), 0) + iota((D, D), 1) == D - 1, 1.0, 0.0).astype(BF16)
    wflip[...] = nn(w_out[...], flip).astype(BF16)

    tok = tok_v[...].astype(F32)
    shifts = [shifted(tok, o, nchunk) for o in range(-3, 4)]
    emb_rows = jnp.concatenate(
        [jnp.zeros((24, D), F32), emb16[0:8, :], jnp.zeros((96, D), F32)], axis=0
    ).astype(BF16)
    for c in range(nchunk):
        hot = window_onehot([sh[c : c + 1, :] for sh in shifts])
        feat[c * CH : (c + 1) * CH, :] = nn(hot, emb_rows).astype(BF16)
        for q, (d, s, k) in enumerate(CHAINS):
            x = silu_half(nn(hot, tw[q]))
            ref = (yad, ybc)[d]
            for i in range(4):
                ref[pl.ds(c * 8 * CH + s * 4 + i, CH, stride=8), :] = x[:, 128 * i : 128 * i + 128]
    total = nchunk * CH
    yad[0:24, :] = jnp.zeros((24, CH), F32)
    ybc[total * 8 - 24 : total * 8, :] = jnp.zeros((24, CH), F32)

    skip0 = cst[0:8, :]
    skip1 = cst[8:16, :]

    def advance(direction, ref, skip_t, t, state):
        u = tok_s[t]
        x = tile_at(ref, t * 8)
        a = tile_at(atab, direction * 64 + u * 8)
        new = [
            a * state[w] + tile_at(gtab, (direction * SYM + w) * 64 + u * 8) * x
            for w in range(SYM)
        ]
        ref[pl.ds(pl.multiple_of(t * 8, 8), 8), :] = pick(new, u) + skip_t * x
        return new, a

    unroll = 8

    def group(g, carry):
        ya, yb, pa, pb = carry
        ya, yb = list(ya), list(yb)
        for i in range(unroll):
            n = g * unroll + i
            ya, a0 = advance(0, yad, skip0, n, ya)
            yb, a1 = advance(1, ybc, skip1, total - 1 - n, yb)
            if i < 3:
                a0 = jnp.where(g == 0, 1.0, a0)
                a1 = jnp.where(g == 0, 1.0, a1)
            pa = pa * a0
            pb = pb * a1
        return tuple(ya), tuple(yb), pa, pb

    def chunk(c, carry):
        pst[pl.ds(pl.multiple_of(c * 8, 8), 8), :] = carry[2]
        pst[pl.ds(pl.multiple_of((2 * nchunk - 1 - c) * 8, 8), 8), :] = carry[3]
        per = CH // unroll
        return lax.fori_loop(c * per, (c + 1) * per, group, carry)

    zero = jnp.zeros((8, CH), F32)
    one = jnp.ones((8, CH), F32)
    lax.fori_loop(0, nchunk, chunk, ((zero,) * SYM, (zero,) * SYM, one, one))


def finish_kernel(
    mine, tok_s, tok_all, yad, ybc, feat, atab, gtab, zg, cst, lac, tw, xch, xcl, pst, w_out, wflip,
    out,
    tok_f, code, tri, hist, svec, xrim, ycar, yrim, gad, gbc, mix,
):
    step = pl.program_id(0)
    nchunk = pl.num_programs(0)
    rows = tok_all.shape[0]
    own = rows // 8
    j = mine[0]

    @pl.when(step == 0)
    def _():
        tok = tok_all[...].astype(F32)
        tok_f[3] = tok
        for o in (-3, -2, -1, 1, 2, 3):
            tok_f[3 + o] = shifted(tok, o, rows)
        lane = iota((rows, CH), 1)
        row = iota((rows, CH), 0)
        lane_f = lane.astype(F32)
        before = 25.0 * tok_f[0] + 5.0 * tok_f[1] + tok_f[2]
        after = 25.0 * tok_f[6] + 5.0 * tok_f[5] + tok_f[4]
        code[0] = jnp.where((row == 0) & (lane < 3), 125.0 + lane_f, before)
        code[1] = jnp.where((row == rows - 1) & (lane >= CH - 3), lane_f, after)
        si = iota((CH, CH), 0)
        ri = iota((CH, CH), 1)
        ones = jnp.ones((CH, CH), F32)
        tri[0] = jnp.concatenate([jnp.where(si > ri, 1.0, 0.0), ones], axis=1).astype(BF16)
        tri[1] = jnp.concatenate([jnp.where(si < ri, 1.0, 0.0), ones], axis=1).astype(BF16)
        hist[...] = jnp.zeros_like(hist)
        sub8 = iota((8, CH), 0).astype(F32)
        subc = iota((CH, CH), 0).astype(F32)

        def block(b, off):
            side = jnp.where(b >= j, 1, 0)
            index = jnp.where(b >= j, b + 1, j - 1 - b)
            off = off * jnp.where(b == j, 0.0, 1.0)
            use_prefix = side.astype(F32)
            at = pl.ds(pl.multiple_of(index * 8, 8), 8)
            tk = tok_f[3, at, :]
            cd = code[side, at, :]
            hots = [jnp.where(tk[m : m + 1, :] == sub8, 1.0, 0.0) for m in range(8)]
            counts = nn(jnp.concatenate(hots, axis=0).astype(BF16), tri[side])
            totals = [counts[8 * m : 8 * m + 8, CH:] for m in range(8)]
            prefix = [jnp.zeros((8, CH), F32)]
            for m in range(8):
                prefix.append(prefix[-1] + totals[m])
            las = [lac[pl.ds(pl.multiple_of((side * SYM + v) * 16, 16), 16), :] for v in range(SYM)]
            acc = jnp.zeros((160, CH), F32)
            for pair in range(4):
                lefts, rights = [], []
                for m in (2 * pair, 2 * pair + 1):
                    suffix = prefix[8] - prefix[m + 1]
                    inside = suffix + use_prefix * (prefix[m] - suffix)
                    count = counts[8 * m : 8 * m + 8, :CH] + off + inside
                    exponent = las[0] * count[0:1, :]
                    for v in range(1, SYM):
                        exponent = exponent + las[v] * count[v : v + 1, :]
                    weight = jnp.exp2(exponent)
                    masked = jnp.concatenate(
                        [jnp.where(tk[m : m + 1, :] == float(v), weight, 0.0) for v in range(SYM)],
                        axis=0,
                    )
                    high, low = split(masked)
                    lefts.append(jnp.concatenate([high, low], axis=0))
                    rights.append(jnp.where(cd[m : m + 1, :] == subc, 1.0, 0.0).astype(BF16))
                acc = acc + nt(
                    jnp.concatenate(lefts, axis=1), jnp.concatenate(rights, axis=1)
                )
            hist[side] = hist[side] + acc
            return off + prefix[8]

        lax.fori_loop(0, own - 1, block, jnp.zeros((8, CH), F32))

        last8 = rows - 8
        mine8 = pl.ds(pl.multiple_of(j * 8, 8), 8)
        xs = {}
        for d in range(2):
            edge = 0 if d == 0 else 7
            seq_at = pl.ds(0 if d == 0 else last8, 8)
            hot_seq = window_onehot([tok_f[o, seq_at, :][edge : edge + 1, :] for o in range(7)])
            hot_own = window_onehot([tok_f[o, mine8, :][edge : edge + 1, :] for o in range(7)])
            for s in range(2):
                q = 2 * d + s
                xseq = silu_half(nn(hot_seq, tw[q]))
                xown = silu_half(nn(hot_own, tw[q]))
                if d == 0:
                    xs[q] = pltpu.roll(xseq[0:8, :], 5, 0)
                else:
                    xs[q] = xseq[CH - 8 :, :]
                for n in range(KW - 1):
                    t = n if d == 0 else CH - 1 - n
                    for i in range(4):
                        at = (d * 3 + n) * 8 + s * 4 + i
                        xrim[at : at + 1, :] = xown[t : t + 1, 128 * i : 128 * i + 128]
        diag = iota((H, E), 0) == (iota((H, E), 1) >> 6)
        sub16 = iota((16, E), 0)
        for q in range(4):
            d, s = q // 2, q % 2
            rim = jnp.concatenate([jnp.zeros((8, E), F32), xs[q]], axis=0)
            rim_h, rim_l = split(rim)
            for v in range(SYM):
                tail = slice((q * SYM + v + 1) * CH - 16, (q * SYM + v + 1) * CH)
                xch[tail, :] = jnp.where(
                    sub16 >= 13, rim_h.astype(F32), xch[tail, :].astype(F32)
                ).astype(BF16)
                xcl[tail, :] = jnp.where(
                    sub16 >= 13, rim_l.astype(F32), xcl[tail, :].astype(F32)
                ).astype(BF16)
                at = v * 16 + s * 8
                w = hist[d, at : at + 8, :] + hist[d, 80 + at : 88 + at, :]
                high, low = split(w)
                both = jnp.concatenate([high.astype(F32), low.astype(F32)], axis=0).astype(BF16)
                table = slice((q * SYM + v) * CH, (q * SYM + v + 1) * CH)
                one = nn(both, xch[table, :])
                two = nn(both, xcl[table, :])
                full = one[0:8, :] + one[8:16, :] + two[0:8, :]
                vec = jnp.sum(jnp.where(diag, full, 0.0), axis=0, keepdims=True)
                for i in range(4):
                    at = (d * SYM + v) * 8 + s * 4 + i
                    svec[at : at + 1, :] = vec[:, 128 * i : 128 * i + 128]
        total = nchunk * CH
        for d in range(2):
            state = []
            for w in range(SYM):
                value = jnp.zeros((8, CH), F32)
                for v in range(SYM):
                    at = (d * SYM + w) * 64 + v * 8
                    sat = (d * SYM + v) * 8
                    value = value + gtab[at : at + 8, :] * svec[sat : sat + 8, :]
                state.append(value)
            skip_t = cst[d * 8 : d * 8 + 8, :]
            for n in range(KW - 1):
                u = tok_s[n if d == 0 else total - 1 - n]
                x = xrim[(d * 3 + n) * 8 : (d * 3 + n) * 8 + 8, :]
                a = tile_at(atab, d * 64 + u * 8)
                state = [
                    a * state[w] + tile_at(gtab, (d * SYM + w) * 64 + u * 8) * x
                    for w in range(SYM)
                ]
                yrim[(d * 3 + n) * 8 : (d * 3 + n) * 8 + 8, :] = pick(state, u) + skip_t * x
            for w in range(SYM):
                ycar[(d * SYM + w) * 8 : (d * SYM + w) * 8 + 8, :] = state[w]

    first = step * CH
    unroll = 8

    def advance(d, ref, dest, n, decay, lead):
        local = n if d == 0 else CH - 1 - n
        u = tok_s[first + local]
        a = tile_at(atab, d * 64 + u * 8)
        if lead is not None:
            a = jnp.where(lead, 1.0, a)
        decay = decay * a
        y = tile_at(ref, local * 8) + decay * tile_at(ycar, d * SYM * 8 + u * 8)
        dest[pl.ds(pl.multiple_of(local * 8, 8), 8), :] = y * tile_at(zg, u * 8)
        return decay

    def group(g, carry):
        pa, pb = carry
        for i in range(unroll):
            n = g * unroll + i
            lead0 = (g == 0) & (step == 0) if i < 3 else None
            lead1 = (g == 0) & (step == nchunk - 1) if i < 3 else None
            pa = advance(0, yad, gad, n, pa, lead0)
            pb = advance(1, ybc, gbc, n, pb, lead1)
        return pa, pb

    lax.fori_loop(
        0, CH // unroll, group, (tile_at(pst, step * 8), tile_at(pst, (nchunk + step) * 8))
    )

    @pl.when(step == 0)
    def _():
        for n in range(3):
            gad[n * 8 : n * 8 + 8, :] = yrim[n * 8 : n * 8 + 8, :] * tile_at(zg, tok_s[n] * 8)

    @pl.when(step == nchunk - 1)
    def _():
        for n in range(3):
            at = (CH - 1 - n) * 8
            gbc[at : at + 8, :] = yrim[24 + n * 8 : 32 + n * 8, :] * tile_at(
                zg, tok_s[first + CH - 1 - n] * 8
            )

    mean = jnp.where(
        ((iota((2 * CH, CH), 0) & 127) >> 6) == (iota((2 * CH, CH), 1) >> 6), 1.0 / 64.0, 0.0
    ).astype(BF16)
    normed = None
    for d, ref in ((0, gad), (1, gbc)):
        g = ref[...]
        high, low = split(g * g)
        meansq = nn(jnp.concatenate([high, low], axis=1), mean)
        scaled = (g * lax.rsqrt(meansq + EPSILON)).reshape(CH, 8, CH) * cst[
            16 + d * 8 : 24 + d * 8, :
        ][None]
        normed = scaled if normed is None else normed + scaled
    mix[...] = normed.reshape(CH * 8, CH)
    parts = [mix[pl.ds(i, CH, stride=8), :].astype(BF16) for i in range(8)]
    mine_out = nn(jnp.concatenate(parts[0:4], axis=1), w_out[...]).astype(BF16).astype(F32)
    other = nn(jnp.concatenate(parts[4:8], axis=1), wflip[...]).astype(BF16).astype(F32)
    out[...] = (feat[...].astype(F32) + mine_out + other).astype(BF16)


def per_device(
    token_ids,
    embed_table,
    input_weight_matrix,
    output_weight_matrix,
    conv_weight,
    dt_bias,
    decay_rate,
    skip_gain,
    norm_gain,
):
    length = token_ids.shape[0]
    nchunk = length // CH
    own = lax.axis_size("seq")
    tok2 = token_ids.reshape(nchunk, CH)
    tok_all = lax.all_gather(tok2, "seq", tiled=True)
    rows = own * nchunk
    vm = pl.BlockSpec(memory_space=pltpu.VMEM)
    sm = pl.BlockSpec(memory_space=pltpu.SMEM)
    sds = jax.ShapeDtypeStruct
    shapes = (
        sds((length * 8, CH), F32),
        sds((length * 8, CH), F32),
        sds((length, D), BF16),
        sds((2 * 64, CH), F32),
        sds((2 * SYM * 64, CH), F32),
        sds((64, CH), F32),
        sds((32, CH), F32),
        sds((2 * SYM * 16, CH), F32),
        sds((4, CH, E), BF16),
        sds((4 * SYM * CH, E), BF16),
        sds((4 * SYM * CH, E), BF16),
        sds((2 * nchunk * 8, CH), F32),
        sds((E, D), BF16),
    )
    yad, ybc, feat, atab, gtab, zg, cst, lac, tw, xch, xcl, pst, wflip = pl.pallas_call(
        local_kernel,
        out_shape=shapes,
        in_specs=[sm] + [vm] * 9,
        out_specs=[vm] * len(shapes),
        scratch_shapes=[pltpu.VMEM((16, D), F32)],
        compiler_params=pltpu.CompilerParams(vmem_limit_bytes=40 * 1024 * 1024),
        cost_estimate=pl.CostEstimate(
            flops=4_000_000_000, bytes_accessed=16_000_000, transcendentals=4_000_000
        ),
        name="local_chains",
    )(
        token_ids, tok2, embed_table, input_weight_matrix, output_weight_matrix, conv_weight,
        dt_bias, decay_rate, skip_gain, norm_gain,
    )
    mine = lax.axis_index("seq").reshape(1).astype(jnp.int32)
    chunk_spec = pl.BlockSpec((CH * 8, CH), lambda i: (i, 0))
    out_spec = pl.BlockSpec((CH, D), lambda i: (i, 0))
    return pl.pallas_call(
        finish_kernel,
        grid=(nchunk,),
        out_shape=sds((length, D), BF16),
        in_specs=[sm, sm, vm, chunk_spec, chunk_spec, out_spec] + [vm] * 11,
        out_specs=out_spec,
        scratch_shapes=[
            pltpu.VMEM((7, rows, CH), F32),
            pltpu.VMEM((2, rows, CH), F32),
            pltpu.VMEM((2, CH, 2 * CH), BF16),
            pltpu.VMEM((2, 160, CH), F32),
            pltpu.VMEM((2 * SYM * 8, CH), F32),
            pltpu.VMEM((2 * 3 * 8, CH), F32),
            pltpu.VMEM((2 * SYM * 8, CH), F32),
            pltpu.VMEM((2 * 3 * 8, CH), F32),
            pltpu.VMEM((CH * 8, CH), F32),
            pltpu.VMEM((CH * 8, CH), F32),
            pltpu.VMEM((CH * 8, CH), F32),
        ],
        compiler_params=pltpu.CompilerParams(vmem_limit_bytes=40 * 1024 * 1024),
        cost_estimate=pl.CostEstimate(
            flops=4_000_000_000, bytes_accessed=16_000_000, transcendentals=1_000_000
        ),
        name="finish_chains",
    )(
        mine, token_ids, tok_all, yad, ybc, feat, atab, gtab, zg, cst, lac, tw, xch, xcl, pst,
        output_weight_matrix, wflip,
    )


def solution(mesh):
    placed = (P(("batch", "seq")), P(), P(), P(), P(), P(), P(), P(), P())
    return jax.shard_map(
        per_device, mesh=mesh, in_specs=placed, out_specs=P(("batch", "seq"), None), check_vma=False
    )
```

time: 448 us -> 94.8 us (0.21); the launches traced: 441 us -> 94 us
  matrix products: 162 us -> 0 us
  blocking collectives: 104 us -> 32.2 us
  local copies, waits for them, and re-layouts: 93.3 us -> 27.4 us
  waiting for transfers between devices: 36.5 us -> 0 us
  Pallas kernels: 0 us -> 34.4 us
  other arithmetic: 31.9 us -> 0 us
  starting transfers between devices: 11.3 us -> 0 us
    dot_general x70 -> x0, matrix products: 162 us -> none  [the longest x16 64.6 us: block_step(): jnp.einsum('trh,rhp->thp', scores[:, :, None] * decay, weighted, precisio...]
    all_gather x4 -> x1, blocking collectives: 104 us -> 32.2 us  [per_device(): tok_all = lax.all_gather(tok2, 'seq', tiled=True)]
    ppermute x8 -> x0, waiting for transfers between devices: 36.5 us -> none  [the longest x6 36.5 us: swapped(): return lax.ppermute(block, axis, route)]
    pallas_call x0 -> x2, Pallas kernels: none -> 34.4 us  [the longest x1 17.2 us: per_device(): pl.pallas_call(finish_kernel, grid=(nchunk,), out_shape=sds((length, D),...]
    squeeze x33 -> x0, local copies, waits for them, and re-layouts: 26.4 us -> none  [the longest x32 26.4 us: processor_sequence(): end_state, outputs = lax.scan(jax.vmap(block_step), init, pieces)]
    unnamed x41 -> x57, local copies, waits for them, and re-layouts: 3.9 us -> 27.4 us
    rev x10 -> x0, local copies, waits for them, and re-layouts: 18.9 us -> none  [the longest x1 7.33 us: processor_sequence(): outputs = jnp.flip(outputs, axis=1)]
    another operation x24 -> x0, other arithmetic: 13.4 us -> none
  transfers between devices with their start and end apart: 8 -> 0, of which waited for: 5 -> 0; matrix products, arithmetic and copies ran while one was open for 5% -> 0% of each run, Pallas kernels for 0% -> 0%
where the time goes in v1:
time: 94.8 us; the launch traced here: 94 us
  Pallas kernels  34.4 us (36%)
  blocking collectives  32.2 us (34%)
  local copies, waits for them, and re-layouts  27.4 us (29%)
    all_gather x1, blocking collectives, per_device(): tok_all = lax.all_gather(tok2, 'seq', tiled=True)  32.2 us
    unnamed x57, local copies, waits for them, and re-layouts  27.4 us
    pallas_call x1, Pallas kernels, per_device(): pl.pallas_call(finish_kernel, grid=(nchunk,), out_shape=sds((length, D),...  17.2 us
    pallas_call x1, Pallas kernels, per_device(): pl.pallas_call(local_kernel, out_shape=shapes, in_specs=[sm] + [vm] * 9,...  17.2 us

profile of v1, /device:TPU:0, one launch (start us, length us, event | category | flops | bytes accessed | tf_op | source)
XLA Modules:
  0.0 94.0 jit_solution(3371457985295479331)
XLA Ops:
  0.0 1.3 %copy.10.w_in = bf16[256,1064]{1,0:T(8,128)(2,1)S(1)} copy(bf16[256,1064]{0,1:T(8,128)(2,1)} %param.11) | data formatting | bytes 1089536 | tf_op args[2]
  1.3 0.0 copy-start.8
  1.4 0.9 %copy-done.8 = bf16[512,256]{1,0:T(8,128)(2,1)S(1)} copy-done((bf16[512,256]{1,0:T(8,128)(2,1)S(1)}, bf16[512,256]{1,0:T(8,128)(2,1)}, u32[]{:S(2)}) %copy-start.8) | copy-done | bytes 262168
  2.3 0.0 copy-start.20
  2.3 0.7 copy-done.20
  3.0 0.0 copy-start.22
  3.0 0.7 copy-done.22
  3.7 0.0 copy-start.23
  3.7 0.7 copy-done.23
  4.4 0.0 copy-start.24
  4.4 0.7 copy-done.24
  5.1 0.0 copy-start.25
  5.1 0.7 copy-done.25
  5.8 0.0 copy-start.26
  5.8 0.7 copy-done.26
  6.4 0.0 copy-start.27
  6.4 0.7 copy-done.27
  7.1 17.2 %local_chains.1 = (f32[8192,128]{1,0:T(8,128)S(1)}, f32[8192,128]{1,0:T(8,128)}, bf16[1024,256]{1,0:T(8,128)(2,1)S(1)}, f32[128,128]{1,0:T(8,128)S(1)}, f32[640,...) custom-call(s32[1024]{0:T(1024)S(1)} %copy-done.20, ...), custom_call_target="tpu_custom_call" | custom-call | flops 4000000000 | bytes 16000000 | tf_op jit(solution)/shard_map/local_chains/pallas_call | solution.py:480
  24.3 0.0 copy-start
  24.3 2.0 %copy-done = f32[8192,128]{1,0:T(8,128)} copy-done((f32[8192,128]{1,0:T(8,128)}, f32[8192,128]{1,0:T(8,128)S(1)}, u32[]{:S(2)}) %copy-start) | copy-done | bytes 4194328
  26.3 0.0 copy-start.2
  26.3 1.6 %copy-done.2 = bf16[2560,512]{1,0:T(8,128)(2,1)} copy-done((bf16[2560,512]{1,0:T(8,128)(2,1)}, bf16[2560,512]{1,0:T(8,128)(2,1)S(1)}, u32[]{:S(2)}) %copy-start.2) | copy-done | bytes 2621464
  27.9 0.0 copy-start.4
  27.9 0.8 copy-done.4
  28.7 0.0 copy-start.6
  28.7 0.8 copy-done.6
  29.5 0.0 copy-start.10
  29.5 0.7 copy-done.10
  30.2 0.0 copy-start.12
  30.2 0.6 copy-done.12
  30.8 0.0 copy-start.14
  30.8 0.6 copy-done.14
  31.4 0.0 copy-start.16
  31.4 0.6 copy-done.16
  32.0 0.0 copy-start.18
  32.0 0.6 copy-done.18
  32.6 32.2 %all_gather.3.tok_all = s32[64,128]{1,0:T(8,128)S(1)} all-gather(s32[8,128]{1,0:T(8,128)S(1)} %bitcast.3), channel_id=1, replica_groups=mesh['seq'=8,'batch'=4] {'seq'}, dimensions={0}, use_global_device_ids=true | all-gather | bytes 36864 | tf_op jit(solution)/shard_map/all_gather | solution.py:460
  64.8 0.0 copy-start.1
  64.8 2.2 %copy-done.1 = f32[8192,128]{1,0:T(8,128)S(1)} copy-done((f32[8192,128]{1,0:T(8,128)S(1)}, f32[8192,128]{1,0:T(8,128)}, u32[]{:S(2)}) %copy-start.1) | copy-done | bytes 4194328
  67.0 0.0 copy-start.3
  67.0 1.7 %copy-done.3 = bf16[2560,512]{1,0:T(8,128)(2,1)S(1)} copy-done((bf16[2560,512]{1,0:T(8,128)(2,1)S(1)}, bf16[2560,512]{1,0:T(8,128)(2,1)}, u32[]{:S(2)}) %copy-start.3) | copy-done | bytes 2621464
  68.7 0.0 copy-start.5
  68.7 1.0 %copy-done.5 = bf16[1024,256]{1,0:T(8,128)(2,1)S(1)} copy-done((bf16[1024,256]{1,0:T(8,128)(2,1)S(1)}, bf16[1024,256]{1,0:T(8,128)(2,1)}, u32[]{:S(2)}) %copy-start.5) | copy-done | bytes 524312
  69.8 0.0 copy-start.7
  69.8 1.0 %copy-done.7 = bf16[4,128,512]{2,1,0:T(8,128)(2,1)S(1)} copy-done((bf16[4,128,512]{2,1,0:T(8,128)(2,1)S(1)}, bf16[4,128,512]{2,1,0:T(8,128)(2,1)}, u32[]{:S(2)}) %copy-start.7) | copy-done | bytes 524312
  70.8 0.0 copy-start.9
  70.8 0.9 %copy-done.9 = bf16[512,256]{1,0:T(8,128)(2,1)S(1)} copy-done((bf16[512,256]{1,0:T(8,128)(2,1)S(1)}, bf16[512,256]{1,0:T(8,128)(2,1)}, u32[]{:S(2)}) %copy-start.9) | copy-done | bytes 262168
  71.8 0.0 copy-start.11
  71.8 0.9 %copy-done.11 = bf16[512,256]{1,0:T(8,128)(2,1)S(1)} copy-done((bf16[512,256]{1,0:T(8,128)(2,1)S(1)}, bf16[512,256]{1,0:T(8,128)(2,1)}, u32[]{:S(2)}) %copy-start.11) | copy-done | bytes 262168
  72.7 0.0 copy-start.13
  72.7 0.9 copy-done.13
  73.6 0.0 copy-start.15
  73.6 0.8 copy-done.15
  74.5 0.0 copy-start.17
  74.5 0.8 copy-done.17
  75.3 0.0 copy-start.19
  75.3 0.8 copy-done.19
  76.1 0.0 copy-start.21
  76.1 0.7 copy-done.21
  76.7 17.2 %finish_chains.1 = bf16[1024,256]{1,0:T(8,128)(2,1)} custom-call(s32[1]{0:T(128)} %bitcast.mine, s32[1024]{0:T(1024)S(1)} %copy-done.21, s32[64,128]{1,0:T(8,128)S(1)} %all_gather.3.tok_all, f32[8192,128]{1,0:T(8,128)S(1)} %copy-done.1, f32[8192,128]{1,0:T(8,128)} %get-tuple-element.19.ybc, bf16[1024,256]{1,0:T(8,128)(2,1)S(1)} %copy-done.5, ...), custom_call_target="tpu_custom_call" | custom-call | flops 4000000000 | bytes 16000000 | tf_op jit(solution)/shard_map/finish_chains/pallas_call | solution.py:498
Async XLA Ops:
  1.3 1.0 %copy-start.8 = (bf16[512,256]{1,0:T(8,128)(2,1)S(1)}, bf16[512,256]{1,0:T(8,128)(2,1)}, u32[]{:S(2)}) copy-start(bf16[512,256]{1,0:T(8,128)(2,1)} %w_out.3) | copy-start | bytes 786436
  2.3 0.7 copy-start.20
  3.0 0.7 copy-start.22
  3.7 0.7 copy-start.23
  4.4 0.7 copy-start.24
  5.1 0.7 copy-start.25
  5.8 0.7 copy-start.26
  6.4 0.7 copy-start.27
  24.3 2.0 %copy-start = (f32[8192,128]{1,0:T(8,128)}, f32[8192,128]{1,0:T(8,128)S(1)}, u32[]{:S(2)}) copy-start(f32[8192,128]{1,0:T(8,128)S(1)} %get-tuple-element.18.yad) | copy-start | bytes 12582916
  26.3 1.6 %copy-start.2 = (bf16[2560,512]{1,0:T(8,128)(2,1)}, bf16[2560,512]{1,0:T(8,128)(2,1)S(1)}, u32[]{:S(2)}) copy-start(bf16[2560,512]{1,0:T(8,128)(2,1)S(1)} %get-tuple-element.28.xcl) | copy-start | bytes 7864324
  27.9 0.8 copy-start.4
  28.7 0.8 copy-start.6
  29.5 0.7 copy-start.10
  30.2 0.6 copy-start.12
  30.8 0.6 copy-start.14
  31.4 0.6 copy-start.16
  32.0 0.6 copy-start.18
  64.8 2.2 %copy-start.1 = (f32[8192,128]{1,0:T(8,128)S(1)}, f32[8192,128]{1,0:T(8,128)}, u32[]{:S(2)}) copy-start(f32[8192,128]{1,0:T(8,128)} %copy-done) | copy-start | bytes 12582916
  67.0 1.7 %copy-start.3 = (bf16[2560,512]{1,0:T(8,128)(2,1)S(1)}, bf16[2560,512]{1,0:T(8,128)(2,1)}, u32[]{:S(2)}) copy-start(bf16[2560,512]{1,0:T(8,128)(2,1)} %copy-done.2) | copy-start | bytes 7864324
  68.7 1.0 %copy-start.5 = (bf16[1024,256]{1,0:T(8,128)(2,1)S(1)}, bf16[1024,256]{1,0:T(8,128)(2,1)}, u32[]{:S(2)}) copy-start(bf16[1024,256]{1,0:T(8,128)(2,1)} %copy-done.4) | copy-start | bytes 1572868
  69.8 1.0 %copy-start.7 = (bf16[4,128,512]{2,1,0:T(8,128)(2,1)S(1)}, bf16[4,128,512]{2,1,0:T(8,128)(2,1)}, u32[]{:S(2)}) copy-start(bf16[4,128,512]{2,1,0:T(8,128)(2,1)} %copy-done.6) | copy-start | bytes 1572868
  70.8 0.9 %copy-start.9 = (bf16[512,256]{1,0:T(8,128)(2,1)S(1)}, bf16[512,256]{1,0:T(8,128)(2,1)}, u32[]{:S(2)}) copy-start(bf16[512,256]{1,0:T(8,128)(2,1)} %w_out.3) | copy-start | bytes 786436
  71.8 0.9 %copy-start.11 = (bf16[512,256]{1,0:T(8,128)(2,1)S(1)}, bf16[512,256]{1,0:T(8,128)(2,1)}, u32[]{:S(2)}) copy-start(bf16[512,256]{1,0:T(8,128)(2,1)} %copy-done.10) | copy-start | bytes 786436
  72.7 0.9 copy-start.13
  73.6 0.8 copy-start.15
  74.5 0.8 copy-start.17
  75.3 0.8 copy-start.19
  76.1 0.7 copy-start.21

commit v2 on v1

v2 whole, which is shorter than its diff:
```python
import jax
import jax.numpy as jnp
from jax import lax
from jax.experimental import pallas as pl
from jax.experimental.pallas import tpu as pltpu
from jax.sharding import PartitionSpec as P

D = 256
E = 512
NS = 16
H = 8
KW = 4
SYM = 5
LOG2E = 1.4426950408889634
EPSILON = 1e-05
CH = 128

F32 = jnp.float32
BF16 = jnp.bfloat16

CHAINS = ((0, 0, 0), (0, 1, 1), (1, 0, 1), (1, 1, 0))


def iota(shape, dim):
    return lax.broadcasted_iota(jnp.int32, shape, dim)


def nn(a, b, **kw):
    return lax.dot_general(a, b, (((1,), (0,)), ((), ())), preferred_element_type=F32, **kw)


def nt(a, b, **kw):
    return lax.dot_general(a, b, (((1,), (1,)), ((), ())), preferred_element_type=F32, **kw)


def split(value):
    high = value.astype(BF16)
    low = (value - high.astype(F32)).astype(BF16)
    return high, low


def softplus(x):
    return jnp.maximum(x, 0.0) + jnp.log1p(jnp.exp(-jnp.abs(x)))


def silu_half(half):
    return half + half * jnp.tanh(half)


def tap_row(direction, j):
    return j if direction == 0 else 2 * (KW - 1) - j


def window_onehot(rows):
    sub = iota((8, CH), 0).astype(F32)
    blocks = [jnp.where(row == sub, 1.0, 0.0) for row in rows]
    blocks.append(jnp.zeros((8, CH), F32))
    stacked = jnp.concatenate(blocks + blocks, axis=0)
    return stacked.T.astype(BF16)


def shifted(tok, offset, rows):
    if offset == 0:
        return tok
    lane = iota((rows, CH), 1)
    row = iota((rows, CH), 0)
    moved = pltpu.roll(tok, (-offset) % CH, 1)
    if offset < 0:
        other = pltpu.roll(moved, 1, 0)
        crossing = lane < -offset
        outside = crossing & (row == 0)
    else:
        other = pltpu.roll(moved, rows - 1, 0)
        crossing = lane >= CH - offset
        outside = crossing & (row == rows - 1)
    return jnp.where(outside, 5.0, jnp.where(crossing, other, moved))


def pick(values, u):
    out = values[0]
    for k in range(1, SYM):
        out = jnp.where(u == k, values[k], out)
    return out


def tile_at(ref, row):
    return ref[pl.ds(pl.multiple_of(row, 8), 8), :]


def table_kernel(
    emb_h, w_in_h, w_out_h, cw_h, bias_h, rate_h, skip_h, gain_h,
    atab, gtab, zg, cst, lac, tw, xch, xcl, wflip, embk,
    emb, w_in, w_out, cw, bias, rate, skip, gain, emb16, sems,
):
    sources = (emb_h, w_in_h, w_out_h, cw_h, bias_h, rate_h, skip_h, gain_h)
    targets = (emb, w_in, w_out, cw, bias, rate, skip, gain)
    copies = [
        pltpu.make_async_copy(a, b, sems.at[i]) for i, (a, b) in enumerate(zip(sources, targets))
    ]
    for copy in copies:
        copy.start()
    for copy in copies:
        copy.wait()
    highest = lax.Precision.HIGHEST
    emb16[...] = jnp.zeros_like(emb16)
    e32 = emb[...].astype(F32)
    emb16[0:SYM, :] = e32
    for v in range(4):
        emb16[8 + v : 9 + v, :] = e32[3 - v : 4 - v, :]
    emb16[12:13, :] = e32[4:5, :]
    embs = emb16[...].astype(BF16)
    z16 = nt(embs, w_in[0:E, :]).astype(BF16).astype(F32)
    x16 = nt(embs, w_in[E : 2 * E, :]).astype(BF16).astype(F32)
    rest = nt(embs, w_in[2 * E :, :]).astype(BF16)
    nrest = 2 * NS + H
    expand = jnp.where(
        iota((nrest, E), 0) == (iota((nrest, E), 1) >> 6) + 2 * NS, 1.0, 0.0
    ).astype(BF16)
    heads = jnp.where(iota((H, E), 0) == (iota((H, E), 1) >> 6), 1.0, 0.0)
    r_exp = nn(rest, expand)
    bias_e = nn(bias[...], heads, precision=highest)
    rate_e = nn(rate[...], heads, precision=highest)
    skip_e = nn(skip[...], heads, precision=highest)
    shift = jnp.where(
        iota((nrest, nrest), 0) + NS == iota((nrest, nrest), 1),
        jnp.where(iota((nrest, nrest), 0) < NS, 1.0, 0.0),
        0.0,
    ).astype(BF16)
    rest_b = nn(rest, shift).astype(BF16)
    cb = nt(rest_b, rest)
    sz = z16 * (0.5 + 0.5 * jnp.tanh(0.5 * z16))
    for s in range(2):
        for i in range(4):
            zg[pl.ds(s * 4 + i, 8, stride=8), :] = sz[8 * s : 8 * s + 8, 128 * i : 128 * i + 128]
    pick_r = jnp.where(
        iota((H, nrest), 0) + 2 * NS == iota((H, nrest), 1), 1.0, 0.0
    ).astype(BF16)
    r_t = nt(pick_r, rest)
    eye = jnp.where(iota((H, H), 0) == iota((H, H), 1), 1.0, 0.0)
    bias_t = nt(eye, bias[...], precision=highest)
    rate_t = nt(eye, rate[...], precision=highest)
    for q, (d, s, k) in enumerate(CHAINS):
        dt = softplus(r_exp[8 * s : 8 * s + 8, :] + bias_e[k : k + 1, :])
        a = jnp.exp(-rate_e[k : k + 1, :] * dt)
        for i in range(4):
            lanes = slice(128 * i, 128 * i + 128)
            atab[pl.ds(d * 64 + s * 4 + i, 8, stride=8), :] = a[:, lanes]
            cst[d * 8 + s * 4 + i : d * 8 + s * 4 + i + 1, :] = skip_e[k : k + 1, lanes]
            cst[16 + d * 8 + s * 4 + i : 17 + d * 8 + s * 4 + i, :] = gain[k : k + 1, lanes]
        for u in range(SYM):
            g = cb[8 * s : 8 * s + 8, 8 * s + u : 8 * s + u + 1] * dt
            for i in range(4):
                gtab[pl.ds((d * SYM + u) * 64 + s * 4 + i, 8, stride=8), :] = g[
                    :, 128 * i : 128 * i + 128
                ]
        la = (
            -rate_t[:, k : k + 1] * softplus(r_t[:, 8 * s : 8 * s + 8] + bias_t[:, k : k + 1])
        ) * LOG2E
        for v in range(SYM):
            lac[(d * SYM + v) * 16 + s * 8 : (d * SYM + v) * 16 + s * 8 + 8, :] = jnp.broadcast_to(
                la[:, v : v + 1], (8, CH)
            )
        xs = x16[8 * s : 8 * s + 8, :]
        blocks = [jnp.zeros((8, E), F32)] * 8
        for j in range(KW):
            blocks[tap_row(d, j)] = (0.5 * cw[k, j : j + 1, :]) * xs
        high, low = split(jnp.concatenate(blocks, axis=0))
        tw[q, 0:64, :] = high
        tw[q, 64:128, :] = low
        code = iota((CH, CH), 0).astype(F32)
        lane = iota((CH, CH), 1) & 63
        slot = lane >> 3
        sym = (lane & 7).astype(F32)
        d0 = jnp.floor((code + 0.5) * (1.0 / 25.0))
        d01 = jnp.floor((code + 0.5) * (1.0 / 5.0))
        digits = (d0, d01 - 5.0 * d0, code - 5.0 * d01)
        hot = jnp.zeros((CH, CH), F32)
        for j in range(KW - 1):
            hot = jnp.where(
                slot == tap_row(d, j), jnp.where(sym == digits[j], 1.0, 0.0), hot
            )
        partial = nn(hot.astype(BF16), tw[q])
        last = blocks[tap_row(d, KW - 1)]
        for v in range(SYM):
            high, low = split(silu_half(partial + last[v : v + 1, :]))
            xch[(q * SYM + v) * CH : (q * SYM + v + 1) * CH, :] = high
            xcl[(q * SYM + v) * CH : (q * SYM + v + 1) * CH, :] = low
    flip = jnp.where(iota((D, D), 0) + iota((D, D), 1) == D - 1, 1.0, 0.0).astype(BF16)
    embk[...] = jnp.concatenate(
        [jnp.zeros((24, D), F32), emb16[0:8, :], jnp.zeros((96, D), F32)], axis=0
    ).astype(BF16)
    wflip[...] = nn(w_out[...], flip).astype(BF16)


def conv_kernel(tok_v, tw, embk, yad, ybc, feat):
    nchunk = tok_v.shape[0]
    tok = tok_v[...].astype(F32)
    shifts = [shifted(tok, o, nchunk) for o in range(-3, 4)]
    for c in range(nchunk):
        hot = window_onehot([sh[c : c + 1, :] for sh in shifts])
        feat[c * CH : (c + 1) * CH, :] = nn(hot, embk[...]).astype(BF16)
        for q, (d, s, k) in enumerate(CHAINS):
            x = silu_half(nn(hot, tw[q]))
            ref = (yad, ybc)[d]
            for i in range(4):
                ref[pl.ds(c * 8 * CH + s * 4 + i, CH, stride=8), :] = x[:, 128 * i : 128 * i + 128]
    total = nchunk * CH
    yad[0:24, :] = jnp.zeros((24, CH), F32)
    ybc[total * 8 - 24 : total * 8, :] = jnp.zeros((24, CH), F32)


def scan_kernel(tok_s, atab, gtab, cst, xad, xbc, yad, ybc, pst):
    total = tok_s.shape[0]
    nchunk = total // CH
    skip0 = cst[0:8, :]
    skip1 = cst[8:16, :]

    def advance(direction, src, ref, skip_t, t, state):
        u = tok_s[t]
        x = tile_at(src, t * 8)
        a = tile_at(atab, direction * 64 + u * 8)
        new = [
            a * state[w] + tile_at(gtab, (direction * SYM + w) * 64 + u * 8) * x
            for w in range(SYM)
        ]
        ref[pl.ds(pl.multiple_of(t * 8, 8), 8), :] = pick(new, u) + skip_t * x
        return new, a

    unroll = 8

    def group(g, carry):
        ya, yb, pa, pb = carry
        ya, yb = list(ya), list(yb)
        for i in range(unroll):
            n = g * unroll + i
            ya, a0 = advance(0, xad, yad, skip0, n, ya)
            yb, a1 = advance(1, xbc, ybc, skip1, total - 1 - n, yb)
            if i < 3:
                a0 = jnp.where(g == 0, 1.0, a0)
                a1 = jnp.where(g == 0, 1.0, a1)
            pa = pa * a0
            pb = pb * a1
        return tuple(ya), tuple(yb), pa, pb

    def chunk(c, carry):
        pst[pl.ds(pl.multiple_of(c * 8, 8), 8), :] = carry[2]
        pst[pl.ds(pl.multiple_of((2 * nchunk - 1 - c) * 8, 8), 8), :] = carry[3]
        per = CH // unroll
        return lax.fori_loop(c * per, (c + 1) * per, group, carry)

    zero = jnp.zeros((8, CH), F32)
    one = jnp.ones((8, CH), F32)
    lax.fori_loop(0, nchunk, chunk, ((zero,) * SYM, (zero,) * SYM, one, one))


def history_kernel(
    mine, tok_s, tok_all, atab, gtab, cst, lac, tw, xch, xcl,
    ycar, yrim,
    tok_f, code, tri, hist, svec, xrim,
):
    rows = tok_all.shape[0]
    own = rows // 8
    j = mine[0]
    for b in range(own):
        slot = (j ^ b) * 8
        tok_f[3, 8 * b : 8 * b + 8, :] = tok_all[pl.ds(pl.multiple_of(slot, 8), 8), :].astype(F32)
    tok = tok_f[3]
    for o in (-3, -2, -1, 1, 2, 3):
        tok_f[3 + o] = shifted(tok, o, rows)
    lane = iota((rows, CH), 1)
    row = iota((rows, CH), 0)
    lane_f = lane.astype(F32)
    before = 25.0 * tok_f[0] + 5.0 * tok_f[1] + tok_f[2]
    after = 25.0 * tok_f[6] + 5.0 * tok_f[5] + tok_f[4]
    code[0] = jnp.where((row == 0) & (lane < 3), 125.0 + lane_f, before)
    code[1] = jnp.where((row == rows - 1) & (lane >= CH - 3), lane_f, after)
    si = iota((CH, CH), 0)
    ri = iota((CH, CH), 1)
    ones = jnp.ones((CH, CH), F32)
    tri[0] = jnp.concatenate([jnp.where(si > ri, 1.0, 0.0), ones], axis=1).astype(BF16)
    tri[1] = jnp.concatenate([jnp.where(si < ri, 1.0, 0.0), ones], axis=1).astype(BF16)
    hist[...] = jnp.zeros_like(hist)
    sub8 = iota((8, CH), 0).astype(F32)
    subc = iota((CH, CH), 0).astype(F32)

    def block(b, off):
        side = jnp.where(b >= j, 1, 0)
        index = jnp.where(b >= j, b + 1, j - 1 - b)
        off = off * jnp.where(b == j, 0.0, 1.0)
        use_prefix = side.astype(F32)
        at = pl.ds(pl.multiple_of(index * 8, 8), 8)
        tk = tok_f[3, at, :]
        cd = code[side, at, :]
        hots = [jnp.where(tk[m : m + 1, :] == sub8, 1.0, 0.0) for m in range(8)]
        counts = nn(jnp.concatenate(hots, axis=0).astype(BF16), tri[side])
        totals = [counts[8 * m : 8 * m + 8, CH:] for m in range(8)]
        prefix = [jnp.zeros((8, CH), F32)]
        for m in range(8):
            prefix.append(prefix[-1] + totals[m])
        las = [lac[pl.ds(pl.multiple_of((side * SYM + v) * 16, 16), 16), :] for v in range(SYM)]
        acc = jnp.zeros((160, CH), F32)
        for pair in range(4):
            lefts, rights = [], []
            for m in (2 * pair, 2 * pair + 1):
                suffix = prefix[8] - prefix[m + 1]
                inside = suffix + use_prefix * (prefix[m] - suffix)
                count = counts[8 * m : 8 * m + 8, :CH] + off + inside
                exponent = las[0] * count[0:1, :]
                for v in range(1, SYM):
                    exponent = exponent + las[v] * count[v : v + 1, :]
                weight = jnp.exp2(exponent)
                masked = jnp.concatenate(
                    [jnp.where(tk[m : m + 1, :] == float(v), weight, 0.0) for v in range(SYM)],
                    axis=0,
                )
                high, low = split(masked)
                lefts.append(jnp.concatenate([high, low], axis=0))
                rights.append(jnp.where(cd[m : m + 1, :] == subc, 1.0, 0.0).astype(BF16))
            acc = acc + nt(
                jnp.concatenate(lefts, axis=1), jnp.concatenate(rights, axis=1)
            )
        hist[side] = hist[side] + acc
        return off + prefix[8]

    lax.fori_loop(0, own - 1, block, jnp.zeros((8, CH), F32))

    last8 = rows - 8
    mine8 = pl.ds(pl.multiple_of(j * 8, 8), 8)
    xs = {}
    for d in range(2):
        edge = 0 if d == 0 else 7
        seq_at = pl.ds(0 if d == 0 else last8, 8)
        hot_seq = window_onehot([tok_f[o, seq_at, :][edge : edge + 1, :] for o in range(7)])
        hot_own = window_onehot([tok_f[o, mine8, :][edge : edge + 1, :] for o in range(7)])
        for s in range(2):
            q = 2 * d + s
            xseq = silu_half(nn(hot_seq, tw[q]))
            xown = silu_half(nn(hot_own, tw[q]))
            if d == 0:
                xs[q] = pltpu.roll(xseq[0:8, :], 5, 0)
            else:
                xs[q] = xseq[CH - 8 :, :]
            for n in range(KW - 1):
                t = n if d == 0 else CH - 1 - n
                for i in range(4):
                    at = (d * 3 + n) * 8 + s * 4 + i
                    xrim[at : at + 1, :] = xown[t : t + 1, 128 * i : 128 * i + 128]
    diag = iota((H, E), 0) == (iota((H, E), 1) >> 6)
    sub16 = iota((16, E), 0)
    for q in range(4):
        d, s = q // 2, q % 2
        rim = jnp.concatenate([jnp.zeros((8, E), F32), xs[q]], axis=0)
        rim_h, rim_l = split(rim)
        for v in range(SYM):
            start = (q * SYM + v) * CH
            body = slice(start, start + CH - 16)
            tail = slice(start + CH - 16, start + CH)
            tail_h = jnp.where(sub16 >= 13, rim_h.astype(F32), xch[tail, :].astype(F32))
            tail_l = jnp.where(sub16 >= 13, rim_l.astype(F32), xcl[tail, :].astype(F32))
            table_h = jnp.concatenate([xch[body, :], tail_h.astype(BF16)], axis=0)
            table_l = jnp.concatenate([xcl[body, :], tail_l.astype(BF16)], axis=0)
            at = v * 16 + s * 8
            w = hist[d, at : at + 8, :] + hist[d, 80 + at : 88 + at, :]
            high, low = split(w)
            both = jnp.concatenate([high.astype(F32), low.astype(F32)], axis=0).astype(BF16)
            one = nn(both, table_h)
            two = nn(both, table_l)
            full = one[0:8, :] + one[8:16, :] + two[0:8, :]
            vec = jnp.sum(jnp.where(diag, full, 0.0), axis=0, keepdims=True)
            for i in range(4):
                at = (d * SYM + v) * 8 + s * 4 + i
                svec[at : at + 1, :] = vec[:, 128 * i : 128 * i + 128]
    total = tok_s.shape[0]
    for d in range(2):
        state = []
        for w in range(SYM):
            value = jnp.zeros((8, CH), F32)
            for v in range(SYM):
                at = (d * SYM + w) * 64 + v * 8
                sat = (d * SYM + v) * 8
                value = value + gtab[at : at + 8, :] * svec[sat : sat + 8, :]
            state.append(value)
        skip_t = cst[d * 8 : d * 8 + 8, :]
        for n in range(KW - 1):
            u = tok_s[n if d == 0 else total - 1 - n]
            x = xrim[(d * 3 + n) * 8 : (d * 3 + n) * 8 + 8, :]
            a = tile_at(atab, d * 64 + u * 8)
            state = [
                a * state[w] + tile_at(gtab, (d * SYM + w) * 64 + u * 8) * x
                for w in range(SYM)
            ]
            yrim[(d * 3 + n) * 8 : (d * 3 + n) * 8 + 8, :] = pick(state, u) + skip_t * x
        for w in range(SYM):
            ycar[(d * SYM + w) * 8 : (d * SYM + w) * 8 + 8, :] = state[w]


def finish_kernel(
    tok_s, yad, ybc, feat, atab, zg, cst, pst, ycar, yrim, w_out, wflip,
    out,
    gad, gbc, mix,
):
    step = pl.program_id(0)
    nchunk = pl.num_programs(0)
    first = step * CH
    unroll = 8

    def advance(d, ref, dest, n, decay, lead):
        local = n if d == 0 else CH - 1 - n
        u = tok_s[first + local]
        a = tile_at(atab, d * 64 + u * 8)
        if lead is not None:
            a = jnp.where(lead, 1.0, a)
        decay = decay * a
        y = tile_at(ref, local * 8) + decay * tile_at(ycar, d * SYM * 8 + u * 8)
        dest[pl.ds(pl.multiple_of(local * 8, 8), 8), :] = y * tile_at(zg, u * 8)
        return decay

    def group(g, carry):
        pa, pb = carry
        for i in range(unroll):
            n = g * unroll + i
            lead0 = (g == 0) & (step == 0) if i < 3 else None
            lead1 = (g == 0) & (step == nchunk - 1) if i < 3 else None
            pa = advance(0, yad, gad, n, pa, lead0)
            pb = advance(1, ybc, gbc, n, pb, lead1)
        return pa, pb

    lax.fori_loop(
        0, CH // unroll, group, (tile_at(pst, step * 8), tile_at(pst, (nchunk + step) * 8))
    )

    @pl.when(step == 0)
    def _():
        for n in range(3):
            gad[n * 8 : n * 8 + 8, :] = yrim[n * 8 : n * 8 + 8, :] * tile_at(zg, tok_s[n] * 8)

    @pl.when(step == nchunk - 1)
    def _():
        for n in range(3):
            at = (CH - 1 - n) * 8
            gbc[at : at + 8, :] = yrim[24 + n * 8 : 32 + n * 8, :] * tile_at(
                zg, tok_s[first + CH - 1 - n] * 8
            )

    mean = jnp.where(
        ((iota((2 * CH, CH), 0) & 127) >> 6) == (iota((2 * CH, CH), 1) >> 6), 1.0 / 64.0, 0.0
    ).astype(BF16)
    normed = None
    for d, ref in ((0, gad), (1, gbc)):
        g = ref[...]
        high, low = split(g * g)
        meansq = nn(jnp.concatenate([high, low], axis=1), mean)
        scaled = (g * lax.rsqrt(meansq + EPSILON)).reshape(CH, 8, CH) * cst[
            16 + d * 8 : 24 + d * 8, :
        ][None]
        normed = scaled if normed is None else normed + scaled
    mix[...] = normed.reshape(CH * 8, CH)
    parts = [mix[pl.ds(i, CH, stride=8), :].astype(BF16) for i in range(8)]
    mine_out = nn(jnp.concatenate(parts[0:4], axis=1), w_out[...]).astype(BF16).astype(F32)
    other = nn(jnp.concatenate(parts[4:8], axis=1), wflip[...]).astype(BF16).astype(F32)
    out[...] = (feat[...].astype(F32) + mine_out + other).astype(BF16)


def per_device(
    token_ids,
    embed_table,
    input_weight_matrix,
    output_weight_matrix,
    conv_weight,
    dt_bias,
    decay_rate,
    skip_gain,
    norm_gain,
):
    length = token_ids.shape[0]
    nchunk = length // CH
    own = lax.axis_size("seq")
    tok2 = token_ids.reshape(nchunk, CH)
    rounds = own.bit_length() - 1
    rows = own * nchunk
    vm = pl.BlockSpec(memory_space=pltpu.VMEM)
    sm = pl.BlockSpec(memory_space=pltpu.SMEM)
    hbm = pl.BlockSpec(memory_space=pl.ANY)
    sds = jax.ShapeDtypeStruct
    mib = 1024 * 1024

    def exchanged(blocks, bit):
        route = [(i, i ^ (1 << bit)) for i in range(own)]
        return jnp.concatenate([blocks, lax.ppermute(blocks, "seq", route)], axis=0)

    def params(limit):
        return pltpu.CompilerParams(vmem_limit_bytes=limit * mib)

    def cost(flops, moved):
        return pl.CostEstimate(flops=flops, bytes_accessed=moved, transcendentals=0)

    blocks = exchanged(tok2, 0)
    table_shapes = (
        sds((2 * 64, CH), F32),
        sds((2 * SYM * 64, CH), F32),
        sds((64, CH), F32),
        sds((32, CH), F32),
        sds((2 * SYM * 16, CH), F32),
        sds((4, CH, E), BF16),
        sds((4 * SYM * CH, E), BF16),
        sds((4 * SYM * CH, E), BF16),
        sds((E, D), BF16),
        sds((CH, D), BF16),
    )
    weights = (
        embed_table, input_weight_matrix.T, output_weight_matrix, conv_weight, dt_bias, decay_rate,
        skip_gain, norm_gain,
    )
    atab, gtab, zg, cst, lac, tw, xch, xcl, wflip, embk = pl.pallas_call(
        table_kernel,
        out_shape=table_shapes,
        in_specs=[hbm] * 8,
        out_specs=[vm] * len(table_shapes),
        scratch_shapes=[pltpu.VMEM(w.shape, w.dtype) for w in weights]
        + [pltpu.VMEM((16, D), F32), pltpu.SemaphoreType.DMA((8,))],
        compiler_params=params(56),
        cost_estimate=cost(1_000_000_000, 8_000_000),
        name="symbol_tables",
    )(*weights)
    blocks, tw, embk = lax.optimization_barrier((blocks, tw, embk))
    if rounds > 1:
        blocks = exchanged(blocks, 1)
    xad, xbc, feat = pl.pallas_call(
        conv_kernel,
        out_shape=(sds((length * 8, CH), F32), sds((length * 8, CH), F32), sds((length, D), BF16)),
        in_specs=[vm] * 3,
        out_specs=[vm] * 3,
        compiler_params=params(20),
        cost_estimate=cost(2_000_000_000, 9_000_000),
        name="convolve",
    )(tok2, tw, embk)
    blocks, xad, xbc = lax.optimization_barrier((blocks, xad, xbc))
    for bit in range(2, rounds):
        blocks = exchanged(blocks, bit)
    yad, ybc, pst = pl.pallas_call(
        scan_kernel,
        out_shape=(
            sds((length * 8, CH), F32),
            sds((length * 8, CH), F32),
            sds((2 * nchunk * 8, CH), F32),
        ),
        in_specs=[sm] + [vm] * 5,
        out_specs=[vm] * 3,
        input_output_aliases={4: 0, 5: 1},
        compiler_params=params(20),
        cost_estimate=cost(4_000_000_000, 16_000_000),
        name="scan_block",
    )(token_ids, atab, gtab, cst, xad, xbc)
    blocks, yad, ybc, pst = lax.optimization_barrier((blocks, yad, ybc, pst))
    mine = lax.axis_index("seq").reshape(1).astype(jnp.int32)
    ycar, yrim = pl.pallas_call(
        history_kernel,
        out_shape=(sds((2 * SYM * 8, CH), F32), sds((2 * 3 * 8, CH), F32)),
        in_specs=[sm, sm] + [vm] * 8,
        out_specs=[vm] * 2,
        scratch_shapes=[
            pltpu.VMEM((7, rows, CH), F32),
            pltpu.VMEM((2, rows, CH), F32),
            pltpu.VMEM((2, CH, 2 * CH), BF16),
            pltpu.VMEM((2, 160, CH), F32),
            pltpu.VMEM((2 * SYM * 8, CH), F32),
            pltpu.VMEM((2 * 3 * 8, CH), F32),
        ],
        compiler_params=params(20),
        cost_estimate=cost(2_000_000_000, 6_000_000),
        name="history",
    )(mine, token_ids, blocks, atab, gtab, cst, lac, tw, xch, xcl)
    chunk_spec = pl.BlockSpec((CH * 8, CH), lambda i: (i, 0))
    out_spec = pl.BlockSpec((CH, D), lambda i: (i, 0))
    return pl.pallas_call(
        finish_kernel,
        grid=(nchunk,),
        out_shape=sds((length, D), BF16),
        in_specs=[sm, chunk_spec, chunk_spec, out_spec] + [vm] * 8,
        out_specs=out_spec,
        scratch_shapes=[pltpu.VMEM((CH * 8, CH), F32)] * 3,
        compiler_params=params(20),
        cost_estimate=cost(4_000_000_000, 16_000_000),
        name="finish",
    )(
        token_ids, yad, ybc, feat, atab, zg, cst, pst, ycar, yrim, output_weight_matrix, wflip
    )


def solution(mesh):
    placed = (P(("batch", "seq")), P(), P(), P(), P(), P(), P(), P(), P())
    return jax.shard_map(
        per_device, mesh=mesh, in_specs=placed, out_specs=P(("batch", "seq"), None), check_vma=False
    )
```

time: 94.8 us -> 48 us (0.51)
  blocking collectives: 32.2 us -> 0 us
  local copies, waits for them, and re-layouts: 27.4 us -> 2.62 us
  starting transfers between devices: 0 us -> 7.2 us
  Pallas kernels: 34.4 us -> 36.9 us
    all_gather x1 -> x0, blocking collectives: 32.2 us -> none  [per_device(): tok_all = lax.all_gather(tok2, 'seq', tiled=True)]
    unnamed x57 -> x28, local copies, waits for them, and re-layouts: 27.4 us -> 2.62 us
    pallas_call x1 -> x4, Pallas kernels: 17.2 us -> 24.4 us  [the longest x1 11.9 us: per_device(): pl.pallas_call(scan_kernel, out_shape=(sds((length * 8, CH), F32), sds((l...]
    ppermute x0 -> x3, starting transfers between devices: none -> 7.2 us  [exchanged(): return jnp.concatenate([blocks, lax.ppermute(blocks, 'seq', route)], axis=0)]
    pallas_call x1, Pallas kernels: 17.2 us -> 12.4 us  [per_device(): pl.pallas_call(finish_kernel, grid=(nchunk,), out_shape=sds((length, D),...]
  transfers between devices with their start and end apart: 0 -> 3, of which waited for: 0 -> 0; matrix products, arithmetic and copies ran while one was open for 0% -> 0% of each run, Pallas kernels for 0% -> 41%
where the time goes in v2:
time: 48 us; the launch traced here: 47.7 us
  Pallas kernels  36.9 us (77%)
  starting transfers between devices  7.2 us (15%)
  local copies, waits for them, and re-layouts  2.62 us (5%)
  other arithmetic  0.74 us (2%)
    pallas_call x1, Pallas kernels, per_device(): pl.pallas_call(finish_kernel, grid=(nchunk,), out_shape=sds((length, D),...  12.4 us
    pallas_call x1, Pallas kernels, per_device(): pl.pallas_call(scan_kernel, out_shape=(sds((length * 8, CH), F32), sds((l...  11.9 us
    ppermute x3, starting transfers between devices, exchanged(): return jnp.concatenate([blocks, lax.ppermute(blocks, 'seq', route)], axis=0)  7.2 us
    pallas_call x1, Pallas kernels, per_device(): pl.pallas_call(table_kernel, out_shape=table_shapes, in_specs=[hbm] * 8,...  5.78 us
    pallas_call x1, Pallas kernels, per_device(): pl.pallas_call(history_kernel, out_shape=(sds((2 * SYM * 8, CH), F32), sd...  4.84 us
    unnamed x28, local copies, waits for them, and re-layouts  2.62 us
    pallas_call x1, Pallas kernels, per_device(): pl.pallas_call(conv_kernel, out_shape=(sds((length * 8, CH), F32), sds((l...  1.96 us
  transfers between devices with their start and end apart: 3, of which 0 were waited for; matrix products, arithmetic and copies ran while one was open for 0% of the time, Pallas kernels for 41%

profile of v2, /device:TPU:0, one launch (start us, length us, event | category | flops | bytes accessed | tf_op | source)
XLA Modules:
  0.0 47.7 jit_solution(10137109735460283114)
XLA Ops:
  0.0 3.0 %collective-permute-start = (s32[8,128]{1,0:T(8,128)}, s32[8,128]{1,0:T(8,128)S(1)}, u32[]{:S(2)}, u32[]{:S(2)}) collective-permute-start(s32[8,128]{1,0:T(8,128)} %bitcast.3), channel_id=1, source_target_pairs={{0,4},{4,0},{8,12},{12,8},{16,20},{20,16},{24,28},{28,24},{1,5},{5... | collective-permute-start | bytes 12296 | tf_op jit(solution)/shard_map/ppermute | solution.py:489
  3.0 5.8 %symbol_tables.1 = (f32[128,128]{1,0:T(8,128)}, f32[640,128]{1,0:T(8,128)}, f32[64,128]{1,0:T(8,128)}, f32[32,128]{1,0:T(8,128)}, f32[160,128]{1,0:T(8,128)}, /*...) custom-call(bf16[5,256]{1,0:T(8,128)(2,1)} %emb_h.1, ...), custom_call_target="tpu_custom_call" | custom-call | flops 1000000000 | bytes 8000000 | tf_op jit(solution)/shard_map/symbol_tables/pallas_call | solution.py:514
  8.8 0.0 copy-start.1
  8.8 0.0 copy-start.11
  8.8 0.0 collective-permute-done
  8.8 0.7 %pad_add_fusion.2 = s32[16,128]{1,0:T(8,128)S(1)} fusion(s32[8,128]{1,0:T(8,128)S(1)} %collective-permute-done, s32[8,128]{1,0:T(8,128)} %bitcast.4), kind=kLoop, calls=%fused_computation.2 | loop fusion | flops 2048 | bytes 16384 | tf_op jit(solution)/shard_map/concatenate | solution.py:489
  9.5 1.6 %collective-permute-start.1 = (s32[16,128]{1,0:T(8,128)S(1)}, s32[16,128]{1,0:T(8,128)S(1)}, u32[]{:S(2)}, u32[]{:S(2)}) collective-permute-start(s32[16,128]{1,0:T(8,128)S(1)} %pad_add_fusion.2), channel_id=1, source_target_pairs={{0,8},{4,12},{8,0},{12,4},{16,24},{20,28},{24,16},{28,20},{1,9},{5... | collective-permute-start | bytes 24584 | tf_op jit(solution)/shard_map/ppermute | solution.py:489
  11.1 0.0 copy-start
  11.1 0.7 %copy-done = s32[1024]{0:T(1024)S(1)} copy-done((s32[1024]{0:T(1024)S(1)}, s32[1024]{0:T(1024)}, u32[]{:S(2)}) %copy-start) | copy-done | bytes 4120
  11.8 0.0 copy-start.5
  11.8 1.0 %copy-done.5 = bf16[4,128,512]{2,1,0:T(8,128)(2,1)S(1)} copy-done((bf16[4,128,512]{2,1,0:T(8,128)(2,1)S(1)}, bf16[4,128,512]{2,1,0:T(8,128)(2,1)}, u32[]{:S(2)}) %copy-start.5) | copy-done | bytes 524312
  12.8 0.0 copy-start.12
  12.8 0.8 %copy-done.12 = bf16[128,256]{1,0:T(8,128)(2,1)S(1)} copy-done((bf16[128,256]{1,0:T(8,128)(2,1)S(1)}, bf16[128,256]{1,0:T(8,128)(2,1)}, u32[]{:S(2)}) %copy-start.12) | copy-done | bytes 65560
  13.7 0.0 copy-start.7
  13.7 0.0 copy-start.9
  13.7 2.0 %convolve.1 = (f32[8192,128]{1,0:T(8,128)S(1)}, f32[8192,128]{1,0:T(8,128)S(1)}, bf16[1024,256]{1,0:T(8,128)(2,1)S(1)}) custom-call(s32[8,128]{1,0:T(8,128)S(1)} %bitcast.5, bf16[4,128,512]{2,1,0:T(8,128)(2,1)S(1)} %copy-done.5, bf16[128,256]{1,0:T(8,128)(2,1)S(1)} %copy-done.12), custom_call_target="tpu_custom_call" | custom-call | flops 2000000000 | bytes 9000000 | tf_op jit(solution)/shard_map/convolve/pallas_call | solution.py:528
  15.6 0.0 collective-permute-done.1
  15.7 2.7 %collective-permute-start.2 = (s32[32,128]{1,0:T(8,128)S(1)}, s32[32,128]{1,0:T(8,128)S(1)}, u32[]{:S(2)}, u32[]{:S(2)}) collective-permute-start(s32[32,128]{1,0:T(8,128)S(1)} %pad_add_fusion.1), channel_id=1, source_target_pairs={{0,16},{4,20},{8,24},{12,28},{16,0},{20,4},{24,8},{28,12},{1,17},{... | collective-permute-start | bytes 49160 | tf_op jit(solution)/shard_map/ppermute | solution.py:489
  18.3 0.0 copy-done.1
  18.3 0.0 copy-done.11
  18.3 0.0 copy-done.7
  18.3 0.0 copy-done.9
  18.3 0.0 copy-start.3
  18.3 0.0 copy-start.4
  18.4 0.0 copy-start.6
  18.4 0.0 copy-start.8
  18.4 11.9 %scan_block.1 = (f32[8192,128]{1,0:T(8,128)S(1)}, f32[8192,128]{1,0:T(8,128)S(1)}, f32[128,128]{1,0:T(8,128)S(1)}) custom-call(s32[1024]{0:T(1024)S(1)} %copy-done.1, f32[128,128]{1,0:T(8,128)S(1)} %copy-done.9, f32[640,128]{1,0:T(8,128)S(1)} %copy-done.7, f32[32,128]{1,0:T(8,128)S(1)} %copy-done.11, ...), custom_call_target="tpu_custom_call", output_to_operand_aliasing={{0}: (4, {}), {1}: (5, {})} | custom-call | flops 4000000000 | bytes 16000000 | tf_op jit(solution)/shard_map/scan_block/pallas_call | solution.py:540
  30.2 0.0 copy-start.2
  30.3 0.0 copy-start.10
  30.3 0.0 copy-start.13
  30.3 0.0 collective-permute-done.2
  30.3 0.0 copy-done.3
  30.3 0.0 copy-done.4
  30.3 0.0 copy-done.6
  30.3 0.0 copy-done.8
  30.3 4.8 %history.1 = (f32[80,128]{1,0:T(8,128)S(1)}, f32[48,128]{1,0:T(8,128)S(1)}) custom-call(s32[1]{0:T(128)} %bitcast.2.mine, s32[1024]{0:T(1024)S(1)} %copy-done.1, s32[64,128]{1,0:T(8,128)S(1)} %pad_add_fusion.tok_all, f32[128,128]{1,0:T(8,128)S(1)} %copy-done.9, f32[640,128]{1,0:T(8,128)S(1)} %copy-done.7, f32[32,128]{1,0:T(8,128)S(1)} %copy-done.11, ...), custom_call_target="tpu_custom_call" | custom-call | flops 2000000000 | bytes 6000000 | tf_op jit(solution)/shard_map/history/pallas_call | solution.py:556
  35.2 0.0 copy-done.2
  35.2 0.0 copy-done.10
  35.2 0.0 copy-done.13
  35.2 12.4 %finish.1 = bf16[1024,256]{1,0:T(8,128)(2,1)} custom-call(s32[1024]{0:T(1024)S(1)} %copy-done.1, f32[8192,128]{1,0:T(8,128)S(1)} %get-tuple-element.49.yad, f32[8192,128]{1,0:T(8,128)S(1)} %get-tuple-element.50.ybc, bf16[1024,256]{1,0:T(8,128)(2,1)S(1)} %get-tuple-element.51.feat, f32[128,128]{1,0:T(8,128)S(1)} %copy-done.9, f32[64,128]{1,0:T(8,128)S(1)} %copy-done.13, ...), custom_call_target="tpu_custom_call" | custom-call | flops 4000000000 | bytes 16000000 | tf_op jit(solution)/shard_map/finish/pallas_call | solution.py:575
  (2 shorter events, 0.0 us)
Async XLA Ops:
  0.0 8.8 %collective-permute-start = (s32[8,128]{1,0:T(8,128)}, s32[8,128]{1,0:T(8,128)S(1)}, u32[]{:S(2)}, u32[]{:S(2)}) collective-permute-start(s32[8,128]{1,0:T(8,128)} %bitcast.3), channel_id=1, source_target_pairs={{0,4},{4,0},{8,12},{12,8},{16,20},{20,16},{24,28},{28,24},{1,5},{5... | collective-permute-start | bytes 12296 | tf_op jit(solution)/shard_map/ppermute | solution.py:489
  8.8 9.6 %copy-start.1 = (s32[1024]{0:T(1024)S(1)}, s32[1024]{0:T(1024)}, u32[]{:S(2)}) copy-start(s32[1024]{0:T(1024)} %tok_s.5) | copy-start | bytes 12292
  8.8 9.6 %copy-start.11 = (f32[32,128]{1,0:T(8,128)S(1)}, f32[32,128]{1,0:T(8,128)}, u32[]{:S(2)}) copy-start(f32[32,128]{1,0:T(8,128)} %get-tuple-element.43.cst) | copy-start | bytes 49156
  9.5 6.1 %collective-permute-start.1 = (s32[16,128]{1,0:T(8,128)S(1)}, s32[16,128]{1,0:T(8,128)S(1)}, u32[]{:S(2)}, u32[]{:S(2)}) collective-permute-start(s32[16,128]{1,0:T(8,128)S(1)} %pad_add_fusion.2), channel_id=1, source_target_pairs={{0,8},{4,12},{8,0},{12,4},{16,24},{20,28},{24,16},{28,20},{1,9},{5... | collective-permute-start | bytes 24584 | tf_op jit(solution)/shard_map/ppermute | solution.py:489
  11.1 0.7 %copy-start = (s32[1024]{0:T(1024)S(1)}, s32[1024]{0:T(1024)}, u32[]{:S(2)}) copy-start(s32[1024]{0:T(1024)} %tok_s.5) | copy-start | bytes 12292
  11.8 1.0 %copy-start.5 = (bf16[4,128,512]{2,1,0:T(8,128)(2,1)S(1)}, bf16[4,128,512]{2,1,0:T(8,128)(2,1)}, u32[]{:S(2)}) copy-start(bf16[4,128,512]{2,1,0:T(8,128)(2,1)} %get-tuple-element.36.tw) | copy-start | bytes 1572868
  12.8 0.8 %copy-start.12 = (bf16[128,256]{1,0:T(8,128)(2,1)S(1)}, bf16[128,256]{1,0:T(8,128)(2,1)}, u32[]{:S(2)}) copy-start(bf16[128,256]{1,0:T(8,128)(2,1)} %get-tuple-element.37.embk) | copy-start | bytes 196612
  13.7 4.7 %copy-start.7 = (f32[640,128]{1,0:T(8,128)S(1)}, f32[640,128]{1,0:T(8,128)}, u32[]{:S(2)}) copy-start(f32[640,128]{1,0:T(8,128)} %get-tuple-element.42.gtab) | copy-start | bytes 983044
  13.7 4.7 %copy-start.9 = (f32[128,128]{1,0:T(8,128)S(1)}, f32[128,128]{1,0:T(8,128)}, u32[]{:S(2)}) copy-start(f32[128,128]{1,0:T(8,128)} %get-tuple-element.41.atab) | copy-start | bytes 196612
  15.7 14.6 %collective-permute-start.2 = (s32[32,128]{1,0:T(8,128)S(1)}, s32[32,128]{1,0:T(8,128)S(1)}, u32[]{:S(2)}, u32[]{:S(2)}) collective-permute-start(s32[32,128]{1,0:T(8,128)S(1)} %pad_add_fusion.1), channel_id=1, source_target_pairs={{0,16},{4,20},{8,24},{12,28},{16,0},{20,4},{24,8},{28,12},{1,17},{... | collective-permute-start | bytes 49160 | tf_op jit(solution)/shard_map/ppermute | solution.py:489
  18.3 12.0 %copy-start.3 = (bf16[2560,512]{1,0:T(8,128)(2,1)S(1)}, bf16[2560,512]{1,0:T(8,128)(2,1)}, u32[]{:S(2)}) copy-start(bf16[2560,512]{1,0:T(8,128)(2,1)} %get-tuple-element.56.xch) | copy-start | bytes 7864324
  18.3 12.0 %copy-start.4 = (bf16[2560,512]{1,0:T(8,128)(2,1)S(1)}, bf16[2560,512]{1,0:T(8,128)(2,1)}, u32[]{:S(2)}) copy-start(bf16[2560,512]{1,0:T(8,128)(2,1)} %get-tuple-element.57.xcl) | copy-start | bytes 7864324
  18.4 12.0 %copy-start.6 = (bf16[4,128,512]{2,1,0:T(8,128)(2,1)S(1)}, bf16[4,128,512]{2,1,0:T(8,128)(2,1)}, u32[]{:S(2)}) copy-start(bf16[4,128,512]{2,1,0:T(8,128)(2,1)} %get-tuple-element.36.tw) | copy-start | bytes 1572868
  18.4 12.0 %copy-start.8 = (f32[160,128]{1,0:T(8,128)S(1)}, f32[160,128]{1,0:T(8,128)}, u32[]{:S(2)}) copy-start(f32[160,128]{1,0:T(8,128)} %get-tuple-element.55.lac) | copy-start | bytes 245764
  30.2 4.9 %copy-start.2 = (bf16[512,256]{1,0:T(8,128)(2,1)S(1)}, bf16[512,256]{1,0:T(8,128)(2,1)}, u32[]{:S(2)}) copy-start(bf16[512,256]{1,0:T(8,128)(2,1)} %w_out.1) | copy-start | bytes 786436
  30.3 4.9 %copy-start.10 = (bf16[512,256]{1,0:T(8,128)(2,1)S(1)}, bf16[512,256]{1,0:T(8,128)(2,1)}, u32[]{:S(2)}) copy-start(bf16[512,256]{1,0:T(8,128)(2,1)} %get-tuple-element.60.wflip) | copy-start | bytes 786436
  30.3 4.9 %copy-start.13 = (f32[64,128]{1,0:T(8,128)S(1)}, f32[64,128]{1,0:T(8,128)}, u32[]{:S(2)}) copy-start(f32[64,128]{1,0:T(8,128)} %get-tuple-element.52.zg) | copy-start | bytes 98308

commit v3 on v2

--- a/solution.py
+++ b/solution.py
@@ -77,10 +77,10 @@
 
 
 def pick(values, u):
-    out = values[0]
-    for k in range(1, SYM):
-        out = jnp.where(u == k, values[k], out)
-    return out
+    low = (u & 1) == 1
+    first = jnp.where(low, values[1], values[0])
+    second = jnp.where(low, values[3], values[2])
+    return jnp.where(u > 3, values[4], jnp.where((u & 2) == 2, second, first))
 
 
 def tile_at(ref, row):
@@ -88,22 +88,17 @@
 
 
 def table_kernel(
-    emb_h, w_in_h, w_out_h, cw_h, bias_h, rate_h, skip_h, gain_h,
-    atab, gtab, zg, cst, lac, tw, xch, xcl, wflip, embk,
-    emb, w_in, w_out, cw, bias, rate, skip, gain, emb16, sems,
+    pack, w_in,
+    atab, gtab, zg, cst, lac, tw, xch, xcl, embk,
+    emb16,
 ):
-    sources = (emb_h, w_in_h, w_out_h, cw_h, bias_h, rate_h, skip_h, gain_h)
-    targets = (emb, w_in, w_out, cw, bias, rate, skip, gain)
-    copies = [
-        pltpu.make_async_copy(a, b, sems.at[i]) for i, (a, b) in enumerate(zip(sources, targets))
-    ]
-    for copy in copies:
-        copy.start()
-    for copy in copies:
-        copy.wait()
+    gain = pack[8:10, :]
+    bias = pack[10:12, 0:H]
+    rate = pack[12:14, 0:H]
+    skip = pack[14:16, 0:H]
+    e32 = pack[16:21, 0:D]
     highest = lax.Precision.HIGHEST
     emb16[...] = jnp.zeros_like(emb16)
-    e32 = emb[...].astype(F32)
     emb16[0:SYM, :] = e32
     for v in range(4):
         emb16[8 + v : 9 + v, :] = e32[3 - v : 4 - v, :]
@@ -118,9 +113,9 @@
     ).astype(BF16)
     heads = jnp.where(iota((H, E), 0) == (iota((H, E), 1) >> 6), 1.0, 0.0)
     r_exp = nn(rest, expand)
-    bias_e = nn(bias[...], heads, precision=highest)
-    rate_e = nn(rate[...], heads, precision=highest)
-    skip_e = nn(skip[...], heads, precision=highest)
+    bias_e = nn(bias, heads, precision=highest)
+    rate_e = nn(rate, heads, precision=highest)
+    skip_e = nn(skip, heads, precision=highest)
     shift = jnp.where(
         iota((nrest, nrest), 0) + NS == iota((nrest, nrest), 1),
         jnp.where(iota((nrest, nrest), 0) < NS, 1.0, 0.0),
@@ -137,8 +132,8 @@
     ).astype(BF16)
     r_t = nt(pick_r, rest)
     eye = jnp.where(iota((H, H), 0) == iota((H, H), 1), 1.0, 0.0)
-    bias_t = nt(eye, bias[...], precision=highest)
-    rate_t = nt(eye, rate[...], precision=highest)
+    bias_t = nt(eye, bias, precision=highest)
+    rate_t = nt(eye, rate, precision=highest)
     for q, (d, s, k) in enumerate(CHAINS):
         dt = softplus(r_exp[8 * s : 8 * s + 8, :] + bias_e[k : k + 1, :])
         a = jnp.exp(-rate_e[k : k + 1, :] * dt)
@@ -163,7 +158,7 @@
         xs = x16[8 * s : 8 * s + 8, :]
         blocks = [jnp.zeros((8, E), F32)] * 8
         for j in range(KW):
-            blocks[tap_row(d, j)] = (0.5 * cw[k, j : j + 1, :]) * xs
+            blocks[tap_row(d, j)] = (0.5 * pack[KW * k + j : KW * k + j + 1, :]) * xs
         high, low = split(jnp.concatenate(blocks, axis=0))
         tw[q, 0:64, :] = high
         tw[q, 64:128, :] = low
@@ -185,11 +180,9 @@
             high, low = split(silu_half(partial + last[v : v + 1, :]))
             xch[(q * SYM + v) * CH : (q * SYM + v + 1) * CH, :] = high
             xcl[(q * SYM + v) * CH : (q * SYM + v + 1) * CH, :] = low
-    flip = jnp.where(iota((D, D), 0) + iota((D, D), 1) == D - 1, 1.0, 0.0).astype(BF16)
     embk[...] = jnp.concatenate(
         [jnp.zeros((24, D), F32), emb16[0:8, :], jnp.zeros((96, D), F32)], axis=0
     ).astype(BF16)
-    wflip[...] = nn(w_out[...], flip).astype(BF16)
 
 
 def conv_kernel(tok_v, tw, embk, yad, ybc, feat):
@@ -215,7 +208,7 @@
     skip0 = cst[0:8, :]
     skip1 = cst[8:16, :]
 
-    def advance(direction, src, ref, skip_t, t, state):
+    def advance(direction, src, skip_t, t, state):
         u = tok_s[t]
         x = tile_at(src, t * 8)
         a = tile_at(atab, direction * 64 + u * 8)
@@ -223,23 +216,30 @@
             a * state[w] + tile_at(gtab, (direction * SYM + w) * 64 + u * 8) * x
             for w in range(SYM)
         ]
-        ref[pl.ds(pl.multiple_of(t * 8, 8), 8), :] = pick(new, u) + skip_t * x
-        return new, a
-
-    unroll = 8
+        return new, a, pick(new, u) + skip_t * x
+
+    unroll = 32
+    held = 8
 
     def group(g, carry):
         ya, yb, pa, pb = carry
         ya, yb = list(ya), list(yb)
-        for i in range(unroll):
-            n = g * unroll + i
-            ya, a0 = advance(0, xad, yad, skip0, n, ya)
-            yb, a1 = advance(1, xbc, ybc, skip1, total - 1 - n, yb)
-            if i < 3:
-                a0 = jnp.where(g == 0, 1.0, a0)
-                a1 = jnp.where(g == 0, 1.0, a1)
-            pa = pa * a0
-            pb = pb * a1
+        for begin in range(0, unroll, held):
+            done = []
+            for i in range(begin, begin + held):
+                n = g * unroll + i
+                m = total - 1 - n
+                ya, a0, out0 = advance(0, xad, skip0, n, ya)
+                yb, a1, out1 = advance(1, xbc, skip1, m, yb)
+                done.append((n, m, out0, out1))
+                if i < 3:
+                    a0 = jnp.where(g == 0, 1.0, a0)
+                    a1 = jnp.where(g == 0, 1.0, a1)
+                pa = pa * a0
+                pb = pb * a1
+            for n, m, out0, out1 in done:
+                yad[pl.ds(pl.multiple_of(n * 8, 8), 8), :] = out0
+                ybc[pl.ds(pl.multiple_of(m * 8, 8), 8), :] = out1
         return tuple(ya), tuple(yb), pa, pb
 
     def chunk(c, carry):
@@ -395,70 +395,87 @@
 
 
 def finish_kernel(
-    tok_s, yad, ybc, feat, atab, zg, cst, pst, ycar, yrim, w_out, wflip,
+    tok_s, yad, ybc, feat, atab, zg, cst, pst, ycar, yrim, w_out,
     out,
-    gad, gbc, mix,
+    gad, gbc, mix, carry_g, wflip,
 ):
-    step = pl.program_id(0)
-    nchunk = pl.num_programs(0)
-    first = step * CH
-    unroll = 8
-
-    def advance(d, ref, dest, n, decay, lead):
+    nchunk = tok_s.shape[0] // CH
+    for d in range(2):
+        for u in range(SYM):
+            at = slice((d * SYM + u) * 8, (d * SYM + u) * 8 + 8)
+            carry_g[at, :] = ycar[at, :] * zg[u * 8 : u * 8 + 8, :]
+    flip = jnp.where(iota((D, D), 0) + iota((D, D), 1) == D - 1, 1.0, 0.0).astype(BF16)
+    wflip[...] = nn(w_out[...], flip).astype(BF16)
+    unroll = 32
+    held = 8
+    mean = jnp.where(
+        ((iota((2 * CH, CH), 0) & 127) >> 6) == (iota((2 * CH, CH), 1) >> 6), 1.0 / 64.0, 0.0
+    ).astype(BF16)
+
+    def advance(d, ref, first, n, decay, lead):
         local = n if d == 0 else CH - 1 - n
         u = tok_s[first + local]
         a = tile_at(atab, d * 64 + u * 8)
         if lead is not None:
             a = jnp.where(lead, 1.0, a)
         decay = decay * a
-        y = tile_at(ref, local * 8) + decay * tile_at(ycar, d * SYM * 8 + u * 8)
-        dest[pl.ds(pl.multiple_of(local * 8, 8), 8), :] = y * tile_at(zg, u * 8)
-        return decay
-
-    def group(g, carry):
-        pa, pb = carry
-        for i in range(unroll):
-            n = g * unroll + i
-            lead0 = (g == 0) & (step == 0) if i < 3 else None
-            lead1 = (g == 0) & (step == nchunk - 1) if i < 3 else None
-            pa = advance(0, yad, gad, n, pa, lead0)
-            pb = advance(1, ybc, gbc, n, pb, lead1)
-        return pa, pb
-
-    lax.fori_loop(
-        0, CH // unroll, group, (tile_at(pst, step * 8), tile_at(pst, (nchunk + step) * 8))
-    )
-
-    @pl.when(step == 0)
-    def _():
-        for n in range(3):
-            gad[n * 8 : n * 8 + 8, :] = yrim[n * 8 : n * 8 + 8, :] * tile_at(zg, tok_s[n] * 8)
-
-    @pl.when(step == nchunk - 1)
-    def _():
-        for n in range(3):
-            at = (CH - 1 - n) * 8
-            gbc[at : at + 8, :] = yrim[24 + n * 8 : 32 + n * 8, :] * tile_at(
-                zg, tok_s[first + CH - 1 - n] * 8
-            )
-
-    mean = jnp.where(
-        ((iota((2 * CH, CH), 0) & 127) >> 6) == (iota((2 * CH, CH), 1) >> 6), 1.0 / 64.0, 0.0
-    ).astype(BF16)
-    normed = None
-    for d, ref in ((0, gad), (1, gbc)):
-        g = ref[...]
-        high, low = split(g * g)
-        meansq = nn(jnp.concatenate([high, low], axis=1), mean)
-        scaled = (g * lax.rsqrt(meansq + EPSILON)).reshape(CH, 8, CH) * cst[
-            16 + d * 8 : 24 + d * 8, :
-        ][None]
-        normed = scaled if normed is None else normed + scaled
-    mix[...] = normed.reshape(CH * 8, CH)
-    parts = [mix[pl.ds(i, CH, stride=8), :].astype(BF16) for i in range(8)]
-    mine_out = nn(jnp.concatenate(parts[0:4], axis=1), w_out[...]).astype(BF16).astype(F32)
-    other = nn(jnp.concatenate(parts[4:8], axis=1), wflip[...]).astype(BF16).astype(F32)
-    out[...] = (feat[...].astype(F32) + mine_out + other).astype(BF16)
+        part = tile_at(ref, (first + local) * 8) * tile_at(zg, u * 8)
+        return decay, local, part + decay * tile_at(carry_g, d * SYM * 8 + u * 8)
+
+    def chunk(step, _):
+        first = step * CH
+
+        def group(g, carry):
+            pa, pb = carry
+            for begin in range(0, unroll, held):
+                done = []
+                for i in range(begin, begin + held):
+                    n = g * unroll + i
+                    lead0 = (g == 0) & (step == 0) if i < 3 else None
+                    lead1 = (g == 0) & (step == nchunk - 1) if i < 3 else None
+                    pa, at0, out0 = advance(0, yad, first, n, pa, lead0)
+                    pb, at1, out1 = advance(1, ybc, first, n, pb, lead1)
+                    done.append((at0, at1, out0, out1))
+                for at0, at1, out0, out1 in done:
+                    gad[pl.ds(pl.multiple_of(at0 * 8, 8), 8), :] = out0
+                    gbc[pl.ds(pl.multiple_of(at1 * 8, 8), 8), :] = out1
+            return pa, pb
+
+        lax.fori_loop(
+            0, CH // unroll, group, (tile_at(pst, step * 8), tile_at(pst, (nchunk + step) * 8))
+        )
+
+        @pl.when(step == 0)
+        def _():
+            for n in range(3):
+                gad[n * 8 : n * 8 + 8, :] = yrim[n * 8 : n * 8 + 8, :] * tile_at(zg, tok_s[n] * 8)
+
+        @pl.when(step == nchunk - 1)
+        def _():
+            for n in range(3):
+                at = (CH - 1 - n) * 8
+                gbc[at : at + 8, :] = yrim[24 + n * 8 : 32 + n * 8, :] * tile_at(
+                    zg, tok_s[first + CH - 1 - n] * 8
+                )
+
+        normed = None
+        for d, ref in ((0, gad), (1, gbc)):
+            g = ref[...]
+            high, low = split(g * g)
+            meansq = nn(jnp.concatenate([high, low], axis=1), mean)
+            scaled = (g * lax.rsqrt(meansq + EPSILON)).reshape(CH, 8, CH) * cst[
+                16 + d * 8 : 24 + d * 8, :
+            ][None]
+            normed = scaled if normed is None else normed + scaled
+        mix[...] = normed.reshape(CH * 8, CH)
+        parts = [mix[pl.ds(i, CH, stride=8), :].astype(BF16) for i in range(8)]
+        mine_out = nn(jnp.concatenate(parts[0:4], axis=1), w_out[...]).astype(BF16).astype(F32)
+        other = nn(jnp.concatenate(parts[4:8], axis=1), wflip[...]).astype(BF16).astype(F32)
+        at = pl.ds(pl.multiple_of(step * CH, CH), CH)
+        out[at, :] = (feat[at, :].astype(F32) + mine_out + other).astype(BF16)
+        return 0
+
+    lax.fori_loop(0, nchunk, chunk, 0)
 
 
 def per_device(
@@ -480,7 +497,6 @@
     rows = own * nchunk
     vm = pl.BlockSpec(memory_space=pltpu.VMEM)
     sm = pl.BlockSpec(memory_space=pltpu.SMEM)
-    hbm = pl.BlockSpec(memory_space=pl.ANY)
     sds = jax.ShapeDtypeStruct
     mib = 1024 * 1024
 
@@ -504,24 +520,28 @@
         sds((4, CH, E), BF16),
         sds((4 * SYM * CH, E), BF16),
         sds((4 * SYM * CH, E), BF16),
-        sds((E, D), BF16),
         sds((CH, D), BF16),
     )
-    weights = (
-        embed_table, input_weight_matrix.T, output_weight_matrix, conv_weight, dt_bias, decay_rate,
-        skip_gain, norm_gain,
+    heads = jnp.concatenate([dt_bias, decay_rate, skip_gain], axis=0)
+    pack = jnp.concatenate(
+        [
+            conv_weight.reshape(2 * KW, E),
+            norm_gain,
+            jnp.pad(heads, ((0, 0), (0, E - H))),
+            jnp.pad(embed_table.astype(F32), ((0, 3), (0, E - D))),
+        ],
+        axis=0,
     )
-    atab, gtab, zg, cst, lac, tw, xch, xcl, wflip, embk = pl.pallas_call(
+    atab, gtab, zg, cst, lac, tw, xch, xcl, embk = pl.pallas_call(
         table_kernel,
         out_shape=table_shapes,
-        in_specs=[hbm] * 8,
+        in_specs=[vm] * 2,
         out_specs=[vm] * len(table_shapes),
-        scratch_shapes=[pltpu.VMEM(w.shape, w.dtype) for w in weights]
-        + [pltpu.VMEM((16, D), F32), pltpu.SemaphoreType.DMA((8,))],
-        compiler_params=params(56),
+        scratch_shapes=[pltpu.VMEM((16, D), F32)],
+        compiler_params=params(20),
         cost_estimate=cost(1_000_000_000, 8_000_000),
         name="symbol_tables",
-    )(*weights)
+    )(pack, input_weight_matrix.T)
     blocks, tw, embk = lax.optimization_barrier((blocks, tw, embk))
     if rounds > 1:
         blocks = exchanged(blocks, 1)
@@ -570,20 +590,17 @@
         cost_estimate=cost(2_000_000_000, 6_000_000),
         name="history",
     )(mine, token_ids, blocks, atab, gtab, cst, lac, tw, xch, xcl)
-    chunk_spec = pl.BlockSpec((CH * 8, CH), lambda i: (i, 0))
-    out_spec = pl.BlockSpec((CH, D), lambda i: (i, 0))
     return pl.pallas_call(
         finish_kernel,
-        grid=(nchunk,),
         out_shape=sds((length, D), BF16),
-        in_specs=[sm, chunk_spec, chunk_spec, out_spec] + [vm] * 8,
-        out_specs=out_spec,
-        scratch_shapes=[pltpu.VMEM((CH * 8, CH), F32)] * 3,
+        in_specs=[sm] + [vm] * 10,
+        out_specs=vm,
+        scratch_shapes=[pltpu.VMEM((CH * 8, CH), F32)] * 3 + [pltpu.VMEM((2 * SYM * 8, CH), F32), pltpu.VMEM((E, D), BF16)],
         compiler_params=params(20),
         cost_estimate=cost(4_000_000_000, 16_000_000),
         name="finish",
     )(
-        token_ids, yad, ybc, feat, atab, zg, cst, pst, ycar, yrim, output_weight_matrix, wflip
+        token_ids, yad, ybc, feat, atab, zg, cst, pst, ycar, yrim, output_weight_matrix
     )
 
 

time: 48 us -> 49.2 us (1.025)
  Pallas kernels: 36.9 us -> 31.3 us
  local copies, waits for them, and re-layouts: 2.62 us -> 7.27 us
  other arithmetic: 0.74 us -> 2.87 us
    unnamed x28, local copies, waits for them, and re-layouts: 2.62 us -> 6.55 us
    pallas_call x2, Pallas kernels: 18.2 us -> 15.3 us  [the longest x1 13.4 us: per_device(): pl.pallas_call(finish_kernel, out_shape=sds((length, D), BF16), in_specs=...]
    pallas_call x1, Pallas kernels: 11.9 us -> 9.17 us  [per_device(): pl.pallas_call(scan_kernel, out_shape=(sds((length * 8, CH), F32), sds((l...]
    concatenate x0 -> x2, other arithmetic: none -> 1.42 us  [the longest x1 0.72 us: per_device(): heads = jnp.concatenate([dt_bias, decay_rate, skip_gain], axis=0)]
    reshape x0 -> x1, local copies, waits for them, and re-layouts: none -> 0.73 us  [per_device(): conv_weight.reshape(2 * KW, E)]
    pad x0 -> x1, other arithmetic: none -> 0.69 us  [per_device(): jnp.pad(embed_table.astype(F32), ((0, 3), (0, E - D)))]
  transfers between devices with their start and end apart: 3 -> 3, of which waited for: 0 -> 0; matrix products, arithmetic and copies ran while one was open for 0% -> 6% of each run, Pallas kernels for 41% -> 27%
where the time goes in v3:
time: 49.2 us; the launch traced here: 48.8 us
  Pallas kernels  31.3 us (64%)
  local copies, waits for them, and re-layouts  7.27 us (15%)
  starting transfers between devices  7.18 us (15%)
  other arithmetic  2.87 us (6%)
    pallas_call x1, Pallas kernels, per_device(): pl.pallas_call(finish_kernel, out_shape=sds((length, D), BF16), in_specs=...  13.4 us
    pallas_call x1, Pallas kernels, per_device(): pl.pallas_call(scan_kernel, out_shape=(sds((length * 8, CH), F32), sds((l...  9.17 us
    ppermute x3, starting transfers between devices, exchanged(): return jnp.concatenate([blocks, lax.ppermute(blocks, 'seq', route)], axis=0)  7.18 us
    unnamed x28, local copies, waits for them, and re-layouts  6.55 us
    pallas_call x1, Pallas kernels, per_device(): pl.pallas_call(history_kernel, out_shape=(sds((2 * SYM * 8, CH), F32), sd...  4.84 us
    pallas_call x1, Pallas kernels, per_device(): pl.pallas_call(conv_kernel, out_shape=(sds((length * 8, CH), F32), sds((l...  1.97 us
    pallas_call x1, Pallas kernels, per_device(): pl.pallas_call(table_kernel, out_shape=table_shapes, in_specs=[vm] * 2, o...  1.88 us
  transfers between devices with their start and end apart: 3, of which 0 were waited for; matrix products, arithmetic and copies ran while one was open for 6% of the time, Pallas kernels for 27%

profile of v3, /device:TPU:0, one launch (start us, length us, event | category | flops | bytes accessed | tf_op | source)
XLA Modules:
  0.0 48.8 jit_solution(328359324723108556)
XLA Ops:
  0.0 3.0 %collective-permute-start = (s32[8,128]{1,0:T(8,128)}, s32[8,128]{1,0:T(8,128)S(1)}, u32[]{:S(2)}, u32[]{:S(2)}) collective-permute-start(s32[8,128]{1,0:T(8,128)} %bitcast.3), channel_id=1, source_target_pairs={{0,4},{4,0},{8,12},{12,8},{16,20},{20,16},{24,28},{28,24},{1,5},{5... | collective-permute-start | bytes 12296 | tf_op jit(solution)/shard_map/ppermute | solution.py:505
  3.0 0.7 %pad_convert_fusion = f32[8,512]{1,0:T(8,128)S(1)} fusion(bf16[5,256]{1,0:T(8,128)(2,1)} %param.10), kind=kLoop, calls=%fused_computation.7 | loop fusion | flops 4096 | bytes 18944 | tf_op jit(solution)/shard_map/jit(_pad)/pad | solution.py:531
  3.7 0.7 %reshape.10 = f32[8,512]{1,0:T(8,128)S(1)} reshape(f32[2,4,512]{2,1,0:T(4,128)} %param.13) | data formatting | bytes 32768 | tf_op jit(solution)/shard_map/reshape | solution.py:528
  4.4 0.7 %select_maximum_fusion = f32[6,512]{1,0:T(8,128)S(1)} fusion(f32[2,8]{1,0:T(2,128)} %param.16, f32[2,8]{1,0:T(2,128)} %param.15, f32[2,8]{1,0:T(2,128)} %param.14), kind=kLoop, calls=%fused_computation.2 | loop fusion | flops 18432 | bytes 12480 | tf_op jit(solution)/shard_map/concatenate | solution.py:525
  5.1 0.7 %pad_maximum_fusion.pack = f32[24,512]{1,0:T(8,128)S(1)} fusion(f32[8,512]{1,0:T(8,128)S(1)} %pad_convert_fusion, f32[6,512]{1,0:T(8,128)S(1)} %select_maximum_fusion, f32[2,512]{1,0:T(2,128)} %param.17, f32[8,512]{1,0:T(8,128)S(1)} %reshape.10), kind=kLoop, calls=%fused_computation | loop fusion | flops 36864 | bytes 98304 | tf_op jit(solution)/shard_map/concatenate | solution.py:526
  5.8 0.0 copy-start.2
  5.8 1.0 %copy-done.2 = bf16[256,1064]{0,1:T(8,128)(2,1)S(1)} copy-done((bf16[256,1064]{0,1:T(8,128)(2,1)S(1)}, bf16[256,1064]{0,1:T(8,128)(2,1)}, u32[]{:S(2)}) %copy-start.2) | copy-done | bytes 544792
  6.9 1.9 %symbol_tables.1 = (f32[128,128]{1,0:T(8,128)S(1)}, f32[640,128]{1,0:T(8,128)S(1)}, f32[64,128]{1,0:T(8,128)S(1)}, f32[32,128]{1,0:T(8,128)S(1)}, f32[160,128]{1...) custom-call(f32[24,512]{1,0:T(8,128)S(1)} %pad_maximum_fusion.pack, ...), custom_call_target="tpu_custom_call" | custom-call | flops 1000000000 | bytes 8000000 | tf_op jit(solution)/shard_map/symbol_tables/pallas_call | solution.py:535
  8.7 0.0 copy-start.4
  8.8 1.5 %copy-done.4 = bf16[2560,512]{1,0:T(8,128)(2,1)} copy-done((bf16[2560,512]{1,0:T(8,128)(2,1)}, bf16[2560,512]{1,0:T(8,128)(2,1)S(1)}, u32[]{:S(2)}) %copy-start.4) | copy-done | bytes 2621464
  10.2 0.0 copy-start.6
  10.2 0.6 %copy-done.6 = f32[160,128]{1,0:T(8,128)} copy-done((f32[160,128]{1,0:T(8,128)}, f32[160,128]{1,0:T(8,128)S(1)}, u32[]{:S(2)}) %copy-start.6) | copy-done | bytes 81944
  10.9 0.0 copy-start.8
  10.9 0.6 %copy-done.8 = f32[32,128]{1,0:T(8,128)} copy-done((f32[32,128]{1,0:T(8,128)}, f32[32,128]{1,0:T(8,128)S(1)}, u32[]{:S(2)}) %copy-start.8) | copy-done | bytes 16408
  11.5 0.0 copy-start.10
  11.5 0.6 %copy-done.10 = bf16[128,256]{1,0:T(8,128)(2,1)} copy-done((bf16[128,256]{1,0:T(8,128)(2,1)}, bf16[128,256]{1,0:T(8,128)(2,1)S(1)}, u32[]{:S(2)}) %copy-start.10) | copy-done | bytes 65560
  12.1 0.0 copy-start.12
  12.1 0.6 %copy-done.12 = f32[64,128]{1,0:T(8,128)} copy-done((f32[64,128]{1,0:T(8,128)}, f32[64,128]{1,0:T(8,128)S(1)}, u32[]{:S(2)}) %copy-start.12) | copy-done | bytes 32792
  12.7 0.0 copy-start.1
  12.7 0.0 copy-start.9
  12.7 0.0 collective-permute-done
  12.7 0.8 %pad_add_fusion.2 = s32[16,128]{1,0:T(8,128)S(1)} fusion(s32[8,128]{1,0:T(8,128)S(1)} %collective-permute-done, s32[8,128]{1,0:T(8,128)} %bitcast.4), kind=kLoop, calls=%fused_computation.6 | loop fusion | flops 2048 | bytes 16384 | tf_op jit(solution)/shard_map/concatenate | solution.py:505
  13.5 1.6 %collective-permute-start.1 = (s32[16,128]{1,0:T(8,128)S(1)}, s32[16,128]{1,0:T(8,128)S(1)}, u32[]{:S(2)}, u32[]{:S(2)}) collective-permute-start(s32[16,128]{1,0:T(8,128)S(1)} %pad_add_fusion.2), channel_id=1, source_target_pairs={{0,8},{4,12},{8,0},{12,4},{16,24},{20,28},{24,16},{28,20},{1,9},{5... | collective-permute-start | bytes 24584 | tf_op jit(solution)/shard_map/ppermute | solution.py:505
  15.1 0.0 copy-start
  15.1 0.7 %copy-done = s32[1024]{0:T(1024)S(1)} copy-done((s32[1024]{0:T(1024)S(1)}, s32[1024]{0:T(1024)}, u32[]{:S(2)}) %copy-start) | copy-done | bytes 4120
  15.7 0.0 copy-start.11
  15.7 0.8 %copy-done.11 = bf16[128,256]{1,0:T(8,128)(2,1)S(1)} copy-done((bf16[128,256]{1,0:T(8,128)(2,1)S(1)}, bf16[128,256]{1,0:T(8,128)(2,1)}, u32[]{:S(2)}) %copy-start.11) | copy-done | bytes 65560
  16.6 2.0 %convolve.1 = (f32[8192,128]{1,0:T(8,128)S(1)}, f32[8192,128]{1,0:T(8,128)S(1)}, bf16[1024,256]{1,0:T(8,128)(2,1)S(1)}) custom-call(s32[8,128]{1,0:T(8,128)S(1)} %bitcast.5, bf16[4,128,512]{2,1,0:T(8,128)(2,1)S(1)} %get-tuple-element.35.tw, bf16[128,256]{1,0:T(8,128)(2,1)S(1)} %copy-done.11), custom_call_target="tpu_custom_call" | custom-call | flops 2000000000 | bytes 9000000 | tf_op jit(solution)/shard_map/convolve/pallas_call | solution.py:548
  18.6 0.0 collective-permute-done.1
  18.6 2.6 %collective-permute-start.2 = (s32[32,128]{1,0:T(8,128)S(1)}, s32[32,128]{1,0:T(8,128)S(1)}, u32[]{:S(2)}, u32[]{:S(2)}) collective-permute-start(s32[32,128]{1,0:T(8,128)S(1)} %pad_add_fusion.1), channel_id=1, source_target_pairs={{0,16},{4,20},{8,24},{12,28},{16,0},{20,4},{24,8},{28,12},{1,17},{... | collective-permute-start | bytes 49160 | tf_op jit(solution)/shard_map/ppermute | solution.py:505
  21.2 0.0 copy-done.1
  21.2 0.0 copy-done.9
  21.2 0.0 copy-start.5
  21.2 0.0 copy-start.7
  21.2 9.2 %scan_block.1 = (f32[8192,128]{1,0:T(8,128)S(1)}, f32[8192,128]{1,0:T(8,128)S(1)}, f32[128,128]{1,0:T(8,128)S(1)}) custom-call(s32[1024]{0:T(1024)S(1)} %copy-done.1, f32[128,128]{1,0:T(8,128)S(1)} %get-tuple-element.40.atab, f32[640,128]{1,0:T(8,128)S(1)} %get-tuple-element.41.gtab, ...), custom_call_target="tpu_custom_call", output_to_operand_aliasing={{0}: (4, {}), {1}: (5, {})} | custom-call | flops 4000000000 | bytes 16000000 | tf_op jit(solution)/shard_map/scan_block/pallas_call | solution.py:560
  30.4 0.0 copy-start.3
  30.4 0.0 copy-start.13
  30.4 0.0 collective-permute-done.2
  30.5 0.0 copy-done.5
  30.5 0.0 copy-done.7
  30.5 4.8 %history.1 = (f32[80,128]{1,0:T(8,128)S(1)}, f32[48,128]{1,0:T(8,128)S(1)}) custom-call(s32[1]{0:T(128)} %bitcast.2.mine, s32[1024]{0:T(1024)S(1)} %copy-done.1, s32[64,128]{1,0:T(8,128)S(1)} %pad_add_fusion.tok_all, f32[128,128]{1,0:T(8,128)S(1)} %get-tuple-element.40.atab, f32[640,128]{1,0:T(8,128)S(1)} %get-tuple-element.41.gtab, ...), custom_call_target="tpu_custom_call" | custom-call | flops 2000000000 | bytes 6000000 | tf_op jit(solution)/shard_map/history/pallas_call | solution.py:576
  35.3 0.0 copy-done.3
  35.3 0.0 copy-done.13
  35.3 13.4 %finish.1 = bf16[1024,256]{1,0:T(8,128)(2,1)} custom-call(s32[1024]{0:T(1024)S(1)} %copy-done.1, f32[8192,128]{1,0:T(8,128)S(1)} %get-tuple-element.48.yad, f32[8192,128]{1,0:T(8,128)S(1)} %get-tuple-element.49.ybc, bf16[1024,256]{1,0:T(8,128)(2,1)S(1)} %get-tuple-element.50.feat, f32[128,128]{1,0:T(8,128)S(1)} %get-tuple-element.40.atab, ...), custom_call_target="tpu_custom_call" | custom-call | flops 4000000000 | bytes 16000000 | tf_op jit(solution)/shard_map/finish/pallas_call | solution.py:593
  (2 shorter events, 0.0 us)
Async XLA Ops:
  0.0 12.7 %collective-permute-start = (s32[8,128]{1,0:T(8,128)}, s32[8,128]{1,0:T(8,128)S(1)}, u32[]{:S(2)}, u32[]{:S(2)}) collective-permute-start(s32[8,128]{1,0:T(8,128)} %bitcast.3), channel_id=1, source_target_pairs={{0,4},{4,0},{8,12},{12,8},{16,20},{20,16},{24,28},{28,24},{1,5},{5... | collective-permute-start | bytes 12296 | tf_op jit(solution)/shard_map/ppermute | solution.py:505
  5.8 1.1 %copy-start.2 = (bf16[256,1064]{0,1:T(8,128)(2,1)S(1)}, bf16[256,1064]{0,1:T(8,128)(2,1)}, u32[]{:S(2)}) copy-start(bf16[256,1064]{0,1:T(8,128)(2,1)} %param.11) | copy-start | bytes 1634308
  8.7 1.5 %copy-start.4 = (bf16[2560,512]{1,0:T(8,128)(2,1)}, bf16[2560,512]{1,0:T(8,128)(2,1)S(1)}, u32[]{:S(2)}) copy-start(bf16[2560,512]{1,0:T(8,128)(2,1)S(1)} %get-tuple-element.56.xcl) | copy-start | bytes 7864324
  10.2 0.6 %copy-start.6 = (f32[160,128]{1,0:T(8,128)}, f32[160,128]{1,0:T(8,128)S(1)}, u32[]{:S(2)}) copy-start(f32[160,128]{1,0:T(8,128)S(1)} %get-tuple-element.54.lac) | copy-start | bytes 245764
  10.9 0.6 %copy-start.8 = (f32[32,128]{1,0:T(8,128)}, f32[32,128]{1,0:T(8,128)S(1)}, u32[]{:S(2)}) copy-start(f32[32,128]{1,0:T(8,128)S(1)} %get-tuple-element.42.cst) | copy-start | bytes 49156
  11.5 0.6 %copy-start.10 = (bf16[128,256]{1,0:T(8,128)(2,1)}, bf16[128,256]{1,0:T(8,128)(2,1)S(1)}, u32[]{:S(2)}) copy-start(bf16[128,256]{1,0:T(8,128)(2,1)S(1)} %get-tuple-element.36.embk) | copy-start | bytes 196612
  12.1 0.6 %copy-start.12 = (f32[64,128]{1,0:T(8,128)}, f32[64,128]{1,0:T(8,128)S(1)}, u32[]{:S(2)}) copy-start(f32[64,128]{1,0:T(8,128)S(1)} %get-tuple-element.51.zg) | copy-start | bytes 98308
  12.7 8.5 %copy-start.1 = (s32[1024]{0:T(1024)S(1)}, s32[1024]{0:T(1024)}, u32[]{:S(2)}) copy-start(s32[1024]{0:T(1024)} %tok_s.5) | copy-start | bytes 12292
  12.7 8.5 %copy-start.9 = (f32[32,128]{1,0:T(8,128)S(1)}, f32[32,128]{1,0:T(8,128)}, u32[]{:S(2)}) copy-start(f32[32,128]{1,0:T(8,128)} %copy-done.8) | copy-start | bytes 49156
  13.5 5.1 %collective-permute-start.1 = (s32[16,128]{1,0:T(8,128)S(1)}, s32[16,128]{1,0:T(8,128)S(1)}, u32[]{:S(2)}, u32[]{:S(2)}) collective-permute-start(s32[16,128]{1,0:T(8,128)S(1)} %pad_add_fusion.2), channel_id=1, source_target_pairs={{0,8},{4,12},{8,0},{12,4},{16,24},{20,28},{24,16},{28,20},{1,9},{5... | collective-permute-start | bytes 24584 | tf_op jit(solution)/shard_map/ppermute | solution.py:505
  15.1 0.7 %copy-start = (s32[1024]{0:T(1024)S(1)}, s32[1024]{0:T(1024)}, u32[]{:S(2)}) copy-start(s32[1024]{0:T(1024)} %tok_s.5) | copy-start | bytes 12292
  15.7 0.8 %copy-start.11 = (bf16[128,256]{1,0:T(8,128)(2,1)S(1)}, bf16[128,256]{1,0:T(8,128)(2,1)}, u32[]{:S(2)}) copy-start(bf16[128,256]{1,0:T(8,128)(2,1)} %copy-done.10) | copy-start | bytes 196612
  18.6 11.9 %collective-permute-start.2 = (s32[32,128]{1,0:T(8,128)S(1)}, s32[32,128]{1,0:T(8,128)S(1)}, u32[]{:S(2)}, u32[]{:S(2)}) collective-permute-start(s32[32,128]{1,0:T(8,128)S(1)} %pad_add_fusion.1), channel_id=1, source_target_pairs={{0,16},{4,20},{8,24},{12,28},{16,0},{20,4},{24,8},{28,12},{1,17},{... | collective-permute-start | bytes 49160 | tf_op jit(solution)/shard_map/ppermute | solution.py:505
  21.2 9.2 %copy-start.5 = (bf16[2560,512]{1,0:T(8,128)(2,1)S(1)}, bf16[2560,512]{1,0:T(8,128)(2,1)}, u32[]{:S(2)}) copy-start(bf16[2560,512]{1,0:T(8,128)(2,1)} %copy-done.4) | copy-start | bytes 7864324
  21.2 9.2 %copy-start.7 = (f32[160,128]{1,0:T(8,128)S(1)}, f32[160,128]{1,0:T(8,128)}, u32[]{:S(2)}) copy-start(f32[160,128]{1,0:T(8,128)} %copy-done.6) | copy-start | bytes 245764
  30.4 4.9 %copy-start.3 = (bf16[512,256]{1,0:T(8,128)(2,1)S(1)}, bf16[512,256]{1,0:T(8,128)(2,1)}, u32[]{:S(2)}) copy-start(bf16[512,256]{1,0:T(8,128)(2,1)} %w_out.1) | copy-start | bytes 786436
  30.4 4.9 %copy-start.13 = (f32[64,128]{1,0:T(8,128)S(1)}, f32[64,128]{1,0:T(8,128)}, u32[]{:S(2)}) copy-start(f32[64,128]{1,0:T(8,128)} %copy-done.12) | copy-start | bytes 98308

commit v4 on v3

v4 whole, which is shorter than its diff:
```python
import functools

import jax
import jax.numpy as jnp
from jax import lax
from jax.experimental import pallas as pl
from jax.experimental.pallas import tpu as pltpu
from jax.sharding import PartitionSpec as P

D = 256
E = 512
NS = 16
H = 8
KW = 4
SYM = 5
LOG2E = 1.4426950408889634
EPSILON = 1e-05
CH = 128
SUB = 16

F32 = jnp.float32
BF16 = jnp.bfloat16

CHAINS = ((0, 0, 0), (0, 1, 1), (1, 0, 1), (1, 1, 0))


def iota(shape, dim):
    return lax.broadcasted_iota(jnp.int32, shape, dim)


def nn(a, b, **kw):
    return lax.dot_general(a, b, (((1,), (0,)), ((), ())), preferred_element_type=F32, **kw)


def nt(a, b, **kw):
    return lax.dot_general(a, b, (((1,), (1,)), ((), ())), preferred_element_type=F32, **kw)


def split(value):
    high = value.astype(BF16)
    low = (value - high.astype(F32)).astype(BF16)
    return high, low


def softplus(x):
    return jnp.maximum(x, 0.0) + jnp.log1p(jnp.exp(-jnp.abs(x)))


def silu_half(half):
    return half + half * jnp.tanh(half)


def tap_row(direction, j):
    return j if direction == 0 else 2 * (KW - 1) - j


def window_onehot(rows):
    sub = iota((8, CH), 0).astype(F32)
    blocks = [jnp.where(row == sub, 1.0, 0.0) for row in rows]
    blocks.append(jnp.zeros((8, CH), F32))
    stacked = jnp.concatenate(blocks + blocks, axis=0)
    return stacked.T.astype(BF16)


def shifted(tok, offset, rows):
    if offset == 0:
        return tok
    lane = iota((rows, CH), 1)
    row = iota((rows, CH), 0)
    moved = pltpu.roll(tok, (-offset) % CH, 1)
    if offset < 0:
        other = pltpu.roll(moved, 1, 0)
        crossing = lane < -offset
        outside = crossing & (row == 0)
    else:
        other = pltpu.roll(moved, rows - 1, 0)
        crossing = lane >= CH - offset
        outside = crossing & (row == rows - 1)
    return jnp.where(outside, 5.0, jnp.where(crossing, other, moved))


def pick(values, u):
    low = (u & 1) == 1
    first = jnp.where(low, values[1], values[0])
    second = jnp.where(low, values[3], values[2])
    return jnp.where(u > 3, values[4], jnp.where((u & 2) == 2, second, first))


def tile_at(ref, row):
    return ref[pl.ds(pl.multiple_of(row, 8), 8), :]


def fetch(sources, targets, sems):
    copies = [
        pltpu.make_async_copy(a, b, sems.at[i]) for i, (a, b) in enumerate(zip(sources, targets))
    ]
    for copy in copies:
        copy.start()
    for copy in copies:
        copy.wait()


def symbol_tables(
    directions, full, emb, w_in, cw, bias, rate, skip, gain, emb16, atab, gtab, cst, tw
):
    highest = lax.Precision.HIGHEST
    emb16[...] = jnp.zeros_like(emb16)
    e32 = emb[...].astype(F32)
    emb16[0:SYM, :] = e32
    for v in range(4):
        emb16[8 + v : 9 + v, :] = e32[3 - v : 4 - v, :]
    emb16[12:13, :] = e32[4:5, :]
    embs = emb16[...].astype(BF16)
    x16 = nt(embs, w_in[E : 2 * E, :]).astype(BF16).astype(F32)
    rest = nt(embs, w_in[2 * E :, :]).astype(BF16)
    nrest = 2 * NS + H
    expand = jnp.where(
        iota((nrest, E), 0) == (iota((nrest, E), 1) >> 6) + 2 * NS, 1.0, 0.0
    ).astype(BF16)
    heads = jnp.where(iota((H, E), 0) == (iota((H, E), 1) >> 6), 1.0, 0.0)
    r_exp = nn(rest, expand)
    bias_e = nn(bias[...], heads, precision=highest)
    rate_e = nn(rate[...], heads, precision=highest)
    skip_e = nn(skip[...], heads, precision=highest)
    shift = jnp.where(
        iota((nrest, nrest), 0) + NS == iota((nrest, nrest), 1),
        jnp.where(iota((nrest, nrest), 0) < NS, 1.0, 0.0),
        0.0,
    ).astype(BF16)
    rest_b = nn(rest, shift).astype(BF16)
    cb = nt(rest_b, rest)
    if full is not None:
        zg, lac, xch, xcl = full
        z16 = nt(embs, w_in[0:E, :]).astype(BF16).astype(F32)
        sz = z16 * (0.5 + 0.5 * jnp.tanh(0.5 * z16))
        for s in range(2):
            for i in range(4):
                zg[pl.ds(s * 4 + i, 8, stride=8), :] = sz[8 * s : 8 * s + 8, 128 * i : 128 * i + 128]
        pick_r = jnp.where(
            iota((H, nrest), 0) + 2 * NS == iota((H, nrest), 1), 1.0, 0.0
        ).astype(BF16)
        r_t = nt(pick_r, rest)
        eye = jnp.where(iota((H, H), 0) == iota((H, H), 1), 1.0, 0.0)
        bias_t = nt(eye, bias[...], precision=highest)
        rate_t = nt(eye, rate[...], precision=highest)
    for q, (d, s, k) in enumerate(CHAINS):
        if d not in directions:
            continue
        dt = softplus(r_exp[8 * s : 8 * s + 8, :] + bias_e[k : k + 1, :])
        a = jnp.exp(-rate_e[k : k + 1, :] * dt)
        for i in range(4):
            lanes = slice(128 * i, 128 * i + 128)
            atab[pl.ds(d * 64 + s * 4 + i, 8, stride=8), :] = a[:, lanes]
            cst[d * 8 + s * 4 + i : d * 8 + s * 4 + i + 1, :] = skip_e[k : k + 1, lanes]
            cst[16 + d * 8 + s * 4 + i : 17 + d * 8 + s * 4 + i, :] = gain[k : k + 1, lanes]
        for u in range(SYM):
            g = cb[8 * s : 8 * s + 8, 8 * s + u : 8 * s + u + 1] * dt
            for i in range(4):
                gtab[pl.ds((d * SYM + u) * 64 + s * 4 + i, 8, stride=8), :] = g[
                    :, 128 * i : 128 * i + 128
                ]
        xs = x16[8 * s : 8 * s + 8, :]
        blocks = [jnp.zeros((8, E), F32)] * 8
        for j in range(KW):
            blocks[tap_row(d, j)] = (0.5 * cw[k, j : j + 1, :]) * xs
        high, low = split(jnp.concatenate(blocks, axis=0))
        tw[q, 0:64, :] = high
        tw[q, 64:128, :] = low
        if full is None:
            continue
        la = (
            -rate_t[:, k : k + 1] * softplus(r_t[:, 8 * s : 8 * s + 8] + bias_t[:, k : k + 1])
        ) * LOG2E
        for v in range(SYM):
            lac[(d * SYM + v) * 16 + s * 8 : (d * SYM + v) * 16 + s * 8 + 8, :] = jnp.broadcast_to(
                la[:, v : v + 1], (8, CH)
            )
        code = iota((CH, CH), 0).astype(F32)
        lane = iota((CH, CH), 1) & 63
        slot = lane >> 3
        sym = (lane & 7).astype(F32)
        d0 = jnp.floor((code + 0.5) * (1.0 / 25.0))
        d01 = jnp.floor((code + 0.5) * (1.0 / 5.0))
        digits = (d0, d01 - 5.0 * d0, code - 5.0 * d01)
        hot = jnp.zeros((CH, CH), F32)
        for j in range(KW - 1):
            hot = jnp.where(
                slot == tap_row(d, j), jnp.where(sym == digits[j], 1.0, 0.0), hot
            )
        partial = nn(hot.astype(BF16), tw[q])
        last = blocks[tap_row(d, KW - 1)]
        for v in range(SYM):
            high, low = split(silu_half(partial + last[v : v + 1, :]))
            xch[(q * SYM + v) * CH : (q * SYM + v + 1) * CH, :] = high
            xcl[(q * SYM + v) * CH : (q * SYM + v + 1) * CH, :] = low


def direction_kernel(
    direction, tok_s, tok_v, emb_h, w_in_h, cw_h, bias_h, rate_h, skip_h, gain_h,
    y_h, pst,
    emb, w_in, cw, bias, rate, skip, gain, emb16, atab, gtab, cst, tw, x_v, y_v, sems, y_sems,
):
    total = tok_s.shape[0]
    nchunk = total // CH
    fetch((emb_h, w_in_h, cw_h, bias_h, rate_h, skip_h, gain_h),
          (emb, w_in, cw, bias, rate, skip, gain), sems)
    symbol_tables(
        (direction,), None, emb, w_in, cw, bias, rate, skip, gain, emb16, atab, gtab, cst, tw
    )
    tok = tok_v[...].astype(F32)
    shifts = [shifted(tok, o, nchunk) for o in range(1 - KW, KW)]
    for c in range(nchunk):
        hot = window_onehot([sh[c : c + 1, :] for sh in shifts])
        for s in range(2):
            x = silu_half(nn(hot, tw[2 * direction + s]))
            for i in range(4):
                x_v[pl.ds(c * 8 * CH + s * 4 + i, CH, stride=8), :] = x[:, 128 * i : 128 * i + 128]
    rim = (KW - 1) * 8
    if direction == 0:
        x_v[0:rim, :] = jnp.zeros((rim, CH), F32)
    else:
        x_v[total * 8 - rim : total * 8, :] = jnp.zeros((rim, CH), F32)

    skip_t = cst[8 * direction : 8 * direction + 8, :]
    unroll = 32
    held = 8

    def group(g, carry):
        state, decay = list(carry[0]), carry[1]
        for begin in range(0, unroll, held):
            done = []
            for i in range(begin, begin + held):
                n = g * unroll + i
                t = n if direction == 0 else total - 1 - n
                if i % SUB == 0:
                    first = n if direction == 0 else t - SUB + 1
                    pst[pl.ds(pl.multiple_of((first // SUB) * 8, 8), 8), :] = decay
                u = tok_s[t]
                x = tile_at(x_v, t * 8)
                a = tile_at(atab, direction * 64 + u * 8)
                state = [
                    a * state[w] + tile_at(gtab, (direction * SYM + w) * 64 + u * 8) * x
                    for w in range(SYM)
                ]
                done.append((t, pick(state, u) + skip_t * x))
                if i < KW - 1:
                    a = jnp.where(g == 0, 1.0, a)
                decay = decay * a
            for t, y in done:
                y_v[pl.ds(pl.multiple_of(t * 8, 8), 8), :] = y
        return tuple(state), decay

    def stream(c):
        at = c if direction == 0 else nchunk - 1 - c
        rows = pl.ds(pl.multiple_of(at * (CH * 8), CH * 8), CH * 8)
        return pltpu.make_async_copy(y_v.at[rows, :], y_h.at[rows, :], y_sems.at[c])

    def chunk(c, carry):
        per = CH // unroll
        carry = lax.fori_loop(c * per, (c + 1) * per, group, carry)
        stream(c).start()
        return carry

    zero = jnp.zeros((8, CH), F32)
    lax.fori_loop(0, nchunk, chunk, ((zero,) * SYM, jnp.ones((8, CH), F32)))
    for c in range(nchunk):
        stream(c).wait()


def last_kernel(
    mine, tok_s, near, far, yad_h, ybc_h, psta, pstb,
    emb_h, w_in_h, cw_h, bias_h, rate_h, skip_h, gain_h, w_out_h,
    out,
    emb, w_in, cw, bias, rate, skip, gain, w_out, emb16, atab, gtab, cst, tw, zg, lac, xch, xcl,
    tok_x, tok_f, code, tri, hist, svec, xrim, ycar, yrim, carry_g, yad, ybc, mix, sems, y_sems,
):
    half = near.shape[0]
    rows = 2 * half
    own = rows // 8
    nchunk = tok_s.shape[0] // CH
    j = mine[0]

    def incoming(d, c):
        at = pl.ds(pl.multiple_of(c * (CH * 8), CH * 8), CH * 8)
        source, target = ((yad_h, yad), (ybc_h, ybc))[d]
        return pltpu.make_async_copy(source.at[at, :], target.at[at, :], y_sems.at[d, c])

    fetch((emb_h, w_in_h, cw_h, bias_h, rate_h, skip_h, gain_h, w_out_h),
          (emb, w_in, cw, bias, rate, skip, gain, w_out), sems)
    for c in range(nchunk):
        for d in range(2):
            incoming(d, c).start()
    symbol_tables(
        (0, 1), (zg, lac, xch, xcl),
        emb, w_in, cw, bias, rate, skip, gain, emb16, atab, gtab, cst, tw,
    )
    tok_x[0:half, :] = near[...]
    tok_x[half:rows, :] = far[...]
    for b in range(own):
        slot = (j ^ b) * 8
        tok_f[3, 8 * b : 8 * b + 8, :] = tok_x[pl.ds(pl.multiple_of(slot, 8), 8), :].astype(F32)
    tok = tok_f[3]
    for o in (-3, -2, -1, 1, 2, 3):
        tok_f[3 + o] = shifted(tok, o, rows)
    lane = iota((rows, CH), 1)
    row = iota((rows, CH), 0)
    lane_f = lane.astype(F32)
    before = 25.0 * tok_f[0] + 5.0 * tok_f[1] + tok_f[2]
    after = 25.0 * tok_f[6] + 5.0 * tok_f[5] + tok_f[4]
    code[0] = jnp.where((row == 0) & (lane < 3), 125.0 + lane_f, before)
    code[1] = jnp.where((row == rows - 1) & (lane >= CH - 3), lane_f, after)
    si = iota((CH, CH), 0)
    ri = iota((CH, CH), 1)
    ones = jnp.ones((CH, CH), F32)
    tri[0] = jnp.concatenate([jnp.where(si > ri, 1.0, 0.0), ones], axis=1).astype(BF16)
    tri[1] = jnp.concatenate([jnp.where(si < ri, 1.0, 0.0), ones], axis=1).astype(BF16)
    hist[...] = jnp.zeros_like(hist)
    sub8 = iota((8, CH), 0).astype(F32)
    subc = iota((CH, CH), 0).astype(F32)

    def block(b, off):
        side = jnp.where(b >= j, 1, 0)
        index = jnp.where(b >= j, b + 1, j - 1 - b)
        off = off * jnp.where(b == j, 0.0, 1.0)
        use_prefix = side.astype(F32)
        at = pl.ds(pl.multiple_of(index * 8, 8), 8)
        tk = tok_f[3, at, :]
        cd = code[side, at, :]
        hots = [jnp.where(tk[m : m + 1, :] == sub8, 1.0, 0.0) for m in range(8)]
        counts = nn(jnp.concatenate(hots, axis=0).astype(BF16), tri[side])
        totals = [counts[8 * m : 8 * m + 8, CH:] for m in range(8)]
        prefix = [jnp.zeros((8, CH), F32)]
        for m in range(8):
            prefix.append(prefix[-1] + totals[m])
        las = [lac[pl.ds(pl.multiple_of((side * SYM + v) * 16, 16), 16), :] for v in range(SYM)]
        acc = jnp.zeros((160, CH), F32)
        for pair in range(4):
            lefts, rights = [], []
            for m in (2 * pair, 2 * pair + 1):
                suffix = prefix[8] - prefix[m + 1]
                inside = suffix + use_prefix * (prefix[m] - suffix)
                count = counts[8 * m : 8 * m + 8, :CH] + off + inside
                exponent = las[0] * count[0:1, :]
                for v in range(1, SYM):
                    exponent = exponent + las[v] * count[v : v + 1, :]
                weight = jnp.exp2(exponent)
                masked = jnp.concatenate(
                    [jnp.where(tk[m : m + 1, :] == float(v), weight, 0.0) for v in range(SYM)],
                    axis=0,
                )
                high, low = split(masked)
                lefts.append(jnp.concatenate([high, low], axis=0))
                rights.append(jnp.where(cd[m : m + 1, :] == subc, 1.0, 0.0).astype(BF16))
            acc = acc + nt(
                jnp.concatenate(lefts, axis=1), jnp.concatenate(rights, axis=1)
            )
        hist[side] = hist[side] + acc
        return off + prefix[8]

    lax.fori_loop(0, own - 1, block, jnp.zeros((8, CH), F32))

    last8 = rows - 8
    mine8 = pl.ds(pl.multiple_of(j * 8, 8), 8)
    xs = {}
    for d in range(2):
        edge = 0 if d == 0 else 7
        seq_at = pl.ds(0 if d == 0 else last8, 8)
        hot_seq = window_onehot([tok_f[o, seq_at, :][edge : edge + 1, :] for o in range(7)])
        hot_own = window_onehot([tok_f[o, mine8, :][edge : edge + 1, :] for o in range(7)])
        for s in range(2):
            q = 2 * d + s
            xseq = silu_half(nn(hot_seq, tw[q]))
            xown = silu_half(nn(hot_own, tw[q]))
            if d == 0:
                xs[q] = pltpu.roll(xseq[0:8, :], 5, 0)
            else:
                xs[q] = xseq[CH - 8 :, :]
            for n in range(KW - 1):
                t = n if d == 0 else CH - 1 - n
                for i in range(4):
                    at = (d * 3 + n) * 8 + s * 4 + i
                    xrim[at : at + 1, :] = xown[t : t + 1, 128 * i : 128 * i + 128]
    diag = iota((H, E), 0) == (iota((H, E), 1) >> 6)
    sub16 = iota((16, E), 0)
    for q in range(4):
        d, s = q // 2, q % 2
        rim = jnp.concatenate([jnp.zeros((8, E), F32), xs[q]], axis=0)
        rim_h, rim_l = split(rim)
        for v in range(SYM):
            start = (q * SYM + v) * CH
            body = slice(start, start + CH - 16)
            tail = slice(start + CH - 16, start + CH)
            tail_h = jnp.where(sub16 >= 13, rim_h.astype(F32), xch[tail, :].astype(F32))
            tail_l = jnp.where(sub16 >= 13, rim_l.astype(F32), xcl[tail, :].astype(F32))
            table_h = jnp.concatenate([xch[body, :], tail_h.astype(BF16)], axis=0)
            table_l = jnp.concatenate([xcl[body, :], tail_l.astype(BF16)], axis=0)
            at = v * 16 + s * 8
            w = hist[d, at : at + 8, :] + hist[d, 80 + at : 88 + at, :]
            high, low = split(w)
            both = jnp.concatenate([high.astype(F32), low.astype(F32)], axis=0).astype(BF16)
            one = nn(both, table_h)
            two = nn(both, table_l)
            full = one[0:8, :] + one[8:16, :] + two[0:8, :]
            vec = jnp.sum(jnp.where(diag, full, 0.0), axis=0, keepdims=True)
            for i in range(4):
                at = (d * SYM + v) * 8 + s * 4 + i
                svec[at : at + 1, :] = vec[:, 128 * i : 128 * i + 128]
    total = tok_s.shape[0]
    for d in range(2):
        state = []
        for w in range(SYM):
            value = jnp.zeros((8, CH), F32)
            for v in range(SYM):
                at = (d * SYM + w) * 64 + v * 8
                sat = (d * SYM + v) * 8
                value = value + gtab[at : at + 8, :] * svec[sat : sat + 8, :]
            state.append(value)
        skip_t = cst[d * 8 : d * 8 + 8, :]
        for n in range(KW - 1):
            u = tok_s[n if d == 0 else total - 1 - n]
            x = xrim[(d * 3 + n) * 8 : (d * 3 + n) * 8 + 8, :]
            a = tile_at(atab, d * 64 + u * 8)
            state = [
                a * state[w] + tile_at(gtab, (d * SYM + w) * 64 + u * 8) * x
                for w in range(SYM)
            ]
            yrim[(d * 3 + n) * 8 : (d * 3 + n) * 8 + 8, :] = pick(state, u) + skip_t * x
        for w in range(SYM):
            ycar[(d * SYM + w) * 8 : (d * SYM + w) * 8 + 8, :] = state[w]

    for d in range(2):
        for u in range(SYM):
            at = slice((d * SYM + u) * 8, (d * SYM + u) * 8 + 8)
            carry_g[at, :] = ycar[at, :] * zg[u * 8 : u * 8 + 8, :]
    for d in range(2):
        for n in range(KW - 1):
            t = n if d == 0 else nchunk * CH - 1 - n
            at = slice((d * 3 + n) * 8, (d * 3 + n) * 8 + 8)
            yrim[at, :] = yrim[at, :] * tile_at(zg, tok_s[t] * 8)
    flip = jnp.where(iota((D, D), 0) + iota((D, D), 1) == D - 1, 1.0, 0.0).astype(BF16)
    wout = w_out[...]
    wflip = nn(wout, flip).astype(BF16)
    mean = jnp.where(
        (iota((2 * CH, 2 * CH), 0) >> 6) == (iota((2 * CH, 2 * CH), 1) >> 6), 1.0 / 64.0, 0.0
    ).astype(BF16)
    emb_rows = jnp.concatenate(
        [emb16[0:8, :], jnp.zeros((CH - 8, D), F32)], axis=0
    ).astype(BF16)
    gains = (cst[16:24, :], cst[24:32, :])
    sub = iota((8, CH), 0).astype(F32)
    mix[...] = jnp.zeros_like(mix)
    tiles = CH // SUB

    def project(c):
        base = (c & 1) * (CH * 8)
        row = tok_f[3, pl.ds(j * 8 + c, 1), :]
        hot = jnp.concatenate(
            [jnp.where(row == sub, 1.0, 0.0), jnp.zeros((CH - 8, CH), F32)], axis=0
        ).T.astype(BF16)
        parts = [mix[pl.ds(base + i, CH, stride=8), :].astype(BF16) for i in range(8)]
        one = nn(jnp.concatenate(parts[0:4], axis=1), wout).astype(BF16).astype(F32)
        two = nn(jnp.concatenate(parts[4:8], axis=1), wflip).astype(BF16).astype(F32)
        out[pl.ds(pl.multiple_of(c * CH, CH), CH), :] = (nn(hot, emb_rows) + one + two).astype(BF16)

    def tile(c, k):
        base = c * CH + k * SUB
        found = []
        for d, ref, pst in ((0, yad, psta), (1, ybc, pstb)):
            decay = tile_at(pst, (c * tiles + k) * 8)
            edge = c == (0 if d == 0 else nchunk - 1)
            values = [None] * SUB
            for n in range(SUB):
                local = n if d == 0 else SUB - 1 - n
                u = tok_s[base + local]
                a = tile_at(atab, d * 64 + u * 8)
                rim = n < KW - 1 and k == (0 if d == 0 else tiles - 1)
                if rim:
                    a = jnp.where(edge, 1.0, a)
                decay = decay * a
                g = tile_at(ref, (base + local) * 8) * tile_at(zg, u * 8) + decay * tile_at(
                    carry_g, d * SYM * 8 + u * 8
                )
                if rim:
                    at = slice((d * 3 + n) * 8, (d * 3 + n) * 8 + 8)
                    g = jnp.where(edge, yrim[at, :], g)
                values[local] = g
            found.append(jnp.concatenate(values, axis=0))
        high, low = split(jnp.concatenate([g * g for g in found], axis=1))
        scale = lax.rsqrt(nn(high, mean) + nn(low, mean) + EPSILON)
        normed = None
        for d in range(2):
            scaled = (found[d] * scale[:, CH * d : CH * d + CH]).reshape(SUB, 8, CH) * gains[d][None]
            normed = scaled if normed is None else normed + scaled
        at = (c & 1) * (CH * 8) + k * SUB * 8
        mix[pl.ds(pl.multiple_of(at, 8), SUB * 8), :] = normed.reshape(SUB * 8, CH)

    def chunk(c, _):
        for d in range(2):
            incoming(d, c).wait()
        project(jnp.maximum(c - 1, 0))
        for k in range(tiles):
            tile(c, k)
        return 0

    lax.fori_loop(0, nchunk, chunk, 0)
    project(nchunk - 1)


def per_device(
    token_ids,
    embed_table,
    input_weight_matrix,
    output_weight_matrix,
    conv_weight,
    dt_bias,
    decay_rate,
    skip_gain,
    norm_gain,
):
    length = token_ids.shape[0]
    nchunk = length // CH
    own = lax.axis_size("seq")
    tok2 = token_ids.reshape(nchunk, CH)
    rounds = own.bit_length() - 1
    rows = own * nchunk
    vm = pl.BlockSpec(memory_space=pltpu.VMEM)
    sm = pl.BlockSpec(memory_space=pltpu.SMEM)
    hbm = pl.BlockSpec(memory_space=pl.ANY)
    sds = jax.ShapeDtypeStruct
    limit = pltpu.CompilerParams(vmem_limit_bytes=56 * 1024 * 1024)
    weights = (
        embed_table, input_weight_matrix.T, conv_weight, dt_bias, decay_rate, skip_gain, norm_gain,
    )
    dma = pltpu.SemaphoreType.DMA
    table_scratch = [
        pltpu.VMEM((16, D), F32),
        pltpu.VMEM((2 * 64, CH), F32),
        pltpu.VMEM((2 * SYM * 64, CH), F32),
        pltpu.VMEM((32, CH), F32),
        pltpu.VMEM((4, CH, E), BF16),
    ]

    def sent(blocks, bit):
        return lax.ppermute(blocks, "seq", [(i, i ^ (1 << bit)) for i in range(own)])

    def chains(direction):
        return pl.pallas_call(
            functools.partial(direction_kernel, direction),
            out_shape=(sds((length * 8, CH), F32), sds((length // SUB * 8, CH), F32)),
            in_specs=[sm, vm] + [hbm] * 7,
            out_specs=(hbm, vm),
            scratch_shapes=[pltpu.VMEM(w.shape, w.dtype) for w in weights]
            + table_scratch
            + [pltpu.VMEM((length * 8, CH), F32)] * 2
            + [dma((7,)), dma((nchunk,))],
            compiler_params=limit,
            cost_estimate=pl.CostEstimate(
                flops=3_000_000_000, bytes_accessed=16_000_000, transcendentals=0
            ),
            name=("increasing", "decreasing")[direction],
        )(token_ids, tok2, *weights)

    near, far = tok2, sent(tok2, 0)
    if rounds > 1:
        near = jnp.concatenate([near, far], axis=0)
        far = sent(near, 1)
    yad, psta = chains(0)
    near, far, yad, psta = lax.optimization_barrier((near, far, yad, psta))
    for bit in range(2, rounds):
        near = jnp.concatenate([near, far], axis=0)
        far = sent(near, bit)
    ybc, pstb = chains(1)
    near, far, yad, ybc = lax.optimization_barrier((near, far, yad, ybc))
    mine = lax.axis_index("seq").reshape(1).astype(jnp.int32)
    big = pltpu.VMEM((4 * SYM * CH, E), BF16)
    return pl.pallas_call(
        last_kernel,
        out_shape=sds((length, D), BF16),
        in_specs=[sm, sm, vm, vm, hbm, hbm, vm, vm] + [hbm] * 8,
        out_specs=vm,
        scratch_shapes=[pltpu.VMEM(w.shape, w.dtype) for w in weights]
        + [pltpu.VMEM((E, D), BF16)]
        + table_scratch
        + [
            pltpu.VMEM((64, CH), F32),
            pltpu.VMEM((2 * SYM * 16, CH), F32),
            big,
            big,
            pltpu.VMEM((rows, CH), jnp.int32),
            pltpu.VMEM((7, rows, CH), F32),
            pltpu.VMEM((2, rows, CH), F32),
            pltpu.VMEM((2, CH, 2 * CH), BF16),
            pltpu.VMEM((2, 160, CH), F32),
            pltpu.VMEM((2 * SYM * 8, CH), F32),
            pltpu.VMEM((2 * 3 * 8, CH), F32),
            pltpu.VMEM((2 * SYM * 8, CH), F32),
            pltpu.VMEM((2 * 3 * 8, CH), F32),
            pltpu.VMEM((2 * SYM * 8, CH), F32),
            pltpu.VMEM((length * 8, CH), F32),
            pltpu.VMEM((length * 8, CH), F32),
            pltpu.VMEM((2 * CH * 8, CH), F32),
            dma((8,)),
            dma((2, nchunk)),
        ],
        compiler_params=limit,
        cost_estimate=pl.CostEstimate(
            flops=6_000_000_000, bytes_accessed=16_000_000, transcendentals=0
        ),
        name="history_finish",
    )(mine, token_ids, near, far, yad, ybc, psta, pstb, *weights, output_weight_matrix)


def solution(mesh):
    placed = (P(("batch", "seq")), P(), P(), P(), P(), P(), P(), P(), P())
    return jax.shard_map(
        per_device, mesh=mesh, in_specs=placed, out_specs=P(("batch", "seq"), None), check_vma=False
    )
```

time: 49.2 us -> 46.1 us (0.937)
  local copies, waits for them, and re-layouts: 7.27 us -> 0.6 us
  Pallas kernels: 31.3 us -> 34.9 us
  other arithmetic: 2.87 us -> 0.69 us
  waiting for transfers between devices: 0.01 us -> 1.8 us
  starting transfers between devices: 7.18 us -> 7.7 us
    unnamed x28 -> x5, local copies, waits for them, and re-layouts: 6.55 us -> 0.6 us
    pallas_call x5 -> x3, Pallas kernels: 31.3 us -> 34.9 us  [the longest x2 18.7 us: chains(): pl.pallas_call(functools.partial(direction_kernel, direction), out_shape=...]
    ppermute x3, waiting for transfers between devices: 0.01 us -> 1.8 us  [sent(): return lax.ppermute(blocks, 'seq', [(i, i ^ 1 << bit) for i in range(own)])]
    concatenate x5 -> x1, other arithmetic: 2.18 us -> 0.69 us  [per_device(): near = jnp.concatenate([near, far], axis=0)]
    reshape x1 -> x0, local copies, waits for them, and re-layouts: 0.73 us -> none  [per_device(): conv_weight.reshape(2 * KW, E)]
    pad x1 -> x0, other arithmetic: 0.69 us -> none  [per_device(): jnp.pad(embed_table.astype(F32), ((0, 3), (0, E - D)))]
    ppermute x3, starting transfers between devices: 7.18 us -> 7.7 us  [sent(): return lax.ppermute(blocks, 'seq', [(i, i ^ 1 << bit) for i in range(own)])]
  transfers between devices with their start and end apart: 3 -> 3, of which waited for: 0 -> 1; matrix products, arithmetic and copies ran while one was open for 6% -> 0% of each run, Pallas kernels for 27% -> 41%
where the time goes in v4:
time: 46.1 us; the launch traced here: 45.7 us
  Pallas kernels  34.9 us (76%)
  starting transfers between devices  7.7 us (17%)
  waiting for transfers between devices  1.8 us (4%)
  other arithmetic  0.69 us (1%)
  local copies, waits for them, and re-layouts  0.6 us (1%)
    pallas_call x2, Pallas kernels, chains(): pl.pallas_call(functools.partial(direction_kernel, direction), out_shape=...  18.7 us
    pallas_call x1, Pallas kernels, per_device(): pl.pallas_call(last_kernel, out_shape=sds((length, D), BF16), in_specs=[s...  16.2 us
    ppermute x3, starting transfers between devices, sent(): return lax.ppermute(blocks, 'seq', [(i, i ^ 1 << bit) for i in range(own)])  7.7 us
    ppermute x3, waiting for transfers between devices, sent(): return lax.ppermute(blocks, 'seq', [(i, i ^ 1 << bit) for i in range(own)])  1.8 us
  transfers between devices with their start and end apart: 3, of which 1 were waited for; matrix products, arithmetic and copies ran while one was open for 0% of the time, Pallas kernels for 41%

profile of v4, /device:TPU:0, one launch (start us, length us, event | category | flops | bytes accessed | tf_op | source)
XLA Modules:
  0.0 45.7 jit_solution(11028365410605828525)
XLA Ops:
  0.0 3.0 %collective-permute-start = (s32[8,128]{1,0:T(8,128)}, s32[8,128]{1,0:T(8,128)S(1)}, u32[]{:S(2)}, u32[]{:S(2)}) collective-permute-start(s32[8,128]{1,0:T(8,128)} %bitcast.3), channel_id=1, source_target_pairs={{0,4},{4,0},{8,12},{12,8},{16,20},{20,16},{24,28},{28,24},{1,5},{5... | collective-permute-start | bytes 12296 | tf_op jit(solution)/shard_map/ppermute | solution.py:544
  3.0 1.8 %collective-permute-done = s32[8,128]{1,0:T(8,128)S(1)} collective-permute-done((s32[8,128]{1,0:T(8,128)}, s32[8,128]{1,0:T(8,128)S(1)}, u32[]{:S(2)}, u32[]{:S(2)}) %collective-permute-start) | collective-permute-done | bytes 4128 | tf_op jit(solution)/shard_map/ppermute | solution.py:544
  4.8 0.7 %pad_add_fusion = s32[16,128]{1,0:T(8,128)S(1)} fusion(s32[8,128]{1,0:T(8,128)S(1)} %collective-permute-done, s32[8,128]{1,0:T(8,128)} %bitcast.4), kind=kLoop, calls=%fused_computation | loop fusion | flops 2048 | bytes 16384 | tf_op jit(solution)/shard_map/concatenate | solution.py:565
  5.5 2.1 %collective-permute-start.1 = (s32[16,128]{1,0:T(8,128)S(1)}, s32[16,128]{1,0:T(8,128)S(1)}, u32[]{:S(2)}, u32[]{:S(2)}) collective-permute-start(s32[16,128]{1,0:T(8,128)S(1)} %pad_add_fusion), channel_id=1, source_target_pairs={{0,8},{4,12},{8,0},{12,4},{16,24},{20,28},{24,16},{28,20},{1,9},{5... | collective-permute-start | bytes 24584 | tf_op jit(solution)/shard_map/ppermute | solution.py:544
  7.5 8.9 %increasing.1 = (f32[8192,128]{1,0:T(8,128)}, f32[512,128]{1,0:T(8,128)}) custom-call(s32[1024]{0:T(1024)} %tok_s.5, s32[8,128]{1,0:T(8,128)} %bitcast.5, bf16[5,256]{1,0:T(8,128)(2,1)} %emb_h.5, bf16[1064,256]{1,0:T(8,128)(2,1)} %bitcast.7, f32[2,4,512]{2,1,0:T(4,128)} %cw_h.5, f32[2,8]{1,0:T(2,128)} %bias_h.5, f32[2,8]{1,0:T(2,128)} %rate_h.5, ...), custom_call_target="tpu_custom_call" | custom-call | flops 3000000000 | bytes 16000000 | tf_op jit(solution)/shard_map/increasing/pallas_call | solution.py:547
  16.5 0.0 collective-permute-done.1
  16.5 0.0 copy-start
  16.5 2.7 %collective-permute-start.2 = (s32[32,128]{1,0:T(8,128)S(1)}, s32[32,128]{1,0:T(8,128)S(1)}, u32[]{:S(2)}, u32[]{:S(2)}) collective-permute-start(s32[32,128]{1,0:T(8,128)S(1)} %constant_dynamic-update-slice_fusion.near), channel_id=1, source_target_pairs={{0,16},{4,20},{8,24},{12,28},{16,0},{20,4},{24,8},{28,12},{1,17},{... | collective-permute-start | bytes 49160 | tf_op jit(solution)/shard_map/ppermute | solution.py:544
  19.2 9.7 %decreasing.1 = (f32[8192,128]{1,0:T(8,128)}, f32[512,128]{1,0:T(8,128)}) custom-call(s32[1024]{0:T(1024)} %tok_s.5, s32[8,128]{1,0:T(8,128)} %bitcast.6, bf16[5,256]{1,0:T(8,128)(2,1)} %emb_h.5, bf16[1064,256]{1,0:T(8,128)(2,1)} %bitcast.8, f32[2,4,512]{2,1,0:T(4,128)} %cw_h.5, f32[2,8]{1,0:T(2,128)} %bias_h.5, f32[2,8]{1,0:T(2,128)} %rate_h.5, ...), custom_call_target="tpu_custom_call" | custom-call | flops 3000000000 | bytes 16000000 | tf_op jit(solution)/shard_map/decreasing/pallas_call | solution.py:547
  28.9 0.0 copy-done
  28.9 0.0 collective-permute-done.2.far
  29.0 0.0 copy-start.1
  29.0 0.6 %copy-done.1 = s32[32,128]{1,0:T(8,128)} copy-done((s32[32,128]{1,0:T(8,128)}, s32[32,128]{1,0:T(8,128)S(1)}, u32[]{:S(2)}) %copy-start.1) | copy-done | bytes 16408
  29.6 16.2 %history_finish.1 = bf16[1024,256]{1,0:T(8,128)(2,1)} custom-call(s32[1]{0:T(128)} %bitcast.mine, s32[1024]{0:T(1024)} %tok_s.5, s32[32,128]{1,0:T(8,128)} %copy-done, s32[32,128]{1,0:T(8,128)} %copy-done.1, f32[8192,128]{1,0:T(8,128)} %get-tuple-element.25.yad_h, f32[8192,128]{1,0:T(8,128)} %get-tuple-element.26.ybc_h, f32[512,128]{1,0:T(8,128)} %get-tuple-element.27.psta, ...), custom_call_target="tpu_custom_call" | custom-call | flops 6000000000 | bytes 16000000 | tf_op jit(solution)/shard_map/history_finish/pallas_call | solution.py:576
  (2 shorter events, 0.0 us)
Async XLA Ops:
  0.0 4.8 %collective-permute-start = (s32[8,128]{1,0:T(8,128)}, s32[8,128]{1,0:T(8,128)S(1)}, u32[]{:S(2)}, u32[]{:S(2)}) collective-permute-start(s32[8,128]{1,0:T(8,128)} %bitcast.3), channel_id=1, source_target_pairs={{0,4},{4,0},{8,12},{12,8},{16,20},{20,16},{24,28},{28,24},{1,5},{5... | collective-permute-start | bytes 12296 | tf_op jit(solution)/shard_map/ppermute | solution.py:544
  5.5 11.0 %collective-permute-start.1 = (s32[16,128]{1,0:T(8,128)S(1)}, s32[16,128]{1,0:T(8,128)S(1)}, u32[]{:S(2)}, u32[]{:S(2)}) collective-permute-start(s32[16,128]{1,0:T(8,128)S(1)} %pad_add_fusion), channel_id=1, source_target_pairs={{0,8},{4,12},{8,0},{12,4},{16,24},{20,28},{24,16},{28,20},{1,9},{5... | collective-permute-start | bytes 24584 | tf_op jit(solution)/shard_map/ppermute | solution.py:544
  16.5 12.4 %copy-start = (s32[32,128]{1,0:T(8,128)}, s32[32,128]{1,0:T(8,128)S(1)}, u32[]{:S(2)}) copy-start(s32[32,128]{1,0:T(8,128)S(1)} %constant_dynamic-update-slice_fusion.near) | copy-start | bytes 49156
  16.5 12.4 %collective-permute-start.2 = (s32[32,128]{1,0:T(8,128)S(1)}, s32[32,128]{1,0:T(8,128)S(1)}, u32[]{:S(2)}, u32[]{:S(2)}) collective-permute-start(s32[32,128]{1,0:T(8,128)S(1)} %constant_dynamic-update-slice_fusion.near), channel_id=1, source_target_pairs={{0,16},{4,20},{8,24},{12,28},{16,0},{20,4},{24,8},{28,12},{1,17},{... | collective-permute-start | bytes 49160 | tf_op jit(solution)/shard_map/ppermute | solution.py:544
  29.0 0.6 %copy-start.1 = (s32[32,128]{1,0:T(8,128)}, s32[32,128]{1,0:T(8,128)S(1)}, u32[]{:S(2)}) copy-start(s32[32,128]{1,0:T(8,128)S(1)} %collective-permute-done.2.far) | copy-start | bytes 49156

commit v5 on v4

--- a/solution.py
+++ b/solution.py
@@ -195,107 +195,34 @@
             xcl[(q * SYM + v) * CH : (q * SYM + v + 1) * CH, :] = low
 
 
-def direction_kernel(
-    direction, tok_s, tok_v, emb_h, w_in_h, cw_h, bias_h, rate_h, skip_h, gain_h,
-    y_h, pst,
-    emb, w_in, cw, bias, rate, skip, gain, emb16, atab, gtab, cst, tw, x_v, y_v, sems, y_sems,
+def layer_kernel(
+    count, mine, tok_s, emb_h, w_in_h, cw_h, bias_h, rate_h, skip_h, gain_h, w_out_h, *others
 ):
+    finish_layer(
+        others[:count], mine, tok_s, emb_h, w_in_h, cw_h, bias_h, rate_h, skip_h, gain_h, w_out_h,
+        *others[count:]
+    )
+
+
+def finish_layer(
+    blocks, mine, tok_s, emb_h, w_in_h, cw_h, bias_h, rate_h, skip_h, gain_h, w_out_h,
+    out,
+    emb, w_in, cw, bias, rate, skip, gain, w_out, emb16, atab, gtab, cst, tw, zg, lac, xch, xcl,
+    tok_x, tok_f, code, tri, hist, svec, xad, xbc, yad, ybc, mix, sems,
+):
+    rows = tok_x.shape[0]
+    own = rows // 8
     total = tok_s.shape[0]
     nchunk = total // CH
-    fetch((emb_h, w_in_h, cw_h, bias_h, rate_h, skip_h, gain_h),
-          (emb, w_in, cw, bias, rate, skip, gain), sems)
-    symbol_tables(
-        (direction,), None, emb, w_in, cw, bias, rate, skip, gain, emb16, atab, gtab, cst, tw
-    )
-    tok = tok_v[...].astype(F32)
-    shifts = [shifted(tok, o, nchunk) for o in range(1 - KW, KW)]
-    for c in range(nchunk):
-        hot = window_onehot([sh[c : c + 1, :] for sh in shifts])
-        for s in range(2):
-            x = silu_half(nn(hot, tw[2 * direction + s]))
-            for i in range(4):
-                x_v[pl.ds(c * 8 * CH + s * 4 + i, CH, stride=8), :] = x[:, 128 * i : 128 * i + 128]
-    rim = (KW - 1) * 8
-    if direction == 0:
-        x_v[0:rim, :] = jnp.zeros((rim, CH), F32)
-    else:
-        x_v[total * 8 - rim : total * 8, :] = jnp.zeros((rim, CH), F32)
-
-    skip_t = cst[8 * direction : 8 * direction + 8, :]
-    unroll = 32
-    held = 8
-
-    def group(g, carry):
-        state, decay = list(carry[0]), carry[1]
-        for begin in range(0, unroll, held):
-            done = []
-            for i in range(begin, begin + held):
-                n = g * unroll + i
-                t = n if direction == 0 else total - 1 - n
-                if i % SUB == 0:
-                    first = n if direction == 0 else t - SUB + 1
-                    pst[pl.ds(pl.multiple_of((first // SUB) * 8, 8), 8), :] = decay
-                u = tok_s[t]
-                x = tile_at(x_v, t * 8)
-                a = tile_at(atab, direction * 64 + u * 8)
-                state = [
-                    a * state[w] + tile_at(gtab, (direction * SYM + w) * 64 + u * 8) * x
-                    for w in range(SYM)
-                ]
-                done.append((t, pick(state, u) + skip_t * x))
-                if i < KW - 1:
-                    a = jnp.where(g == 0, 1.0, a)
-                decay = decay * a
-            for t, y in done:
-                y_v[pl.ds(pl.multiple_of(t * 8, 8), 8), :] = y
-        return tuple(state), decay
-
-    def stream(c):
-        at = c if direction == 0 else nchunk - 1 - c
-        rows = pl.ds(pl.multiple_of(at * (CH * 8), CH * 8), CH * 8)
-        return pltpu.make_async_copy(y_v.at[rows, :], y_h.at[rows, :], y_sems.at[c])
-
-    def chunk(c, carry):
-        per = CH // unroll
-        carry = lax.fori_loop(c * per, (c + 1) * per, group, carry)
-        stream(c).start()
-        return carry
-
-    zero = jnp.zeros((8, CH), F32)
-    lax.fori_loop(0, nchunk, chunk, ((zero,) * SYM, jnp.ones((8, CH), F32)))
-    for c in range(nchunk):
-        stream(c).wait()
-
-
-def last_kernel(
-    mine, tok_s, near, far, yad_h, ybc_h, psta, pstb,
-    emb_h, w_in_h, cw_h, bias_h, rate_h, skip_h, gain_h, w_out_h,
-    out,
-    emb, w_in, cw, bias, rate, skip, gain, w_out, emb16, atab, gtab, cst, tw, zg, lac, xch, xcl,
-    tok_x, tok_f, code, tri, hist, svec, xrim, ycar, yrim, carry_g, yad, ybc, mix, sems, y_sems,
-):
-    half = near.shape[0]
-    rows = 2 * half
-    own = rows // 8
-    nchunk = tok_s.shape[0] // CH
     j = mine[0]
-
-    def incoming(d, c):
-        at = pl.ds(pl.multiple_of(c * (CH * 8), CH * 8), CH * 8)
-        source, target = ((yad_h, yad), (ybc_h, ybc))[d]
-        return pltpu.make_async_copy(source.at[at, :], target.at[at, :], y_sems.at[d, c])
-
-    fetch((emb_h, w_in_h, cw_h, bias_h, rate_h, skip_h, gain_h, w_out_h),
-          (emb, w_in, cw, bias, rate, skip, gain, w_out), sems)
-    for c in range(nchunk):
-        for d in range(2):
-            incoming(d, c).start()
+    size = rows // len(blocks)
+    fetch((emb_h, w_in_h, cw_h, bias_h, rate_h, skip_h, gain_h, w_out_h, *blocks),
+          (emb, w_in, cw, bias, rate, skip, gain, w_out,
+           *[tok_x.at[size * m : size * m + size, :] for m in range(len(blocks))]), sems)
     symbol_tables(
         (0, 1), (zg, lac, xch, xcl),
         emb, w_in, cw, bias, rate, skip, gain, emb16, atab, gtab, cst, tw,
     )
-    tok_x[0:half, :] = near[...]
-    tok_x[half:rows, :] = far[...]
     for b in range(own):
         slot = (j ^ b) * 8
         tok_f[3, 8 * b : 8 * b + 8, :] = tok_x[pl.ds(pl.multiple_of(slot, 8), 8), :].astype(F32)
@@ -365,21 +292,12 @@
     for d in range(2):
         edge = 0 if d == 0 else 7
         seq_at = pl.ds(0 if d == 0 else last8, 8)
-        hot_seq = window_onehot([tok_f[o, seq_at, :][edge : edge + 1, :] for o in range(7)])
-        hot_own = window_onehot([tok_f[o, mine8, :][edge : edge + 1, :] for o in range(7)])
+        hot = window_onehot([tok_f[o, seq_at, :][edge : edge + 1, :] for o in range(7)])
         for s in range(2):
-            q = 2 * d + s
-            xseq = silu_half(nn(hot_seq, tw[q]))
-            xown = silu_half(nn(hot_own, tw[q]))
             if d == 0:
-                xs[q] = pltpu.roll(xseq[0:8, :], 5, 0)
+                xs[s] = pltpu.roll(silu_half(nn(hot[0:16, :], tw[s]))[0:8, :], 5, 0)
             else:
-                xs[q] = xseq[CH - 8 :, :]
-            for n in range(KW - 1):
-                t = n if d == 0 else CH - 1 - n
-                for i in range(4):
-                    at = (d * 3 + n) * 8 + s * 4 + i
-                    xrim[at : at + 1, :] = xown[t : t + 1, 128 * i : 128 * i + 128]
+                xs[2 + s] = silu_half(nn(hot[CH - 16 :, :], tw[2 + s]))[8:16, :]
     diag = iota((H, E), 0) == (iota((H, E), 1) >> 6)
     sub16 = iota((16, E), 0)
     for q in range(4):
@@ -405,38 +323,56 @@
             for i in range(4):
                 at = (d * SYM + v) * 8 + s * 4 + i
                 svec[at : at + 1, :] = vec[:, 128 * i : 128 * i + 128]
-    total = tok_s.shape[0]
+    starts = []
     for d in range(2):
-        state = []
         for w in range(SYM):
             value = jnp.zeros((8, CH), F32)
             for v in range(SYM):
                 at = (d * SYM + w) * 64 + v * 8
                 sat = (d * SYM + v) * 8
                 value = value + gtab[at : at + 8, :] * svec[sat : sat + 8, :]
-            state.append(value)
-        skip_t = cst[d * 8 : d * 8 + 8, :]
-        for n in range(KW - 1):
-            u = tok_s[n if d == 0 else total - 1 - n]
-            x = xrim[(d * 3 + n) * 8 : (d * 3 + n) * 8 + 8, :]
-            a = tile_at(atab, d * 64 + u * 8)
-            state = [
-                a * state[w] + tile_at(gtab, (d * SYM + w) * 64 + u * 8) * x
-                for w in range(SYM)
-            ]
-            yrim[(d * 3 + n) * 8 : (d * 3 + n) * 8 + 8, :] = pick(state, u) + skip_t * x
-        for w in range(SYM):
-            ycar[(d * SYM + w) * 8 : (d * SYM + w) * 8 + 8, :] = state[w]
-
-    for d in range(2):
-        for u in range(SYM):
-            at = slice((d * SYM + u) * 8, (d * SYM + u) * 8 + 8)
-            carry_g[at, :] = ycar[at, :] * zg[u * 8 : u * 8 + 8, :]
-    for d in range(2):
-        for n in range(KW - 1):
-            t = n if d == 0 else nchunk * CH - 1 - n
-            at = slice((d * 3 + n) * 8, (d * 3 + n) * 8 + 8)
-            yrim[at, :] = yrim[at, :] * tile_at(zg, tok_s[t] * 8)
+            starts.append(value)
+
+    shifts = [tok_f[o, mine8, :] for o in range(7)]
+    for c in range(nchunk):
+        hot = window_onehot([sh[c : c + 1, :] for sh in shifts])
+        for q, (d, s, k) in enumerate(CHAINS):
+            x = silu_half(nn(hot, tw[q]))
+            ref = (xad, xbc)[d]
+            for i in range(4):
+                ref[pl.ds(c * 8 * CH + s * 4 + i, CH, stride=8), :] = x[:, 128 * i : 128 * i + 128]
+
+    skips = (cst[0:8, :], cst[8:16, :])
+
+    def advance(d, src, t, state):
+        u = tok_s[t]
+        x = tile_at(src, t * 8)
+        a = tile_at(atab, d * 64 + u * 8)
+        new = [
+            a * state[w] + tile_at(gtab, (d * SYM + w) * 64 + u * 8) * x for w in range(SYM)
+        ]
+        return new, (pick(new, u) + skips[d] * x) * tile_at(zg, u * 8)
+
+    unroll = 32
+    held = 8
+
+    def group(g, carry):
+        ya, yb = list(carry[:SYM]), list(carry[SYM:])
+        for begin in range(0, unroll, held):
+            done = []
+            for i in range(begin, begin + held):
+                n = g * unroll + i
+                m = total - 1 - n
+                ya, out0 = advance(0, xad, n, ya)
+                yb, out1 = advance(1, xbc, m, yb)
+                done.append((n, m, out0, out1))
+            for n, m, out0, out1 in done:
+                yad[pl.ds(pl.multiple_of(n * 8, 8), 8), :] = out0
+                ybc[pl.ds(pl.multiple_of(m * 8, 8), 8), :] = out1
+        return tuple(ya + yb)
+
+    lax.fori_loop(0, total // unroll, group, tuple(starts))
+
     flip = jnp.where(iota((D, D), 0) + iota((D, D), 1) == D - 1, 1.0, 0.0).astype(BF16)
     wout = w_out[...]
     wflip = nn(wout, flip).astype(BF16)
@@ -463,28 +399,8 @@
         out[pl.ds(pl.multiple_of(c * CH, CH), CH), :] = (nn(hot, emb_rows) + one + two).astype(BF16)
 
     def tile(c, k):
-        base = c * CH + k * SUB
-        found = []
-        for d, ref, pst in ((0, yad, psta), (1, ybc, pstb)):
-            decay = tile_at(pst, (c * tiles + k) * 8)
-            edge = c == (0 if d == 0 else nchunk - 1)
-            values = [None] * SUB
-            for n in range(SUB):
-                local = n if d == 0 else SUB - 1 - n
-                u = tok_s[base + local]
-                a = tile_at(atab, d * 64 + u * 8)
-                rim = n < KW - 1 and k == (0 if d == 0 else tiles - 1)
-                if rim:
-                    a = jnp.where(edge, 1.0, a)
-                decay = decay * a
-                g = tile_at(ref, (base + local) * 8) * tile_at(zg, u * 8) + decay * tile_at(
-                    carry_g, d * SYM * 8 + u * 8
-                )
-                if rim:
-                    at = slice((d * 3 + n) * 8, (d * 3 + n) * 8 + 8)
-                    g = jnp.where(edge, yrim[at, :], g)
-                values[local] = g
-            found.append(jnp.concatenate(values, axis=0))
+        at = pl.ds(pl.multiple_of((c * CH + k * SUB) * 8, SUB * 8), SUB * 8)
+        found = (yad[at, :], ybc[at, :])
         high, low = split(jnp.concatenate([g * g for g in found], axis=1))
         scale = lax.rsqrt(nn(high, mean) + nn(low, mean) + EPSILON)
         normed = None
@@ -495,8 +411,6 @@
         mix[pl.ds(pl.multiple_of(at, 8), SUB * 8), :] = normed.reshape(SUB * 8, CH)
 
     def chunk(c, _):
-        for d in range(2):
-            incoming(d, c).wait()
         project(jnp.maximum(c - 1, 0))
         for k in range(tiles):
             tile(c, k)
@@ -527,87 +441,57 @@
     sm = pl.BlockSpec(memory_space=pltpu.SMEM)
     hbm = pl.BlockSpec(memory_space=pl.ANY)
     sds = jax.ShapeDtypeStruct
-    limit = pltpu.CompilerParams(vmem_limit_bytes=56 * 1024 * 1024)
     weights = (
         embed_table, input_weight_matrix.T, conv_weight, dt_bias, decay_rate, skip_gain, norm_gain,
+        output_weight_matrix,
     )
-    dma = pltpu.SemaphoreType.DMA
-    table_scratch = [
-        pltpu.VMEM((16, D), F32),
-        pltpu.VMEM((2 * 64, CH), F32),
-        pltpu.VMEM((2 * SYM * 64, CH), F32),
-        pltpu.VMEM((32, CH), F32),
-        pltpu.VMEM((4, CH, E), BF16),
-    ]
-
-    def sent(blocks, bit):
-        return lax.ppermute(blocks, "seq", [(i, i ^ (1 << bit)) for i in range(own)])
-
-    def chains(direction):
-        return pl.pallas_call(
-            functools.partial(direction_kernel, direction),
-            out_shape=(sds((length * 8, CH), F32), sds((length // SUB * 8, CH), F32)),
-            in_specs=[sm, vm] + [hbm] * 7,
-            out_specs=(hbm, vm),
-            scratch_shapes=[pltpu.VMEM(w.shape, w.dtype) for w in weights]
-            + table_scratch
-            + [pltpu.VMEM((length * 8, CH), F32)] * 2
-            + [dma((7,)), dma((nchunk,))],
-            compiler_params=limit,
-            cost_estimate=pl.CostEstimate(
-                flops=3_000_000_000, bytes_accessed=16_000_000, transcendentals=0
-            ),
-            name=("increasing", "decreasing")[direction],
-        )(token_ids, tok2, *weights)
-
-    near, far = tok2, sent(tok2, 0)
-    if rounds > 1:
-        near = jnp.concatenate([near, far], axis=0)
-        far = sent(near, 1)
-    yad, psta = chains(0)
-    near, far, yad, psta = lax.optimization_barrier((near, far, yad, psta))
-    for bit in range(2, rounds):
-        near = jnp.concatenate([near, far], axis=0)
-        far = sent(near, bit)
-    ybc, pstb = chains(1)
-    near, far, yad, ybc = lax.optimization_barrier((near, far, yad, ybc))
+
+    def sent(blocks, mask):
+        return lax.ppermute(blocks, "seq", [(i, i ^ mask) for i in range(own)])
+
+    gathered = tok2
+    low = max(rounds - 3, 0)
+    for bit in range(low):
+        gathered = jnp.concatenate([gathered, sent(gathered, 1 << bit)], axis=0)
+    blocks = [gathered] + [sent(gathered, m << low) for m in range(1, own >> low)]
     mine = lax.axis_index("seq").reshape(1).astype(jnp.int32)
-    big = pltpu.VMEM((4 * SYM * CH, E), BF16)
+    table = pltpu.VMEM((4 * SYM * CH, E), BF16)
+    steps = pltpu.VMEM((length * 8, CH), F32)
     return pl.pallas_call(
-        last_kernel,
+        functools.partial(layer_kernel, len(blocks)),
         out_shape=sds((length, D), BF16),
-        in_specs=[sm, sm, vm, vm, hbm, hbm, vm, vm] + [hbm] * 8,
+        in_specs=[sm, sm] + [hbm] * 8 + [hbm] * len(blocks),
         out_specs=vm,
         scratch_shapes=[pltpu.VMEM(w.shape, w.dtype) for w in weights]
-        + [pltpu.VMEM((E, D), BF16)]
-        + table_scratch
         + [
+            pltpu.VMEM((16, D), F32),
+            pltpu.VMEM((2 * 64, CH), F32),
+            pltpu.VMEM((2 * SYM * 64, CH), F32),
+            pltpu.VMEM((32, CH), F32),
+            pltpu.VMEM((4, CH, E), BF16),
             pltpu.VMEM((64, CH), F32),
             pltpu.VMEM((2 * SYM * 16, CH), F32),
-            big,
-            big,
+            table,
+            table,
             pltpu.VMEM((rows, CH), jnp.int32),
             pltpu.VMEM((7, rows, CH), F32),
             pltpu.VMEM((2, rows, CH), F32),
             pltpu.VMEM((2, CH, 2 * CH), BF16),
             pltpu.VMEM((2, 160, CH), F32),
             pltpu.VMEM((2 * SYM * 8, CH), F32),
-            pltpu.VMEM((2 * 3 * 8, CH), F32),
-            pltpu.VMEM((2 * SYM * 8, CH), F32),
-            pltpu.VMEM((2 * 3 * 8, CH), F32),
-            pltpu.VMEM((2 * SYM * 8, CH), F32),
-            pltpu.VMEM((length * 8, CH), F32),
-            pltpu.VMEM((length * 8, CH), F32),
+            steps,
+            steps,
+            steps,
+            steps,
             pltpu.VMEM((2 * CH * 8, CH), F32),
-            dma((8,)),
-            dma((2, nchunk)),
+            pltpu.SemaphoreType.DMA((8 + len(blocks),)),
         ],
-        compiler_params=limit,
+        compiler_params=pltpu.CompilerParams(vmem_limit_bytes=56 * 1024 * 1024),
         cost_estimate=pl.CostEstimate(
-            flops=6_000_000_000, bytes_accessed=16_000_000, transcendentals=0
+            flops=9_000_000_000, bytes_accessed=4_000_000, transcendentals=0
         ),
-        name="history_finish",
-    )(mine, token_ids, near, far, yad, ybc, psta, pstb, *weights, output_weight_matrix)
+        name="bidirectional_layer",
+    )(mine, token_ids, *weights, *blocks)
 
 
 def solution(mesh):

time: 46.1 us -> 41.6 us (0.902)
  Pallas kernels: 34.9 us -> 24.9 us
  starting transfers between devices: 7.7 us -> 12.4 us
  waiting for transfers between devices: 1.8 us -> 3.46 us
  other arithmetic: 0.69 us -> 0 us
    pallas_call x3 -> x1, Pallas kernels: 34.9 us -> 24.9 us  [per_device(): pl.pallas_call(functools.partial(layer_kernel, len(blocks)), out_shape=sd...]
    ppermute x3 -> x7, starting transfers between devices: 7.7 us -> 12.4 us  [sent(): return lax.ppermute(blocks, 'seq', [(i, i ^ mask) for i in range(own)])]
    ppermute x3 -> x7, waiting for transfers between devices: 1.8 us -> 3.46 us  [sent(): return lax.ppermute(blocks, 'seq', [(i, i ^ mask) for i in range(own)])]
    concatenate x1 -> x0, other arithmetic: 0.69 us -> none  [per_device(): near = jnp.concatenate([near, far], axis=0)]
  transfers between devices with their start and end apart: 3 -> 7, of which waited for: 1 -> 3; matrix products, arithmetic and copies ran while one was open for 0% -> 0% of each run, Pallas kernels for 41% -> 0%
where the time goes in v5:
time: 41.6 us; the launch traced here: 41.4 us
  Pallas kernels  24.9 us (60%)
  starting transfers between devices  12.4 us (30%)
  waiting for transfers between devices  3.46 us (8%)
  local copies, waits for them, and re-layouts  0.57 us (1%)
    pallas_call x1, Pallas kernels, per_device(): pl.pallas_call(functools.partial(layer_kernel, len(blocks)), out_shape=sd...  24.9 us
    ppermute x7, starting transfers between devices, sent(): return lax.ppermute(blocks, 'seq', [(i, i ^ mask) for i in range(own)])  12.4 us
    ppermute x7, waiting for transfers between devices, sent(): return lax.ppermute(blocks, 'seq', [(i, i ^ mask) for i in range(own)])  3.46 us
  transfers between devices with their start and end apart: 7, of which 3 were waited for; matrix products, arithmetic and copies ran while one was open for 0% of the time, Pallas kernels for 0%

profile of v5, /device:TPU:0, one launch (start us, length us, event | category | flops | bytes accessed | tf_op | source)
XLA Modules:
  0.0 41.4 jit_solution(14803940657894160100)
XLA Ops:
  0.0 6.0 %collective-permute-start.6 = (s32[8,128]{1,0:T(8,128)}, s32[8,128]{1,0:T(8,128)S(1)}, u32[]{:S(2)}, u32[]{:S(2)}) collective-permute-start(s32[8,128]{1,0:T(8,128)} %bitcast.4), channel_id=1, source_target_pairs={{0,28},{4,24},{8,20},{12,16},{16,12},{20,8},{24,4},{28,0},{1,29},{... | collective-permute-start | bytes 12296 | tf_op jit(solution)/shard_map/ppermute | solution.py:450
  6.0 0.2 collective-permute-start.5
  6.2 0.7 %collective-permute-start.4 = (s32[8,128]{1,0:T(8,128)}, s32[8,128]{1,0:T(8,128)S(1)}, u32[]{:S(2)}, u32[]{:S(2)}) collective-permute-start(s32[8,128]{1,0:T(8,128)} %bitcast.6), channel_id=1, source_target_pairs={{0,20},{4,16},{8,28},{12,24},{16,4},{20,0},{24,12},{28,8},{1,21},{... | collective-permute-start | bytes 12296 | tf_op jit(solution)/shard_map/ppermute | solution.py:450
  7.0 2.0 %collective-permute-start.3 = (s32[8,128]{1,0:T(8,128)}, s32[8,128]{1,0:T(8,128)S(1)}, u32[]{:S(2)}, u32[]{:S(2)}) collective-permute-start(s32[8,128]{1,0:T(8,128)} %bitcast.7), channel_id=1, source_target_pairs={{0,16},{4,20},{8,24},{12,28},{16,0},{20,4},{24,8},{28,12},{1,17},{... | collective-permute-start | bytes 12296 | tf_op jit(solution)/shard_map/ppermute | solution.py:450
  8.9 2.4 %collective-permute-start.2 = (s32[8,128]{1,0:T(8,128)}, s32[8,128]{1,0:T(8,128)S(1)}, u32[]{:S(2)}, u32[]{:S(2)}) collective-permute-start(s32[8,128]{1,0:T(8,128)} %bitcast.8), channel_id=1, source_target_pairs={{0,12},{4,8},{8,4},{12,0},{16,28},{20,24},{24,20},{28,16},{1,13},{... | collective-permute-start | bytes 12296 | tf_op jit(solution)/shard_map/ppermute | solution.py:450
  11.3 0.0 collective-permute-done.6.others_7_
  11.3 0.0 copy-start
  11.3 0.8 %collective-permute-start.1 = (s32[8,128]{1,0:T(8,128)}, s32[8,128]{1,0:T(8,128)S(1)}, u32[]{:S(2)}, u32[]{:S(2)}) collective-permute-start(s32[8,128]{1,0:T(8,128)} %bitcast.9), channel_id=1, source_target_pairs={{0,8},{4,12},{8,0},{12,4},{16,24},{20,28},{24,16},{28,20},{1,9},{5... | collective-permute-start | bytes 12296 | tf_op jit(solution)/shard_map/ppermute | solution.py:450
  12.1 0.0 collective-permute-done.5.others_6_
  12.1 0.0 copy-start.1
  12.1 0.3 collective-permute-start
  12.4 0.0 collective-permute-done.4.others_5_
  12.4 0.0 copy-start.2
  12.4 0.0 collective-permute-done.3.others_4_
  12.4 0.0 copy-start.3
  12.5 1.2 %collective-permute-done.2.others_3_ = s32[8,128]{1,0:T(8,128)S(1)} collective-permute-done((s32[8,128]{1,0:T(8,128)}, s32[8,128]{1,0:T(8,128)S(1)}, u32[]{:S(2)}, u32[]{:S(2)}) %collective-permute-start.2) | collective-permute-done | bytes 4128 | tf_op jit(solution)/shard_map/ppermute | solution.py:450
  13.7 0.0 copy-start.4
  13.7 1.5 %collective-permute-done.1.others_2_ = s32[8,128]{1,0:T(8,128)S(1)} collective-permute-done((s32[8,128]{1,0:T(8,128)}, s32[8,128]{1,0:T(8,128)S(1)}, u32[]{:S(2)}, u32[]{:S(2)}) %collective-permute-start.1) | collective-permute-done | bytes 4128 | tf_op jit(solution)/shard_map/ppermute | solution.py:450
  15.1 0.0 copy-start.5
  15.1 0.8 %collective-permute-done.others_1_ = s32[8,128]{1,0:T(8,128)S(1)} collective-permute-done((s32[8,128]{1,0:T(8,128)}, s32[8,128]{1,0:T(8,128)S(1)}, u32[]{:S(2)}, u32[]{:S(2)}) %collective-permute-start) | collective-permute-done | bytes 4128 | tf_op jit(solution)/shard_map/ppermute | solution.py:450
  15.9 0.0 copy-start.6
  15.9 0.0 copy-done
  15.9 0.0 copy-done.1
  15.9 0.0 copy-done.2
  15.9 0.0 copy-done.3
  15.9 0.0 copy-done.4
  15.9 0.0 copy-done.5
  16.0 0.5 %copy-done.6 = s32[8,128]{1,0:T(8,128)} copy-done((s32[8,128]{1,0:T(8,128)}, s32[8,128]{1,0:T(8,128)S(1)}, u32[]{:S(2)}) %copy-start.6) | copy-done | bytes 4120
  16.5 24.9 %bidirectional_layer.1 = bf16[1024,256]{1,0:T(8,128)(2,1)} custom-call(s32[1]{0:T(128)} %bitcast.mine, s32[1024]{0:T(1024)} %tok_s.1, bf16[5,256]{1,0:T(8,128)(2,1)} %emb_h.1, bf16[1064,256]{1,0:T(8,128)(2,1)} %bitcast.3, f32[2,4,512]{2,1,0:T(4,128)} %cw_h.1, f32[2,8]{1,0:T(2,128)} %bias_h.1, f32[2,8]{1,0:T(2,128)} %rate_h.1, f32[2,8]{1,0:T(2,128)} %skip_h.1, ...), custom_call_target="tpu_custom_call" | custom-call | flops 8999999488 | bytes 4000000 | tf_op jit(solution)/shard_map/bidirectional_layer/pallas_call | solution.py:460
Async XLA Ops:
  0.0 11.3 %collective-permute-start.6 = (s32[8,128]{1,0:T(8,128)}, s32[8,128]{1,0:T(8,128)S(1)}, u32[]{:S(2)}, u32[]{:S(2)}) collective-permute-start(s32[8,128]{1,0:T(8,128)} %bitcast.4), channel_id=1, source_target_pairs={{0,28},{4,24},{8,20},{12,16},{16,12},{20,8},{24,4},{28,0},{1,29},{... | collective-permute-start | bytes 12296 | tf_op jit(solution)/shard_map/ppermute | solution.py:450
  6.0 6.1 %collective-permute-start.5 = (s32[8,128]{1,0:T(8,128)}, s32[8,128]{1,0:T(8,128)S(1)}, u32[]{:S(2)}, u32[]{:S(2)}) collective-permute-start(s32[8,128]{1,0:T(8,128)} %bitcast.5), channel_id=1, source_target_pairs={{0,24},{4,28},{8,16},{12,20},{16,8},{20,12},{24,0},{28,4},{1,25},{... | collective-permute-start | bytes 12296 | tf_op jit(solution)/shard_map/ppermute | solution.py:450
  6.2 6.2 %collective-permute-start.4 = (s32[8,128]{1,0:T(8,128)}, s32[8,128]{1,0:T(8,128)S(1)}, u32[]{:S(2)}, u32[]{:S(2)}) collective-permute-start(s32[8,128]{1,0:T(8,128)} %bitcast.6), channel_id=1, source_target_pairs={{0,20},{4,16},{8,28},{12,24},{16,4},{20,0},{24,12},{28,8},{1,21},{... | collective-permute-start | bytes 12296 | tf_op jit(solution)/shard_map/ppermute | solution.py:450
  7.0 5.5 %collective-permute-start.3 = (s32[8,128]{1,0:T(8,128)}, s32[8,128]{1,0:T(8,128)S(1)}, u32[]{:S(2)}, u32[]{:S(2)}) collective-permute-start(s32[8,128]{1,0:T(8,128)} %bitcast.7), channel_id=1, source_target_pairs={{0,16},{4,20},{8,24},{12,28},{16,0},{20,4},{24,8},{28,12},{1,17},{... | collective-permute-start | bytes 12296 | tf_op jit(solution)/shard_map/ppermute | solution.py:450
  8.9 4.7 %collective-permute-start.2 = (s32[8,128]{1,0:T(8,128)}, s32[8,128]{1,0:T(8,128)S(1)}, u32[]{:S(2)}, u32[]{:S(2)}) collective-permute-start(s32[8,128]{1,0:T(8,128)} %bitcast.8), channel_id=1, source_target_pairs={{0,12},{4,8},{8,4},{12,0},{16,28},{20,24},{24,20},{28,16},{1,13},{... | collective-permute-start | bytes 12296 | tf_op jit(solution)/shard_map/ppermute | solution.py:450
  11.3 4.6 %copy-start = (s32[8,128]{1,0:T(8,128)}, s32[8,128]{1,0:T(8,128)S(1)}, u32[]{:S(2)}) copy-start(s32[8,128]{1,0:T(8,128)S(1)} %collective-permute-done.6.others_7_) | copy-start | bytes 12292
  11.3 3.8 %collective-permute-start.1 = (s32[8,128]{1,0:T(8,128)}, s32[8,128]{1,0:T(8,128)S(1)}, u32[]{:S(2)}, u32[]{:S(2)}) collective-permute-start(s32[8,128]{1,0:T(8,128)} %bitcast.9), channel_id=1, source_target_pairs={{0,8},{4,12},{8,0},{12,4},{16,24},{20,28},{24,16},{28,20},{1,9},{5... | collective-permute-start | bytes 12296 | tf_op jit(solution)/shard_map/ppermute | solution.py:450
  12.1 3.8 %copy-start.1 = (s32[8,128]{1,0:T(8,128)}, s32[8,128]{1,0:T(8,128)S(1)}, u32[]{:S(2)}) copy-start(s32[8,128]{1,0:T(8,128)S(1)} %collective-permute-done.5.others_6_) | copy-start | bytes 12292
  12.1 3.8 %collective-permute-start = (s32[8,128]{1,0:T(8,128)}, s32[8,128]{1,0:T(8,128)S(1)}, u32[]{:S(2)}, u32[]{:S(2)}) collective-permute-start(s32[8,128]{1,0:T(8,128)} %bitcast.10), channel_id=1, source_target_pairs={{0,4},{4,0},{8,12},{12,8},{16,20},{20,16},{24,28},{28,24},{1,5},{5... | collective-permute-start | bytes 12296 | tf_op jit(solution)/shard_map/ppermute | solution.py:450
  12.4 3.5 %copy-start.2 = (s32[8,128]{1,0:T(8,128)}, s32[8,128]{1,0:T(8,128)S(1)}, u32[]{:S(2)}) copy-start(s32[8,128]{1,0:T(8,128)S(1)} %collective-permute-done.4.others_5_) | copy-start | bytes 12292
  12.4 3.5 %copy-start.3 = (s32[8,128]{1,0:T(8,128)}, s32[8,128]{1,0:T(8,128)S(1)}, u32[]{:S(2)}) copy-start(s32[8,128]{1,0:T(8,128)S(1)} %collective-permute-done.3.others_4_) | copy-start | bytes 12292
  13.7 2.3 %copy-start.4 = (s32[8,128]{1,0:T(8,128)}, s32[8,128]{1,0:T(8,128)S(1)}, u32[]{:S(2)}) copy-start(s32[8,128]{1,0:T(8,128)S(1)} %collective-permute-done.2.others_3_) | copy-start | bytes 12292
  15.1 0.8 %copy-start.5 = (s32[8,128]{1,0:T(8,128)}, s32[8,128]{1,0:T(8,128)S(1)}, u32[]{:S(2)}) copy-start(s32[8,128]{1,0:T(8,128)S(1)} %collective-permute-done.1.others_2_) | copy-start | bytes 12292
  15.9 0.6 %copy-start.6 = (s32[8,128]{1,0:T(8,128)}, s32[8,128]{1,0:T(8,128)S(1)}, u32[]{:S(2)}) copy-start(s32[8,128]{1,0:T(8,128)S(1)} %collective-permute-done.others_1_) | copy-start | bytes 12292

commit v6 on v5

--- a/solution.py
+++ b/solution.py
@@ -16,7 +16,7 @@
 LOG2E = 1.4426950408889634
 EPSILON = 1e-05
 CH = 128
-SUB = 16
+SUB = 32
 
 F32 = jnp.float32
 BF16 = jnp.bfloat16
@@ -208,7 +208,8 @@
     blocks, mine, tok_s, emb_h, w_in_h, cw_h, bias_h, rate_h, skip_h, gain_h, w_out_h,
     out,
     emb, w_in, cw, bias, rate, skip, gain, w_out, emb16, atab, gtab, cst, tw, zg, lac, xch, xcl,
-    tok_x, tok_f, code, tri, hist, svec, xad, xbc, yad, ybc, mix, sems,
+    tok_x, tok_f, code, tri, hist, svec, xad, xbc, yad, ybc, mix,
+    ring0, ring1, ring2, ring3, sems,
 ):
     rows = tok_x.shape[0]
     own = rows // 8
@@ -284,7 +285,12 @@
         hist[side] = hist[side] + acc
         return off + prefix[8]
 
-    lax.fori_loop(0, own - 1, block, jnp.zeros((8, CH), F32))
+    if own <= 8:
+        seen = jnp.zeros((8, CH), F32)
+        for b in range(own - 1):
+            seen = block(jnp.int32(b), seen)
+    else:
+        lax.fori_loop(0, own - 1, block, jnp.zeros((8, CH), F32))
 
     last8 = rows - 8
     mine8 = pl.ds(pl.multiple_of(j * 8, 8), 8)
@@ -344,31 +350,36 @@
 
     skips = (cst[0:8, :], cst[8:16, :])
 
-    def advance(d, src, t, state):
+    def advance(d, src, t, state, ring, slot):
         u = tok_s[t]
         x = tile_at(src, t * 8)
         a = tile_at(atab, d * 64 + u * 8)
         new = [
             a * state[w] + tile_at(gtab, (d * SYM + w) * 64 + u * 8) * x for w in range(SYM)
         ]
-        return new, (pick(new, u) + skips[d] * x) * tile_at(zg, u * 8)
+        for w in range(SYM):
+            ring[(slot * SYM + w) * 8 : (slot * SYM + w) * 8 + 8, :] = new[w]
+        return new, x, u
 
     unroll = 32
     held = 8
+    rings = ((ring0, ring1), (ring2, ring3))
 
     def group(g, carry):
         ya, yb = list(carry[:SYM]), list(carry[SYM:])
         for begin in range(0, unroll, held):
+            ra, rb = rings[(begin // held) % 2]
             done = []
-            for i in range(begin, begin + held):
-                n = g * unroll + i
+            for i in range(held):
+                n = g * unroll + begin + i
                 m = total - 1 - n
-                ya, out0 = advance(0, xad, n, ya)
-                yb, out1 = advance(1, xbc, m, yb)
-                done.append((n, m, out0, out1))
-            for n, m, out0, out1 in done:
-                yad[pl.ds(pl.multiple_of(n * 8, 8), 8), :] = out0
-                ybc[pl.ds(pl.multiple_of(m * 8, 8), 8), :] = out1
+                ya, x0, u0 = advance(0, xad, n, ya, ra, i)
+                yb, x1, u1 = advance(1, xbc, m, yb, rb, i)
+                done.append((n, m, x0, x1, u0, u1))
+            for i, (n, m, x0, x1, u0, u1) in enumerate(done):
+                for d, ring, dest, t, x, u in ((0, ra, yad, n, x0, u0), (1, rb, ybc, m, x1, u1)):
+                    y = tile_at(ring, i * SYM * 8 + u * 8) + skips[d] * x
+                    dest[pl.ds(pl.multiple_of(t * 8, 8), 8), :] = y * tile_at(zg, u * 8)
         return tuple(ya + yb)
 
     lax.fori_loop(0, total // unroll, group, tuple(starts))
@@ -377,7 +388,7 @@
     wout = w_out[...]
     wflip = nn(wout, flip).astype(BF16)
     mean = jnp.where(
-        (iota((2 * CH, 2 * CH), 0) >> 6) == (iota((2 * CH, 2 * CH), 1) >> 6), 1.0 / 64.0, 0.0
+        ((iota((4 * CH, 2 * CH), 0) & 255) >> 6) == (iota((4 * CH, 2 * CH), 1) >> 6), 1.0 / 64.0, 0.0
     ).astype(BF16)
     emb_rows = jnp.concatenate(
         [emb16[0:8, :], jnp.zeros((CH - 8, D), F32)], axis=0
@@ -402,7 +413,7 @@
         at = pl.ds(pl.multiple_of((c * CH + k * SUB) * 8, SUB * 8), SUB * 8)
         found = (yad[at, :], ybc[at, :])
         high, low = split(jnp.concatenate([g * g for g in found], axis=1))
-        scale = lax.rsqrt(nn(high, mean) + nn(low, mean) + EPSILON)
+        scale = lax.rsqrt(nn(jnp.concatenate([high, low], axis=1), mean) + EPSILON)
         normed = None
         for d in range(2):
             scaled = (found[d] * scale[:, CH * d : CH * d + CH]).reshape(SUB, 8, CH) * gains[d][None]
@@ -457,6 +468,7 @@
     mine = lax.axis_index("seq").reshape(1).astype(jnp.int32)
     table = pltpu.VMEM((4 * SYM * CH, E), BF16)
     steps = pltpu.VMEM((length * 8, CH), F32)
+    ring = pltpu.VMEM((8 * SYM * 8, CH), F32)
     return pl.pallas_call(
         functools.partial(layer_kernel, len(blocks)),
         out_shape=sds((length, D), BF16),
@@ -484,6 +496,10 @@
             steps,
             steps,
             pltpu.VMEM((2 * CH * 8, CH), F32),
+            ring,
+            ring,
+            ring,
+            ring,
             pltpu.SemaphoreType.DMA((8 + len(blocks),)),
         ],
         compiler_params=pltpu.CompilerParams(vmem_limit_bytes=56 * 1024 * 1024),

time: 41.6 us -> 39.8 us (0.957)
  Pallas kernels: 24.9 us -> 23.1 us
    pallas_call x1, Pallas kernels: 24.9 us -> 23.1 us  [per_device(): pl.pallas_call(functools.partial(layer_kernel, len(blocks)), out_shape=sd...]
where the time goes in v6:
time: 39.8 us; the launch traced here: 39.6 us
  Pallas kernels  23.1 us (58%)
  starting transfers between devices  12.4 us (31%)
  waiting for transfers between devices  3.46 us (9%)
  local copies, waits for them, and re-layouts  0.57 us (1%)
    pallas_call x1, Pallas kernels, per_device(): pl.pallas_call(functools.partial(layer_kernel, len(blocks)), out_shape=sd...  23.1 us
    ppermute x7, starting transfers between devices, sent(): return lax.ppermute(blocks, 'seq', [(i, i ^ mask) for i in range(own)])  12.4 us
    ppermute x7, waiting for transfers between devices, sent(): return lax.ppermute(blocks, 'seq', [(i, i ^ mask) for i in range(own)])  3.46 us
  transfers between devices with their start and end apart: 7, of which 3 were waited for; matrix products, arithmetic and copies ran while one was open for 0% of the time, Pallas kernels for 0%

profile of v6, /device:TPU:0, one launch (start us, length us, event | category | flops | bytes accessed | tf_op | source)
XLA Modules:
  0.0 39.6 jit_solution(4824124436168015444)
XLA Ops:
  0.0 6.0 %collective-permute-start.6 = (s32[8,128]{1,0:T(8,128)}, s32[8,128]{1,0:T(8,128)S(1)}, u32[]{:S(2)}, u32[]{:S(2)}) collective-permute-start(s32[8,128]{1,0:T(8,128)} %bitcast.4), channel_id=1, source_target_pairs={{0,28},{4,24},{8,20},{12,16},{16,12},{20,8},{24,4},{28,0},{1,29},{... | collective-permute-start | bytes 12296 | tf_op jit(solution)/shard_map/ppermute | solution.py:461
  6.0 0.2 collective-permute-start.5
  6.2 0.7 %collective-permute-start.4 = (s32[8,128]{1,0:T(8,128)}, s32[8,128]{1,0:T(8,128)S(1)}, u32[]{:S(2)}, u32[]{:S(2)}) collective-permute-start(s32[8,128]{1,0:T(8,128)} %bitcast.6), channel_id=1, source_target_pairs={{0,20},{4,16},{8,28},{12,24},{16,4},{20,0},{24,12},{28,8},{1,21},{... | collective-permute-start | bytes 12296 | tf_op jit(solution)/shard_map/ppermute | solution.py:461
  7.0 2.0 %collective-permute-start.3 = (s32[8,128]{1,0:T(8,128)}, s32[8,128]{1,0:T(8,128)S(1)}, u32[]{:S(2)}, u32[]{:S(2)}) collective-permute-start(s32[8,128]{1,0:T(8,128)} %bitcast.7), channel_id=1, source_target_pairs={{0,16},{4,20},{8,24},{12,28},{16,0},{20,4},{24,8},{28,12},{1,17},{... | collective-permute-start | bytes 12296 | tf_op jit(solution)/shard_map/ppermute | solution.py:461
  8.9 2.4 %collective-permute-start.2 = (s32[8,128]{1,0:T(8,128)}, s32[8,128]{1,0:T(8,128)S(1)}, u32[]{:S(2)}, u32[]{:S(2)}) collective-permute-start(s32[8,128]{1,0:T(8,128)} %bitcast.8), channel_id=1, source_target_pairs={{0,12},{4,8},{8,4},{12,0},{16,28},{20,24},{24,20},{28,16},{1,13},{... | collective-permute-start | bytes 12296 | tf_op jit(solution)/shard_map/ppermute | solution.py:461
  11.3 0.0 collective-permute-done.6.others_7_
  11.3 0.0 copy-start
  11.3 0.8 %collective-permute-start.1 = (s32[8,128]{1,0:T(8,128)}, s32[8,128]{1,0:T(8,128)S(1)}, u32[]{:S(2)}, u32[]{:S(2)}) collective-permute-start(s32[8,128]{1,0:T(8,128)} %bitcast.9), channel_id=1, source_target_pairs={{0,8},{4,12},{8,0},{12,4},{16,24},{20,28},{24,16},{28,20},{1,9},{5... | collective-permute-start | bytes 12296 | tf_op jit(solution)/shard_map/ppermute | solution.py:461
  12.1 0.0 collective-permute-done.5.others_6_
  12.1 0.0 copy-start.1
  12.1 0.3 collective-permute-start
  12.4 0.0 collective-permute-done.4.others_5_
  12.4 0.0 copy-start.2
  12.4 0.0 collective-permute-done.3.others_4_
  12.4 0.0 copy-start.3
  12.5 1.2 %collective-permute-done.2.others_3_ = s32[8,128]{1,0:T(8,128)S(1)} collective-permute-done((s32[8,128]{1,0:T(8,128)}, s32[8,128]{1,0:T(8,128)S(1)}, u32[]{:S(2)}, u32[]{:S(2)}) %collective-permute-start.2) | collective-permute-done | bytes 4128 | tf_op jit(solution)/shard_map/ppermute | solution.py:461
  13.7 0.0 copy-start.4
  13.7 1.5 %collective-permute-done.1.others_2_ = s32[8,128]{1,0:T(8,128)S(1)} collective-permute-done((s32[8,128]{1,0:T(8,128)}, s32[8,128]{1,0:T(8,128)S(1)}, u32[]{:S(2)}, u32[]{:S(2)}) %collective-permute-start.1) | collective-permute-done | bytes 4128 | tf_op jit(solution)/shard_map/ppermute | solution.py:461
  15.1 0.0 copy-start.5
  15.1 0.8 %collective-permute-done.others_1_ = s32[8,128]{1,0:T(8,128)S(1)} collective-permute-done((s32[8,128]{1,0:T(8,128)}, s32[8,128]{1,0:T(8,128)S(1)}, u32[]{:S(2)}, u32[]{:S(2)}) %collective-permute-start) | collective-permute-done | bytes 4128 | tf_op jit(solution)/shard_map/ppermute | solution.py:461
  15.9 0.0 copy-start.6
  15.9 0.0 copy-done
  15.9 0.0 copy-done.1
  15.9 0.0 copy-done.2
  15.9 0.0 copy-done.3
  15.9 0.0 copy-done.4
  15.9 0.0 copy-done.5
  16.0 0.5 %copy-done.6 = s32[8,128]{1,0:T(8,128)} copy-done((s32[8,128]{1,0:T(8,128)}, s32[8,128]{1,0:T(8,128)S(1)}, u32[]{:S(2)}) %copy-start.6) | copy-done | bytes 4120
  16.5 23.1 %bidirectional_layer.1 = bf16[1024,256]{1,0:T(8,128)(2,1)} custom-call(s32[1]{0:T(128)} %bitcast.mine, s32[1024]{0:T(1024)} %tok_s.1, bf16[5,256]{1,0:T(8,128)(2,1)} %emb_h.1, bf16[1064,256]{1,0:T(8,128)(2,1)} %bitcast.3, f32[2,4,512]{2,1,0:T(4,128)} %cw_h.1, f32[2,8]{1,0:T(2,128)} %bias_h.1, f32[2,8]{1,0:T(2,128)} %rate_h.1, f32[2,8]{1,0:T(2,128)} %skip_h.1, ...), custom_call_target="tpu_custom_call" | custom-call | flops 8999999488 | bytes 4000000 | tf_op jit(solution)/shard_map/bidirectional_layer/pallas_call | solution.py:472
Async XLA Ops:
  0.0 11.3 %collective-permute-start.6 = (s32[8,128]{1,0:T(8,128)}, s32[8,128]{1,0:T(8,128)S(1)}, u32[]{:S(2)}, u32[]{:S(2)}) collective-permute-start(s32[8,128]{1,0:T(8,128)} %bitcast.4), channel_id=1, source_target_pairs={{0,28},{4,24},{8,20},{12,16},{16,12},{20,8},{24,4},{28,0},{1,29},{... | collective-permute-start | bytes 12296 | tf_op jit(solution)/shard_map/ppermute | solution.py:461
  6.0 6.1 %collective-permute-start.5 = (s32[8,128]{1,0:T(8,128)}, s32[8,128]{1,0:T(8,128)S(1)}, u32[]{:S(2)}, u32[]{:S(2)}) collective-permute-start(s32[8,128]{1,0:T(8,128)} %bitcast.5), channel_id=1, source_target_pairs={{0,24},{4,28},{8,16},{12,20},{16,8},{20,12},{24,0},{28,4},{1,25},{... | collective-permute-start | bytes 12296 | tf_op jit(solution)/shard_map/ppermute | solution.py:461
  6.2 6.2 %collective-permute-start.4 = (s32[8,128]{1,0:T(8,128)}, s32[8,128]{1,0:T(8,128)S(1)}, u32[]{:S(2)}, u32[]{:S(2)}) collective-permute-start(s32[8,128]{1,0:T(8,128)} %bitcast.6), channel_id=1, source_target_pairs={{0,20},{4,16},{8,28},{12,24},{16,4},{20,0},{24,12},{28,8},{1,21},{... | collective-permute-start | bytes 12296 | tf_op jit(solution)/shard_map/ppermute | solution.py:461
  7.0 5.5 %collective-permute-start.3 = (s32[8,128]{1,0:T(8,128)}, s32[8,128]{1,0:T(8,128)S(1)}, u32[]{:S(2)}, u32[]{:S(2)}) collective-permute-start(s32[8,128]{1,0:T(8,128)} %bitcast.7), channel_id=1, source_target_pairs={{0,16},{4,20},{8,24},{12,28},{16,0},{20,4},{24,8},{28,12},{1,17},{... | collective-permute-start | bytes 12296 | tf_op jit(solution)/shard_map/ppermute | solution.py:461
  8.9 4.7 %collective-permute-start.2 = (s32[8,128]{1,0:T(8,128)}, s32[8,128]{1,0:T(8,128)S(1)}, u32[]{:S(2)}, u32[]{:S(2)}) collective-permute-start(s32[8,128]{1,0:T(8,128)} %bitcast.8), channel_id=1, source_target_pairs={{0,12},{4,8},{8,4},{12,0},{16,28},{20,24},{24,20},{28,16},{1,13},{... | collective-permute-start | bytes 12296 | tf_op jit(solution)/shard_map/ppermute | solution.py:461
  11.3 4.6 %copy-start = (s32[8,128]{1,0:T(8,128)}, s32[8,128]{1,0:T(8,128)S(1)}, u32[]{:S(2)}) copy-start(s32[8,128]{1,0:T(8,128)S(1)} %collective-permute-done.6.others_7_) | copy-start | bytes 12292
  11.3 3.8 %collective-permute-start.1 = (s32[8,128]{1,0:T(8,128)}, s32[8,128]{1,0:T(8,128)S(1)}, u32[]{:S(2)}, u32[]{:S(2)}) collective-permute-start(s32[8,128]{1,0:T(8,128)} %bitcast.9), channel_id=1, source_target_pairs={{0,8},{4,12},{8,0},{12,4},{16,24},{20,28},{24,16},{28,20},{1,9},{5... | collective-permute-start | bytes 12296 | tf_op jit(solution)/shard_map/ppermute | solution.py:461
  12.1 3.8 %copy-start.1 = (s32[8,128]{1,0:T(8,128)}, s32[8,128]{1,0:T(8,128)S(1)}, u32[]{:S(2)}) copy-start(s32[8,128]{1,0:T(8,128)S(1)} %collective-permute-done.5.others_6_) | copy-start | bytes 12292
  12.1 3.8 %collective-permute-start = (s32[8,128]{1,0:T(8,128)}, s32[8,128]{1,0:T(8,128)S(1)}, u32[]{:S(2)}, u32[]{:S(2)}) collective-permute-start(s32[8,128]{1,0:T(8,128)} %bitcast.10), channel_id=1, source_target_pairs={{0,4},{4,0},{8,12},{12,8},{16,20},{20,16},{24,28},{28,24},{1,5},{5... | collective-permute-start | bytes 12296 | tf_op jit(solution)/shard_map/ppermute | solution.py:461
  12.4 3.5 %copy-start.2 = (s32[8,128]{1,0:T(8,128)}, s32[8,128]{1,0:T(8,128)S(1)}, u32[]{:S(2)}) copy-start(s32[8,128]{1,0:T(8,128)S(1)} %collective-permute-done.4.others_5_) | copy-start | bytes 12292
  12.4 3.5 %copy-start.3 = (s32[8,128]{1,0:T(8,128)}, s32[8,128]{1,0:T(8,128)S(1)}, u32[]{:S(2)}) copy-start(s32[8,128]{1,0:T(8,128)S(1)} %collective-permute-done.3.others_4_) | copy-start | bytes 12292
  13.7 2.3 %copy-start.4 = (s32[8,128]{1,0:T(8,128)}, s32[8,128]{1,0:T(8,128)S(1)}, u32[]{:S(2)}) copy-start(s32[8,128]{1,0:T(8,128)S(1)} %collective-permute-done.2.others_3_) | copy-start | bytes 12292
  15.1 0.8 %copy-start.5 = (s32[8,128]{1,0:T(8,128)}, s32[8,128]{1,0:T(8,128)S(1)}, u32[]{:S(2)}) copy-start(s32[8,128]{1,0:T(8,128)S(1)} %collective-permute-done.1.others_2_) | copy-start | bytes 12292
  15.9 0.6 %copy-start.6 = (s32[8,128]{1,0:T(8,128)}, s32[8,128]{1,0:T(8,128)S(1)}, u32[]{:S(2)}) copy-start(s32[8,128]{1,0:T(8,128)S(1)} %collective-permute-done.others_1_) | copy-start | bytes 12292

commit v7 on v6

--- a/solution.py
+++ b/solution.py
@@ -90,14 +90,13 @@
     return ref[pl.ds(pl.multiple_of(row, 8), 8), :]
 
 
-def fetch(sources, targets, sems):
+def begin(sources, targets, sems):
     copies = [
         pltpu.make_async_copy(a, b, sems.at[i]) for i, (a, b) in enumerate(zip(sources, targets))
     ]
     for copy in copies:
         copy.start()
-    for copy in copies:
-        copy.wait()
+    return copies
 
 
 def symbol_tables(
@@ -217,13 +216,12 @@
     nchunk = total // CH
     j = mine[0]
     size = rows // len(blocks)
-    fetch((emb_h, w_in_h, cw_h, bias_h, rate_h, skip_h, gain_h, w_out_h, *blocks),
-          (emb, w_in, cw, bias, rate, skip, gain, w_out,
-           *[tok_x.at[size * m : size * m + size, :] for m in range(len(blocks))]), sems)
-    symbol_tables(
-        (0, 1), (zg, lac, xch, xcl),
-        emb, w_in, cw, bias, rate, skip, gain, emb16, atab, gtab, cst, tw,
-    )
+    arriving = begin(
+        (*blocks, emb_h, w_in_h, cw_h, bias_h, rate_h, skip_h, gain_h, w_out_h),
+        (*[tok_x.at[size * m : size * m + size, :] for m in range(len(blocks))],
+         emb, w_in, cw, bias, rate, skip, gain, w_out), sems)
+    for copy in arriving[: len(blocks)]:
+        copy.wait()
     for b in range(own):
         slot = (j ^ b) * 8
         tok_f[3, 8 * b : 8 * b + 8, :] = tok_x[pl.ds(pl.multiple_of(slot, 8), 8), :].astype(F32)
@@ -245,6 +243,13 @@
     hist[...] = jnp.zeros_like(hist)
     sub8 = iota((8, CH), 0).astype(F32)
     subc = iota((CH, CH), 0).astype(F32)
+
+    for copy in arriving[len(blocks) :]:
+        copy.wait()
+    symbol_tables(
+        (0, 1), (zg, lac, xch, xcl),
+        emb, w_in, cw, bias, rate, skip, gain, emb16, atab, gtab, cst, tw,
+    )
 
     def block(b, off):
         side = jnp.where(b >= j, 1, 0)
@@ -285,15 +290,31 @@
         hist[side] = hist[side] + acc
         return off + prefix[8]
 
+    mine8 = pl.ds(pl.multiple_of(j * 8, 8), 8)
+    shifts = [tok_f[o, mine8, :] for o in range(7)]
+
+    def convolve(c):
+        hot = window_onehot([sh[c : c + 1, :] for sh in shifts])
+        for q, (d, s, k) in enumerate(CHAINS):
+            x = silu_half(nn(hot, tw[q]))
+            ref = (xad, xbc)[d]
+            for i in range(4):
+                ref[pl.ds(c * 8 * CH + s * 4 + i, CH, stride=8), :] = x[:, 128 * i : 128 * i + 128]
+
     if own <= 8:
         seen = jnp.zeros((8, CH), F32)
         for b in range(own - 1):
             seen = block(jnp.int32(b), seen)
+            if b < nchunk:
+                convolve(b)
+        for c in range(own - 1, nchunk):
+            convolve(c)
     else:
         lax.fori_loop(0, own - 1, block, jnp.zeros((8, CH), F32))
+        for c in range(nchunk):
+            convolve(c)
 
     last8 = rows - 8
-    mine8 = pl.ds(pl.multiple_of(j * 8, 8), 8)
     xs = {}
     for d in range(2):
         edge = 0 if d == 0 else 7
@@ -339,15 +360,6 @@
                 value = value + gtab[at : at + 8, :] * svec[sat : sat + 8, :]
             starts.append(value)
 
-    shifts = [tok_f[o, mine8, :] for o in range(7)]
-    for c in range(nchunk):
-        hot = window_onehot([sh[c : c + 1, :] for sh in shifts])
-        for q, (d, s, k) in enumerate(CHAINS):
-            x = silu_half(nn(hot, tw[q]))
-            ref = (xad, xbc)[d]
-            for i in range(4):
-                ref[pl.ds(c * 8 * CH + s * 4 + i, CH, stride=8), :] = x[:, 128 * i : 128 * i + 128]
-
     skips = (cst[0:8, :], cst[8:16, :])
 
     def advance(d, src, t, state, ring, slot):
@@ -361,7 +373,7 @@
             ring[(slot * SYM + w) * 8 : (slot * SYM + w) * 8 + 8, :] = new[w]
         return new, x, u
 
-    unroll = 32
+    unroll = 128
     held = 8
     rings = ((ring0, ring1), (ring2, ring3))
 

time: 39.8 us -> 39.4 us (0.990)
  Pallas kernels: 23.1 us -> 22.6 us
    pallas_call x1, Pallas kernels: 23.1 us -> 22.6 us  [per_device(): pl.pallas_call(functools.partial(layer_kernel, len(blocks)), out_shape=sd...]
where the time goes in v7:
time: 39.4 us; the launch traced here: 39.1 us
  Pallas kernels  22.6 us (57%)
  starting transfers between devices  12.4 us (31%)
  waiting for transfers between devices  3.46 us (9%)
  local copies, waits for them, and re-layouts  0.57 us (1%)
    pallas_call x1, Pallas kernels, per_device(): pl.pallas_call(functools.partial(layer_kernel, len(blocks)), out_shape=sd...  22.6 us
    ppermute x7, starting transfers between devices, sent(): return lax.ppermute(blocks, 'seq', [(i, i ^ mask) for i in range(own)])  12.4 us
    ppermute x7, waiting for transfers between devices, sent(): return lax.ppermute(blocks, 'seq', [(i, i ^ mask) for i in range(own)])  3.46 us
  transfers between devices with their start and end apart: 7, of which 3 were waited for; matrix products, arithmetic and copies ran while one was open for 0% of the time, Pallas kernels for 0%

profile of v7, /device:TPU:0, one launch (start us, length us, event | category | flops | bytes accessed | tf_op | source)
XLA Modules:
  0.0 39.1 jit_solution(2484916692270582644)
XLA Ops:
  0.0 6.0 %collective-permute-start.6 = (s32[8,128]{1,0:T(8,128)}, s32[8,128]{1,0:T(8,128)S(1)}, u32[]{:S(2)}, u32[]{:S(2)}) collective-permute-start(s32[8,128]{1,0:T(8,128)} %bitcast.4), channel_id=1, source_target_pairs={{0,28},{4,24},{8,20},{12,16},{16,12},{20,8},{24,4},{28,0},{1,29},{... | collective-permute-start | bytes 12296 | tf_op jit(solution)/shard_map/ppermute | solution.py:473
  6.0 0.2 collective-permute-start.5
  6.2 0.7 %collective-permute-start.4 = (s32[8,128]{1,0:T(8,128)}, s32[8,128]{1,0:T(8,128)S(1)}, u32[]{:S(2)}, u32[]{:S(2)}) collective-permute-start(s32[8,128]{1,0:T(8,128)} %bitcast.6), channel_id=1, source_target_pairs={{0,20},{4,16},{8,28},{12,24},{16,4},{20,0},{24,12},{28,8},{1,21},{... | collective-permute-start | bytes 12296 | tf_op jit(solution)/shard_map/ppermute | solution.py:473
  7.0 2.0 %collective-permute-start.3 = (s32[8,128]{1,0:T(8,128)}, s32[8,128]{1,0:T(8,128)S(1)}, u32[]{:S(2)}, u32[]{:S(2)}) collective-permute-start(s32[8,128]{1,0:T(8,128)} %bitcast.7), channel_id=1, source_target_pairs={{0,16},{4,20},{8,24},{12,28},{16,0},{20,4},{24,8},{28,12},{1,17},{... | collective-permute-start | bytes 12296 | tf_op jit(solution)/shard_map/ppermute | solution.py:473
  8.9 2.4 %collective-permute-start.2 = (s32[8,128]{1,0:T(8,128)}, s32[8,128]{1,0:T(8,128)S(1)}, u32[]{:S(2)}, u32[]{:S(2)}) collective-permute-start(s32[8,128]{1,0:T(8,128)} %bitcast.8), channel_id=1, source_target_pairs={{0,12},{4,8},{8,4},{12,0},{16,28},{20,24},{24,20},{28,16},{1,13},{... | collective-permute-start | bytes 12296 | tf_op jit(solution)/shard_map/ppermute | solution.py:473
  11.3 0.0 collective-permute-done.6.others_7_
  11.3 0.0 copy-start
  11.3 0.8 %collective-permute-start.1 = (s32[8,128]{1,0:T(8,128)}, s32[8,128]{1,0:T(8,128)S(1)}, u32[]{:S(2)}, u32[]{:S(2)}) collective-permute-start(s32[8,128]{1,0:T(8,128)} %bitcast.9), channel_id=1, source_target_pairs={{0,8},{4,12},{8,0},{12,4},{16,24},{20,28},{24,16},{28,20},{1,9},{5... | collective-permute-start | bytes 12296 | tf_op jit(solution)/shard_map/ppermute | solution.py:473
  12.1 0.0 collective-permute-done.5.others_6_
  12.1 0.0 copy-start.1
  12.1 0.3 collective-permute-start
  12.4 0.0 collective-permute-done.4.others_5_
  12.4 0.0 copy-start.2
  12.4 0.0 collective-permute-done.3.others_4_
  12.4 0.0 copy-start.3
  12.5 1.2 %collective-permute-done.2.others_3_ = s32[8,128]{1,0:T(8,128)S(1)} collective-permute-done((s32[8,128]{1,0:T(8,128)}, s32[8,128]{1,0:T(8,128)S(1)}, u32[]{:S(2)}, u32[]{:S(2)}) %collective-permute-start.2) | collective-permute-done | bytes 4128 | tf_op jit(solution)/shard_map/ppermute | solution.py:473
  13.7 0.0 copy-start.4
  13.7 1.5 %collective-permute-done.1.others_2_ = s32[8,128]{1,0:T(8,128)S(1)} collective-permute-done((s32[8,128]{1,0:T(8,128)}, s32[8,128]{1,0:T(8,128)S(1)}, u32[]{:S(2)}, u32[]{:S(2)}) %collective-permute-start.1) | collective-permute-done | bytes 4128 | tf_op jit(solution)/shard_map/ppermute | solution.py:473
  15.1 0.0 copy-start.5
  15.1 0.8 %collective-permute-done.others_1_ = s32[8,128]{1,0:T(8,128)S(1)} collective-permute-done((s32[8,128]{1,0:T(8,128)}, s32[8,128]{1,0:T(8,128)S(1)}, u32[]{:S(2)}, u32[]{:S(2)}) %collective-permute-start) | collective-permute-done | bytes 4128 | tf_op jit(solution)/shard_map/ppermute | solution.py:473
  15.9 0.0 copy-start.6
  15.9 0.0 copy-done
  15.9 0.0 copy-done.1
  15.9 0.0 copy-done.2
  15.9 0.0 copy-done.3
  15.9 0.0 copy-done.4
  15.9 0.0 copy-done.5
  16.0 0.5 %copy-done.6 = s32[8,128]{1,0:T(8,128)} copy-done((s32[8,128]{1,0:T(8,128)}, s32[8,128]{1,0:T(8,128)S(1)}, u32[]{:S(2)}) %copy-start.6) | copy-done | bytes 4120
  16.5 22.6 %bidirectional_layer.1 = bf16[1024,256]{1,0:T(8,128)(2,1)} custom-call(s32[1]{0:T(128)} %bitcast.mine, s32[1024]{0:T(1024)} %tok_s.1, bf16[5,256]{1,0:T(8,128)(2,1)} %emb_h.1, bf16[1064,256]{1,0:T(8,128)(2,1)} %bitcast.3, f32[2,4,512]{2,1,0:T(4,128)} %cw_h.1, f32[2,8]{1,0:T(2,128)} %bias_h.1, f32[2,8]{1,0:T(2,128)} %rate_h.1, f32[2,8]{1,0:T(2,128)} %skip_h.1, ...), custom_call_target="tpu_custom_call" | custom-call | flops 8999999488 | bytes 4000000 | tf_op jit(solution)/shard_map/bidirectional_layer/pallas_call | solution.py:484
Async XLA Ops:
  0.0 11.3 %collective-permute-start.6 = (s32[8,128]{1,0:T(8,128)}, s32[8,128]{1,0:T(8,128)S(1)}, u32[]{:S(2)}, u32[]{:S(2)}) collective-permute-start(s32[8,128]{1,0:T(8,128)} %bitcast.4), channel_id=1, source_target_pairs={{0,28},{4,24},{8,20},{12,16},{16,12},{20,8},{24,4},{28,0},{1,29},{... | collective-permute-start | bytes 12296 | tf_op jit(solution)/shard_map/ppermute | solution.py:473
  6.0 6.1 %collective-permute-start.5 = (s32[8,128]{1,0:T(8,128)}, s32[8,128]{1,0:T(8,128)S(1)}, u32[]{:S(2)}, u32[]{:S(2)}) collective-permute-start(s32[8,128]{1,0:T(8,128)} %bitcast.5), channel_id=1, source_target_pairs={{0,24},{4,28},{8,16},{12,20},{16,8},{20,12},{24,0},{28,4},{1,25},{... | collective-permute-start | bytes 12296 | tf_op jit(solution)/shard_map/ppermute | solution.py:473
  6.2 6.2 %collective-permute-start.4 = (s32[8,128]{1,0:T(8,128)}, s32[8,128]{1,0:T(8,128)S(1)}, u32[]{:S(2)}, u32[]{:S(2)}) collective-permute-start(s32[8,128]{1,0:T(8,128)} %bitcast.6), channel_id=1, source_target_pairs={{0,20},{4,16},{8,28},{12,24},{16,4},{20,0},{24,12},{28,8},{1,21},{... | collective-permute-start | bytes 12296 | tf_op jit(solution)/shard_map/ppermute | solution.py:473
  7.0 5.5 %collective-permute-start.3 = (s32[8,128]{1,0:T(8,128)}, s32[8,128]{1,0:T(8,128)S(1)}, u32[]{:S(2)}, u32[]{:S(2)}) collective-permute-start(s32[8,128]{1,0:T(8,128)} %bitcast.7), channel_id=1, source_target_pairs={{0,16},{4,20},{8,24},{12,28},{16,0},{20,4},{24,8},{28,12},{1,17},{... | collective-permute-start | bytes 12296 | tf_op jit(solution)/shard_map/ppermute | solution.py:473
  8.9 4.7 %collective-permute-start.2 = (s32[8,128]{1,0:T(8,128)}, s32[8,128]{1,0:T(8,128)S(1)}, u32[]{:S(2)}, u32[]{:S(2)}) collective-permute-start(s32[8,128]{1,0:T(8,128)} %bitcast.8), channel_id=1, source_target_pairs={{0,12},{4,8},{8,4},{12,0},{16,28},{20,24},{24,20},{28,16},{1,13},{... | collective-permute-start | bytes 12296 | tf_op jit(solution)/shard_map/ppermute | solution.py:473
  11.3 4.6 %copy-start = (s32[8,128]{1,0:T(8,128)}, s32[8,128]{1,0:T(8,128)S(1)}, u32[]{:S(2)}) copy-start(s32[8,128]{1,0:T(8,128)S(1)} %collective-permute-done.6.others_7_) | copy-start | bytes 12292
  11.3 3.8 %collective-permute-start.1 = (s32[8,128]{1,0:T(8,128)}, s32[8,128]{1,0:T(8,128)S(1)}, u32[]{:S(2)}, u32[]{:S(2)}) collective-permute-start(s32[8,128]{1,0:T(8,128)} %bitcast.9), channel_id=1, source_target_pairs={{0,8},{4,12},{8,0},{12,4},{16,24},{20,28},{24,16},{28,20},{1,9},{5... | collective-permute-start | bytes 12296 | tf_op jit(solution)/shard_map/ppermute | solution.py:473
  12.1 3.8 %copy-start.1 = (s32[8,128]{1,0:T(8,128)}, s32[8,128]{1,0:T(8,128)S(1)}, u32[]{:S(2)}) copy-start(s32[8,128]{1,0:T(8,128)S(1)} %collective-permute-done.5.others_6_) | copy-start | bytes 12292
  12.1 3.8 %collective-permute-start = (s32[8,128]{1,0:T(8,128)}, s32[8,128]{1,0:T(8,128)S(1)}, u32[]{:S(2)}, u32[]{:S(2)}) collective-permute-start(s32[8,128]{1,0:T(8,128)} %bitcast.10), channel_id=1, source_target_pairs={{0,4},{4,0},{8,12},{12,8},{16,20},{20,16},{24,28},{28,24},{1,5},{5... | collective-permute-start | bytes 12296 | tf_op jit(solution)/shard_map/ppermute | solution.py:473
  12.4 3.5 %copy-start.2 = (s32[8,128]{1,0:T(8,128)}, s32[8,128]{1,0:T(8,128)S(1)}, u32[]{:S(2)}) copy-start(s32[8,128]{1,0:T(8,128)S(1)} %collective-permute-done.4.others_5_) | copy-start | bytes 12292
  12.4 3.5 %copy-start.3 = (s32[8,128]{1,0:T(8,128)}, s32[8,128]{1,0:T(8,128)S(1)}, u32[]{:S(2)}) copy-start(s32[8,128]{1,0:T(8,128)S(1)} %collective-permute-done.3.others_4_) | copy-start | bytes 12292
  13.7 2.3 %copy-start.4 = (s32[8,128]{1,0:T(8,128)}, s32[8,128]{1,0:T(8,128)S(1)}, u32[]{:S(2)}) copy-start(s32[8,128]{1,0:T(8,128)S(1)} %collective-permute-done.2.others_3_) | copy-start | bytes 12292
  15.1 0.8 %copy-start.5 = (s32[8,128]{1,0:T(8,128)}, s32[8,128]{1,0:T(8,128)S(1)}, u32[]{:S(2)}) copy-start(s32[8,128]{1,0:T(8,128)S(1)} %collective-permute-done.1.others_2_) | copy-start | bytes 12292
  15.9 0.6 %copy-start.6 = (s32[8,128]{1,0:T(8,128)}, s32[8,128]{1,0:T(8,128)S(1)}, u32[]{:S(2)}) copy-start(s32[8,128]{1,0:T(8,128)S(1)} %collective-permute-done.others_1_) | copy-start | bytes 12292

commit v8 on v7

--- a/solution.py
+++ b/solution.py
@@ -208,7 +208,7 @@
     out,
     emb, w_in, cw, bias, rate, skip, gain, w_out, emb16, atab, gtab, cst, tw, zg, lac, xch, xcl,
     tok_x, tok_f, code, tri, hist, svec, xad, xbc, yad, ybc, mix,
-    ring0, ring1, ring2, ring3, sems,
+    tab, ring0, ring1, ring2, ring3, sems,
 ):
     rows = tok_x.shape[0]
     own = rows // 8
@@ -362,37 +362,47 @@
 
     skips = (cst[0:8, :], cst[8:16, :])
 
-    def advance(d, src, t, state, ring, slot):
-        u = tok_s[t]
-        x = tile_at(src, t * 8)
-        a = tile_at(atab, d * 64 + u * 8)
-        new = [
-            a * state[w] + tile_at(gtab, (d * SYM + w) * 64 + u * 8) * x for w in range(SYM)
-        ]
-        for w in range(SYM):
-            ring[(slot * SYM + w) * 8 : (slot * SYM + w) * 8 + 8, :] = new[w]
-        return new, x, u
+    for d in range(2):
+        for u in range(SYM):
+            at = (d * SYM + u) * 64
+            tab[at : at + 8, :] = atab[d * 64 + u * 8 : d * 64 + u * 8 + 8, :]
+            for w in range(SYM):
+                row = (d * SYM + w) * 64 + u * 8
+                tab[at + 8 + w * 8 : at + 16 + w * 8, :] = gtab[row : row + 8, :]
+            tab[at + 48 : at + 56, :] = zg[u * 8 : u * 8 + 8, :]
+
+    def rows8(ref, k):
+        return ref[k * 8 : k * 8 + 8, :]
 
     unroll = 128
     held = 8
     rings = ((ring0, ring1), (ring2, ring3))
 
     def group(g, carry):
-        ya, yb = list(carry[:SYM]), list(carry[SYM:])
+        states = [list(carry[:SYM]), list(carry[SYM:])]
+        firsts = (g * unroll, total - (g + 1) * unroll)
+        spans = [pl.ds(pl.multiple_of(f * 8, unroll * 8), unroll * 8) for f in firsts]
+        sources = (xad.at[spans[0], :], xbc.at[spans[1], :])
+        targets = (yad.at[spans[0], :], ybc.at[spans[1], :])
         for begin in range(0, unroll, held):
-            ra, rb = rings[(begin // held) % 2]
+            pair = rings[(begin // held) % 2]
             done = []
             for i in range(held):
-                n = g * unroll + begin + i
-                m = total - 1 - n
-                ya, x0, u0 = advance(0, xad, n, ya, ra, i)
-                yb, x1, u1 = advance(1, xbc, m, yb, rb, i)
-                done.append((n, m, x0, x1, u0, u1))
-            for i, (n, m, x0, x1, u0, u1) in enumerate(done):
-                for d, ring, dest, t, x, u in ((0, ra, yad, n, x0, u0), (1, rb, ybc, m, x1, u1)):
-                    y = tile_at(ring, i * SYM * 8 + u * 8) + skips[d] * x
-                    dest[pl.ds(pl.multiple_of(t * 8, 8), 8), :] = y * tile_at(zg, u * 8)
-        return tuple(ya + yb)
+                for d in range(2):
+                    n = begin + i
+                    local = n if d == 0 else unroll - 1 - n
+                    u = tok_s[firsts[d] + local]
+                    part = tab.at[pl.ds(pl.multiple_of((d * SYM + u) * 64, 64), 64), :]
+                    x = rows8(sources[d], local)
+                    a = rows8(part, 0)
+                    states[d] = [a * states[d][w] + rows8(part, 1 + w) * x for w in range(SYM)]
+                    for w in range(SYM):
+                        pair[d][(i * SYM + w) * 8 : (i * SYM + w) * 8 + 8, :] = states[d][w]
+                    done.append((d, i, local, x, u, part))
+            for d, i, local, x, u, part in done:
+                y = tile_at(pair[d], i * SYM * 8 + u * 8) + skips[d] * x
+                targets[d][local * 8 : local * 8 + 8, :] = y * rows8(part, 6)
+        return tuple(states[0] + states[1])
 
     lax.fori_loop(0, total // unroll, group, tuple(starts))
 
@@ -508,6 +518,7 @@
             steps,
             steps,
             pltpu.VMEM((2 * CH * 8, CH), F32),
+            pltpu.VMEM((2 * SYM * 64, CH), F32),
             ring,
             ring,
             ring,

time: 39.4 us -> 36.6 us (0.929)
  Pallas kernels: 22.6 us -> 19.9 us
    pallas_call x1, Pallas kernels: 22.6 us -> 19.9 us  [per_device(): pl.pallas_call(functools.partial(layer_kernel, len(blocks)), out_shape=sd...]
where the time goes in v8:
time: 36.6 us; the launch traced here: 36.4 us
  Pallas kernels  19.9 us (54%)
  starting transfers between devices  12.4 us (34%)
  waiting for transfers between devices  3.46 us (9%)
  local copies, waits for them, and re-layouts  0.57 us (2%)
    pallas_call x1, Pallas kernels, per_device(): pl.pallas_call(functools.partial(layer_kernel, len(blocks)), out_shape=sd...  19.9 us
    ppermute x7, starting transfers between devices, sent(): return lax.ppermute(blocks, 'seq', [(i, i ^ mask) for i in range(own)])  12.4 us
    ppermute x7, waiting for transfers between devices, sent(): return lax.ppermute(blocks, 'seq', [(i, i ^ mask) for i in range(own)])  3.46 us
  transfers between devices with their start and end apart: 7, of which 3 were waited for; matrix products, arithmetic and copies ran while one was open for 0% of the time, Pallas kernels for 0%

profile of v8, /device:TPU:0, one launch (start us, length us, event | category | flops | bytes accessed | tf_op | source)
XLA Modules:
  0.0 36.4 jit_solution(13529762948798796330)
XLA Ops:
  0.0 6.0 %collective-permute-start.6 = (s32[8,128]{1,0:T(8,128)}, s32[8,128]{1,0:T(8,128)S(1)}, u32[]{:S(2)}, u32[]{:S(2)}) collective-permute-start(s32[8,128]{1,0:T(8,128)} %bitcast.4), channel_id=1, source_target_pairs={{0,28},{4,24},{8,20},{12,16},{16,12},{20,8},{24,4},{28,0},{1,29},{... | collective-permute-start | bytes 12296 | tf_op jit(solution)/shard_map/ppermute | solution.py:483
  6.0 0.2 collective-permute-start.5
  6.2 0.7 %collective-permute-start.4 = (s32[8,128]{1,0:T(8,128)}, s32[8,128]{1,0:T(8,128)S(1)}, u32[]{:S(2)}, u32[]{:S(2)}) collective-permute-start(s32[8,128]{1,0:T(8,128)} %bitcast.6), channel_id=1, source_target_pairs={{0,20},{4,16},{8,28},{12,24},{16,4},{20,0},{24,12},{28,8},{1,21},{... | collective-permute-start | bytes 12296 | tf_op jit(solution)/shard_map/ppermute | solution.py:483
  7.0 2.0 %collective-permute-start.3 = (s32[8,128]{1,0:T(8,128)}, s32[8,128]{1,0:T(8,128)S(1)}, u32[]{:S(2)}, u32[]{:S(2)}) collective-permute-start(s32[8,128]{1,0:T(8,128)} %bitcast.7), channel_id=1, source_target_pairs={{0,16},{4,20},{8,24},{12,28},{16,0},{20,4},{24,8},{28,12},{1,17},{... | collective-permute-start | bytes 12296 | tf_op jit(solution)/shard_map/ppermute | solution.py:483
  8.9 2.4 %collective-permute-start.2 = (s32[8,128]{1,0:T(8,128)}, s32[8,128]{1,0:T(8,128)S(1)}, u32[]{:S(2)}, u32[]{:S(2)}) collective-permute-start(s32[8,128]{1,0:T(8,128)} %bitcast.8), channel_id=1, source_target_pairs={{0,12},{4,8},{8,4},{12,0},{16,28},{20,24},{24,20},{28,16},{1,13},{... | collective-permute-start | bytes 12296 | tf_op jit(solution)/shard_map/ppermute | solution.py:483
  11.3 0.0 collective-permute-done.6.others_7_
  11.3 0.0 copy-start
  11.3 0.8 %collective-permute-start.1 = (s32[8,128]{1,0:T(8,128)}, s32[8,128]{1,0:T(8,128)S(1)}, u32[]{:S(2)}, u32[]{:S(2)}) collective-permute-start(s32[8,128]{1,0:T(8,128)} %bitcast.9), channel_id=1, source_target_pairs={{0,8},{4,12},{8,0},{12,4},{16,24},{20,28},{24,16},{28,20},{1,9},{5... | collective-permute-start | bytes 12296 | tf_op jit(solution)/shard_map/ppermute | solution.py:483
  12.1 0.0 collective-permute-done.5.others_6_
  12.1 0.0 copy-start.1
  12.1 0.3 collective-permute-start
  12.4 0.0 collective-permute-done.4.others_5_
  12.4 0.0 copy-start.2
  12.4 0.0 collective-permute-done.3.others_4_
  12.4 0.0 copy-start.3
  12.5 1.2 %collective-permute-done.2.others_3_ = s32[8,128]{1,0:T(8,128)S(1)} collective-permute-done((s32[8,128]{1,0:T(8,128)}, s32[8,128]{1,0:T(8,128)S(1)}, u32[]{:S(2)}, u32[]{:S(2)}) %collective-permute-start.2) | collective-permute-done | bytes 4128 | tf_op jit(solution)/shard_map/ppermute | solution.py:483
  13.7 0.0 copy-start.4
  13.7 1.5 %collective-permute-done.1.others_2_ = s32[8,128]{1,0:T(8,128)S(1)} collective-permute-done((s32[8,128]{1,0:T(8,128)}, s32[8,128]{1,0:T(8,128)S(1)}, u32[]{:S(2)}, u32[]{:S(2)}) %collective-permute-start.1) | collective-permute-done | bytes 4128 | tf_op jit(solution)/shard_map/ppermute | solution.py:483
  15.1 0.0 copy-start.5
  15.1 0.8 %collective-permute-done.others_1_ = s32[8,128]{1,0:T(8,128)S(1)} collective-permute-done((s32[8,128]{1,0:T(8,128)}, s32[8,128]{1,0:T(8,128)S(1)}, u32[]{:S(2)}, u32[]{:S(2)}) %collective-permute-start) | collective-permute-done | bytes 4128 | tf_op jit(solution)/shard_map/ppermute | solution.py:483
  15.9 0.0 copy-start.6
  15.9 0.0 copy-done
  15.9 0.0 copy-done.1
  15.9 0.0 copy-done.2
  15.9 0.0 copy-done.3
  15.9 0.0 copy-done.4
  15.9 0.0 copy-done.5
  16.0 0.5 %copy-done.6 = s32[8,128]{1,0:T(8,128)} copy-done((s32[8,128]{1,0:T(8,128)}, s32[8,128]{1,0:T(8,128)S(1)}, u32[]{:S(2)}) %copy-start.6) | copy-done | bytes 4120
  16.5 19.9 %bidirectional_layer.1 = bf16[1024,256]{1,0:T(8,128)(2,1)} custom-call(s32[1]{0:T(128)} %bitcast.mine, s32[1024]{0:T(1024)} %tok_s.1, bf16[5,256]{1,0:T(8,128)(2,1)} %emb_h.1, bf16[1064,256]{1,0:T(8,128)(2,1)} %bitcast.3, f32[2,4,512]{2,1,0:T(4,128)} %cw_h.1, f32[2,8]{1,0:T(2,128)} %bias_h.1, f32[2,8]{1,0:T(2,128)} %rate_h.1, f32[2,8]{1,0:T(2,128)} %skip_h.1, ...), custom_call_target="tpu_custom_call" | custom-call | flops 8999999488 | bytes 4000000 | tf_op jit(solution)/shard_map/bidirectional_layer/pallas_call | solution.py:494
Async XLA Ops:
  0.0 11.3 %collective-permute-start.6 = (s32[8,128]{1,0:T(8,128)}, s32[8,128]{1,0:T(8,128)S(1)}, u32[]{:S(2)}, u32[]{:S(2)}) collective-permute-start(s32[8,128]{1,0:T(8,128)} %bitcast.4), channel_id=1, source_target_pairs={{0,28},{4,24},{8,20},{12,16},{16,12},{20,8},{24,4},{28,0},{1,29},{... | collective-permute-start | bytes 12296 | tf_op jit(solution)/shard_map/ppermute | solution.py:483
  6.0 6.1 %collective-permute-start.5 = (s32[8,128]{1,0:T(8,128)}, s32[8,128]{1,0:T(8,128)S(1)}, u32[]{:S(2)}, u32[]{:S(2)}) collective-permute-start(s32[8,128]{1,0:T(8,128)} %bitcast.5), channel_id=1, source_target_pairs={{0,24},{4,28},{8,16},{12,20},{16,8},{20,12},{24,0},{28,4},{1,25},{... | collective-permute-start | bytes 12296 | tf_op jit(solution)/shard_map/ppermute | solution.py:483
  6.2 6.2 %collective-permute-start.4 = (s32[8,128]{1,0:T(8,128)}, s32[8,128]{1,0:T(8,128)S(1)}, u32[]{:S(2)}, u32[]{:S(2)}) collective-permute-start(s32[8,128]{1,0:T(8,128)} %bitcast.6), channel_id=1, source_target_pairs={{0,20},{4,16},{8,28},{12,24},{16,4},{20,0},{24,12},{28,8},{1,21},{... | collective-permute-start | bytes 12296 | tf_op jit(solution)/shard_map/ppermute | solution.py:483
  7.0 5.5 %collective-permute-start.3 = (s32[8,128]{1,0:T(8,128)}, s32[8,128]{1,0:T(8,128)S(1)}, u32[]{:S(2)}, u32[]{:S(2)}) collective-permute-start(s32[8,128]{1,0:T(8,128)} %bitcast.7), channel_id=1, source_target_pairs={{0,16},{4,20},{8,24},{12,28},{16,0},{20,4},{24,8},{28,12},{1,17},{... | collective-permute-start | bytes 12296 | tf_op jit(solution)/shard_map/ppermute | solution.py:483
  8.9 4.7 %collective-permute-start.2 = (s32[8,128]{1,0:T(8,128)}, s32[8,128]{1,0:T(8,128)S(1)}, u32[]{:S(2)}, u32[]{:S(2)}) collective-permute-start(s32[8,128]{1,0:T(8,128)} %bitcast.8), channel_id=1, source_target_pairs={{0,12},{4,8},{8,4},{12,0},{16,28},{20,24},{24,20},{28,16},{1,13},{... | collective-permute-start | bytes 12296 | tf_op jit(solution)/shard_map/ppermute | solution.py:483
  11.3 4.6 %copy-start = (s32[8,128]{1,0:T(8,128)}, s32[8,128]{1,0:T(8,128)S(1)}, u32[]{:S(2)}) copy-start(s32[8,128]{1,0:T(8,128)S(1)} %collective-permute-done.6.others_7_) | copy-start | bytes 12292
  11.3 3.8 %collective-permute-start.1 = (s32[8,128]{1,0:T(8,128)}, s32[8,128]{1,0:T(8,128)S(1)}, u32[]{:S(2)}, u32[]{:S(2)}) collective-permute-start(s32[8,128]{1,0:T(8,128)} %bitcast.9), channel_id=1, source_target_pairs={{0,8},{4,12},{8,0},{12,4},{16,24},{20,28},{24,16},{28,20},{1,9},{5... | collective-permute-start | bytes 12296 | tf_op jit(solution)/shard_map/ppermute | solution.py:483
  12.1 3.8 %copy-start.1 = (s32[8,128]{1,0:T(8,128)}, s32[8,128]{1,0:T(8,128)S(1)}, u32[]{:S(2)}) copy-start(s32[8,128]{1,0:T(8,128)S(1)} %collective-permute-done.5.others_6_) | copy-start | bytes 12292
  12.1 3.8 %collective-permute-start = (s32[8,128]{1,0:T(8,128)}, s32[8,128]{1,0:T(8,128)S(1)}, u32[]{:S(2)}, u32[]{:S(2)}) collective-permute-start(s32[8,128]{1,0:T(8,128)} %bitcast.10), channel_id=1, source_target_pairs={{0,4},{4,0},{8,12},{12,8},{16,20},{20,16},{24,28},{28,24},{1,5},{5... | collective-permute-start | bytes 12296 | tf_op jit(solution)/shard_map/ppermute | solution.py:483
  12.4 3.5 %copy-start.2 = (s32[8,128]{1,0:T(8,128)}, s32[8,128]{1,0:T(8,128)S(1)}, u32[]{:S(2)}) copy-start(s32[8,128]{1,0:T(8,128)S(1)} %collective-permute-done.4.others_5_) | copy-start | bytes 12292
  12.4 3.5 %copy-start.3 = (s32[8,128]{1,0:T(8,128)}, s32[8,128]{1,0:T(8,128)S(1)}, u32[]{:S(2)}) copy-start(s32[8,128]{1,0:T(8,128)S(1)} %collective-permute-done.3.others_4_) | copy-start | bytes 12292
  13.7 2.3 %copy-start.4 = (s32[8,128]{1,0:T(8,128)}, s32[8,128]{1,0:T(8,128)S(1)}, u32[]{:S(2)}) copy-start(s32[8,128]{1,0:T(8,128)S(1)} %collective-permute-done.2.others_3_) | copy-start | bytes 12292
  15.1 0.8 %copy-start.5 = (s32[8,128]{1,0:T(8,128)}, s32[8,128]{1,0:T(8,128)S(1)}, u32[]{:S(2)}) copy-start(s32[8,128]{1,0:T(8,128)S(1)} %collective-permute-done.1.others_2_) | copy-start | bytes 12292
  15.9 0.6 %copy-start.6 = (s32[8,128]{1,0:T(8,128)}, s32[8,128]{1,0:T(8,128)S(1)}, u32[]{:S(2)}) copy-start(s32[8,128]{1,0:T(8,128)S(1)} %collective-permute-done.others_1_) | copy-start | bytes 12292

commit v9 on v8

--- a/solution.py
+++ b/solution.py
@@ -129,7 +129,7 @@
     rest_b = nn(rest, shift).astype(BF16)
     cb = nt(rest_b, rest)
     if full is not None:
-        zg, lac, xch, xcl = full
+        zg, lac, xch, xcl, done = full
         z16 = nt(embs, w_in[0:E, :]).astype(BF16).astype(F32)
         sz = z16 * (0.5 + 0.5 * jnp.tanh(0.5 * z16))
         for s in range(2):
@@ -192,23 +192,53 @@
             high, low = split(silu_half(partial + last[v : v + 1, :]))
             xch[(q * SYM + v) * CH : (q * SYM + v + 1) * CH, :] = high
             xcl[(q * SYM + v) * CH : (q * SYM + v + 1) * CH, :] = low
-
-
-def layer_kernel(
-    count, mine, tok_s, emb_h, w_in_h, cw_h, bias_h, rate_h, skip_h, gain_h, w_out_h, *others
+        done(q)
+
+
+def table_kernel(
+    emb_h, w_in_h, cw_h, bias_h, rate_h, skip_h, gain_h,
+    tab, cst, lac, tw, emb16, xch_h, xcl_h,
+    emb, w_in, cw, bias, rate, skip, gain, atab, gtab, zg, xch, xcl, sems, out_sems,
 ):
-    finish_layer(
-        others[:count], mine, tok_s, emb_h, w_in_h, cw_h, bias_h, rate_h, skip_h, gain_h, w_out_h,
-        *others[count:]
+    for copy in begin((emb_h, w_in_h, cw_h, bias_h, rate_h, skip_h, gain_h),
+                      (emb, w_in, cw, bias, rate, skip, gain), sems):
+        copy.wait()
+    part = SYM * CH
+    leaving = []
+
+    def done(q):
+        rows = slice(q * part, (q + 1) * part)
+        for i, (source, target) in enumerate(((xch, xch_h), (xcl, xcl_h))):
+            copy = pltpu.make_async_copy(source.at[rows, :], target.at[rows, :], out_sems.at[i, q])
+            copy.start()
+            leaving.append(copy)
+
+    symbol_tables(
+        (0, 1), (zg, lac, xch, xcl, done),
+        emb, w_in, cw, bias, rate, skip, gain, emb16, atab, gtab, cst, tw,
     )
+    for d in range(2):
+        for u in range(SYM):
+            at = (d * SYM + u) * 64
+            tab[at : at + 8, :] = atab[d * 64 + u * 8 : d * 64 + u * 8 + 8, :]
+            for w in range(SYM):
+                row = (d * SYM + w) * 64 + u * 8
+                tab[at + 8 + w * 8 : at + 16 + w * 8, :] = gtab[row : row + 8, :]
+            tab[at + 48 : at + 56, :] = zg[u * 8 : u * 8 + 8, :]
+    for copy in leaving:
+        copy.wait()
+
+
+def layer_kernel(count, mine, tok_s, *others):
+    finish_layer(others[:count], mine, tok_s, *others[count:])
 
 
 def finish_layer(
-    blocks, mine, tok_s, emb_h, w_in_h, cw_h, bias_h, rate_h, skip_h, gain_h, w_out_h,
+    blocks, mine, tok_s, tab_h, cst_h, lac_h, tw_h, emb16_h, w_out_h, xch_h, xcl_h,
     out,
-    emb, w_in, cw, bias, rate, skip, gain, w_out, emb16, atab, gtab, cst, tw, zg, lac, xch, xcl,
+    tab, cst, lac, tw, emb16, w_out, xch, xcl,
     tok_x, tok_f, code, tri, hist, svec, xad, xbc, yad, ybc, mix,
-    tab, ring0, ring1, ring2, ring3, sems,
+    ring0, ring1, ring2, ring3, sems,
 ):
     rows = tok_x.shape[0]
     own = rows // 8
@@ -217,9 +247,9 @@
     j = mine[0]
     size = rows // len(blocks)
     arriving = begin(
-        (*blocks, emb_h, w_in_h, cw_h, bias_h, rate_h, skip_h, gain_h, w_out_h),
+        (*blocks, lac_h, tw_h, tab_h, cst_h, emb16_h, w_out_h, xch_h, xcl_h),
         (*[tok_x.at[size * m : size * m + size, :] for m in range(len(blocks))],
-         emb, w_in, cw, bias, rate, skip, gain, w_out), sems)
+         lac, tw, tab, cst, emb16, w_out, xch, xcl), sems)
     for copy in arriving[: len(blocks)]:
         copy.wait()
     for b in range(own):
@@ -244,12 +274,8 @@
     sub8 = iota((8, CH), 0).astype(F32)
     subc = iota((CH, CH), 0).astype(F32)
 
-    for copy in arriving[len(blocks) :]:
+    for copy in arriving[len(blocks) : len(blocks) + 6]:
         copy.wait()
-    symbol_tables(
-        (0, 1), (zg, lac, xch, xcl),
-        emb, w_in, cw, bias, rate, skip, gain, emb16, atab, gtab, cst, tw,
-    )
 
     def block(b, off):
         side = jnp.where(b >= j, 1, 0)
@@ -314,6 +340,8 @@
         for c in range(nchunk):
             convolve(c)
 
+    for copy in arriving[len(blocks) + 6 :]:
+        copy.wait()
     last8 = rows - 8
     xs = {}
     for d in range(2):
@@ -355,21 +383,12 @@
         for w in range(SYM):
             value = jnp.zeros((8, CH), F32)
             for v in range(SYM):
-                at = (d * SYM + w) * 64 + v * 8
+                at = (d * SYM + v) * 64 + 8 + w * 8
                 sat = (d * SYM + v) * 8
-                value = value + gtab[at : at + 8, :] * svec[sat : sat + 8, :]
+                value = value + tab[at : at + 8, :] * svec[sat : sat + 8, :]
             starts.append(value)
 
     skips = (cst[0:8, :], cst[8:16, :])
-
-    for d in range(2):
-        for u in range(SYM):
-            at = (d * SYM + u) * 64
-            tab[at : at + 8, :] = atab[d * 64 + u * 8 : d * 64 + u * 8 + 8, :]
-            for w in range(SYM):
-                row = (d * SYM + w) * 64 + u * 8
-                tab[at + 8 + w * 8 : at + 16 + w * 8, :] = gtab[row : row + 8, :]
-            tab[at + 48 : at + 56, :] = zg[u * 8 : u * 8 + 8, :]
 
     def rows8(ref, k):
         return ref[k * 8 : k * 8 + 8, :]
@@ -476,7 +495,6 @@
     sds = jax.ShapeDtypeStruct
     weights = (
         embed_table, input_weight_matrix.T, conv_weight, dt_bias, decay_rate, skip_gain, norm_gain,
-        output_weight_matrix,
     )
 
     def sent(blocks, mask):
@@ -487,26 +505,54 @@
     for bit in range(low):
         gathered = jnp.concatenate([gathered, sent(gathered, 1 << bit)], axis=0)
     blocks = [gathered] + [sent(gathered, m << low) for m in range(1, own >> low)]
+    if len(blocks) > 5:
+        tied = lax.optimization_barrier((dt_bias, *blocks[-2:]))
+        weights = weights[:3] + (tied[0],) + weights[4:]
+        blocks[-2:] = tied[1:]
+    limit = pltpu.CompilerParams(vmem_limit_bytes=56 * 1024 * 1024)
+    dma = pltpu.SemaphoreType.DMA
+    window = sds((4 * SYM * CH, E), BF16)
+    shapes = (
+        sds((2 * SYM * 64, CH), F32),
+        sds((32, CH), F32),
+        sds((2 * SYM * 16, CH), F32),
+        sds((4, CH, E), BF16),
+        sds((16, D), F32),
+        window,
+        window,
+    )
+    tab, cst, lac, tw, emb16, xch, xcl = pl.pallas_call(
+        table_kernel,
+        out_shape=shapes,
+        in_specs=[hbm] * 7,
+        out_specs=[vm] * 5 + [hbm] * 2,
+        scratch_shapes=[pltpu.VMEM(w.shape, w.dtype) for w in weights]
+        + [
+            pltpu.VMEM((2 * 64, CH), F32),
+            pltpu.VMEM((2 * SYM * 64, CH), F32),
+            pltpu.VMEM((64, CH), F32),
+            pltpu.VMEM(window.shape, BF16),
+            pltpu.VMEM(window.shape, BF16),
+            dma((7,)),
+            dma((2, 4)),
+        ],
+        compiler_params=limit,
+        cost_estimate=pl.CostEstimate(
+            flops=1_000_000_000, bytes_accessed=6_000_000, transcendentals=0
+        ),
+        name="symbol_tables",
+    )(*weights)
+    fetched = (tab, cst, lac, tw, emb16, output_weight_matrix, xch, xcl)
     mine = lax.axis_index("seq").reshape(1).astype(jnp.int32)
-    table = pltpu.VMEM((4 * SYM * CH, E), BF16)
     steps = pltpu.VMEM((length * 8, CH), F32)
     ring = pltpu.VMEM((8 * SYM * 8, CH), F32)
     return pl.pallas_call(
         functools.partial(layer_kernel, len(blocks)),
         out_shape=sds((length, D), BF16),
-        in_specs=[sm, sm] + [hbm] * 8 + [hbm] * len(blocks),
+        in_specs=[sm, sm] + [hbm] * (len(blocks) + 8),
         out_specs=vm,
-        scratch_shapes=[pltpu.VMEM(w.shape, w.dtype) for w in weights]
+        scratch_shapes=[pltpu.VMEM(w.shape, w.dtype) for w in fetched]
         + [
-            pltpu.VMEM((16, D), F32),
-            pltpu.VMEM((2 * 64, CH), F32),
-            pltpu.VMEM((2 * SYM * 64, CH), F32),
-            pltpu.VMEM((32, CH), F32),
-            pltpu.VMEM((4, CH, E), BF16),
-            pltpu.VMEM((64, CH), F32),
-            pltpu.VMEM((2 * SYM * 16, CH), F32),
-            table,
-            table,
             pltpu.VMEM((rows, CH), jnp.int32),
             pltpu.VMEM((7, rows, CH), F32),
             pltpu.VMEM((2, rows, CH), F32),
@@ -518,19 +564,18 @@
             steps,
             steps,
             pltpu.VMEM((2 * CH * 8, CH), F32),
-            pltpu.VMEM((2 * SYM * 64, CH), F32),
             ring,
             ring,
             ring,
             ring,
-            pltpu.SemaphoreType.DMA((8 + len(blocks),)),
+            dma((8 + len(blocks),)),
         ],
-        compiler_params=pltpu.CompilerParams(vmem_limit_bytes=56 * 1024 * 1024),
+        compiler_params=limit,
         cost_estimate=pl.CostEstimate(
             flops=9_000_000_000, bytes_accessed=4_000_000, transcendentals=0
         ),
         name="bidirectional_layer",
-    )(mine, token_ids, *weights, *blocks)
+    )(mine, token_ids, *blocks, *fetched)
 
 
 def solution(mesh):

time: 36.6 us -> 38.7 us (1.057)
  Pallas kernels: 19.9 us -> 25.3 us
  waiting for transfers between devices: 3.46 us -> 0.02 us
    pallas_call x0 -> x1, Pallas kernels: none -> 5.8 us  [per_device(): pl.pallas_call(table_kernel, out_shape=shapes, in_specs=[hbm] * 7, out_sp...]
    ppermute x7, waiting for transfers between devices: 3.46 us -> 0.02 us  [sent(): return lax.ppermute(blocks, 'seq', [(i, i ^ mask) for i in range(own)])]
  transfers between devices with their start and end apart: 7 -> 7, of which waited for: 3 -> 0; matrix products, arithmetic and copies ran while one was open for 0% -> 0% of each run, Pallas kernels for 0% -> 15%
where the time goes in v9:
time: 38.7 us; the launch traced here: 38.4 us
  Pallas kernels  25.3 us (65%)
  starting transfers between devices  12.4 us (32%)
  local copies, waits for them, and re-layouts  0.57 us (1%)
    pallas_call x1, Pallas kernels, per_device(): pl.pallas_call(functools.partial(layer_kernel, len(blocks)), out_shape=sd...  19.5 us
    ppermute x7, starting transfers between devices, sent(): return lax.ppermute(blocks, 'seq', [(i, i ^ mask) for i in range(own)])  12.4 us
    pallas_call x1, Pallas kernels, per_device(): pl.pallas_call(table_kernel, out_shape=shapes, in_specs=[hbm] * 7, out_sp...  5.8 us
  transfers between devices with their start and end apart: 7, of which 0 were waited for; matrix products, arithmetic and copies ran while one was open for 0% of the time, Pallas kernels for 15%

profile of v9, /device:TPU:0, one launch (start us, length us, event | category | flops | bytes accessed | tf_op | source)
XLA Modules:
  0.0 38.4 jit_solution(16005659490700997567)
XLA Ops:
  0.0 6.0 %collective-permute-start.6 = (s32[8,128]{1,0:T(8,128)}, s32[8,128]{1,0:T(8,128)S(1)}, u32[]{:S(2)}, u32[]{:S(2)}) collective-permute-start(s32[8,128]{1,0:T(8,128)} %bitcast.4), channel_id=1, source_target_pairs={{0,28},{4,24},{8,20},{12,16},{16,12},{20,8},{24,4},{28,0},{1,29},{... | collective-permute-start | bytes 12296 | tf_op jit(solution)/shard_map/ppermute | solution.py:501
  6.0 0.2 collective-permute-start.5
  6.2 0.7 %collective-permute-start.4 = (s32[8,128]{1,0:T(8,128)}, s32[8,128]{1,0:T(8,128)S(1)}, u32[]{:S(2)}, u32[]{:S(2)}) collective-permute-start(s32[8,128]{1,0:T(8,128)} %bitcast.6), channel_id=1, source_target_pairs={{0,20},{4,16},{8,28},{12,24},{16,4},{20,0},{24,12},{28,8},{1,21},{... | collective-permute-start | bytes 12296 | tf_op jit(solution)/shard_map/ppermute | solution.py:501
  7.0 2.0 %collective-permute-start.3 = (s32[8,128]{1,0:T(8,128)}, s32[8,128]{1,0:T(8,128)S(1)}, u32[]{:S(2)}, u32[]{:S(2)}) collective-permute-start(s32[8,128]{1,0:T(8,128)} %bitcast.7), channel_id=1, source_target_pairs={{0,16},{4,20},{8,24},{12,28},{16,0},{20,4},{24,8},{28,12},{1,17},{... | collective-permute-start | bytes 12296 | tf_op jit(solution)/shard_map/ppermute | solution.py:501
  8.9 2.4 %collective-permute-start.2 = (s32[8,128]{1,0:T(8,128)}, s32[8,128]{1,0:T(8,128)S(1)}, u32[]{:S(2)}, u32[]{:S(2)}) collective-permute-start(s32[8,128]{1,0:T(8,128)} %bitcast.8), channel_id=1, source_target_pairs={{0,12},{4,8},{8,4},{12,0},{16,28},{20,24},{24,20},{28,16},{1,13},{... | collective-permute-start | bytes 12296 | tf_op jit(solution)/shard_map/ppermute | solution.py:501
  11.3 0.0 collective-permute-done.6.others_7_
  11.3 0.0 copy-start
  11.3 0.8 %collective-permute-start.1 = (s32[8,128]{1,0:T(8,128)}, s32[8,128]{1,0:T(8,128)S(1)}, u32[]{:S(2)}, u32[]{:S(2)}) collective-permute-start(s32[8,128]{1,0:T(8,128)} %bitcast.9), channel_id=1, source_target_pairs={{0,8},{4,12},{8,0},{12,4},{16,24},{20,28},{24,16},{28,20},{1,9},{5... | collective-permute-start | bytes 12296 | tf_op jit(solution)/shard_map/ppermute | solution.py:501
  12.1 0.0 collective-permute-done.5.others_6_
  12.1 0.0 copy-start.1
  12.1 0.3 collective-permute-start
  12.4 5.8 %symbol_tables.1 = (f32[640,128]{1,0:T(8,128)}, f32[32,128]{1,0:T(8,128)}, f32[160,128]{1,0:T(8,128)}, bf16[4,128,512]{2,1,0:T(8,128)(2,1)}, f32[16,256]{1,0:T(8...) custom-call(bf16[5,256]{1,0:T(8,128)(2,1)} %emb_h.1, bf16[1064,256]{1,0:T(8,128)(2,1)} %bitcast.3, ...), custom_call_target="tpu_custom_call" | custom-call | flops 1000000000 | bytes 6000000 | tf_op jit(solution)/shard_map/symbol_tables/pallas_call | solution.py:524
  18.2 0.0 collective-permute-done.4.others_5_
  18.3 0.0 copy-start.2
  18.3 0.0 collective-permute-done.3.others_4_
  18.3 0.0 copy-start.3
  18.3 0.0 collective-permute-done.2.others_3_
  18.3 0.0 copy-start.4
  18.3 0.0 collective-permute-done.1.others_2_
  18.3 0.0 copy-start.5
  18.3 0.0 collective-permute-done.others_1_
  18.3 0.0 copy-start.6
  18.3 0.0 copy-done
  18.4 0.0 copy-done.1
  18.4 0.5 %copy-done.2 = s32[8,128]{1,0:T(8,128)} copy-done((s32[8,128]{1,0:T(8,128)}, s32[8,128]{1,0:T(8,128)S(1)}, u32[]{:S(2)}) %copy-start.2) | copy-done | bytes 4120
  18.8 0.0 copy-done.3
  18.9 0.0 copy-done.4
  18.9 0.0 copy-done.5
  18.9 0.0 copy-done.6
  18.9 19.5 %bidirectional_layer.1 = bf16[1024,256]{1,0:T(8,128)(2,1)} custom-call(s32[1]{0:T(128)} %bitcast.mine, s32[1024]{0:T(1024)} %tok_s.1, s32[8,128]{1,0:T(8,128)} %bitcast.11, s32[8,128]{1,0:T(8,128)} %copy-done.6, s32[8,128]{1,0:T(8,128)} %copy-done.5, s32[8,128]{1,0:T(8,128)} %copy-done.4, s32[8,128]{1,0:T(8,128)} %copy-done.3, s32[8,128]{1,0:T(8,128)} %copy-done.2, ...), custom_call_target="tpu_custom_call" | custom-call | flops 8999999488 | bytes 4000000 | tf_op jit(solution)/shard_map/bidirectional_layer/pallas_call | solution.py:549
Async XLA Ops:
  0.0 11.3 %collective-permute-start.6 = (s32[8,128]{1,0:T(8,128)}, s32[8,128]{1,0:T(8,128)S(1)}, u32[]{:S(2)}, u32[]{:S(2)}) collective-permute-start(s32[8,128]{1,0:T(8,128)} %bitcast.4), channel_id=1, source_target_pairs={{0,28},{4,24},{8,20},{12,16},{16,12},{20,8},{24,4},{28,0},{1,29},{... | collective-permute-start | bytes 12296 | tf_op jit(solution)/shard_map/ppermute | solution.py:501
  6.0 6.1 %collective-permute-start.5 = (s32[8,128]{1,0:T(8,128)}, s32[8,128]{1,0:T(8,128)S(1)}, u32[]{:S(2)}, u32[]{:S(2)}) collective-permute-start(s32[8,128]{1,0:T(8,128)} %bitcast.5), channel_id=1, source_target_pairs={{0,24},{4,28},{8,16},{12,20},{16,8},{20,12},{24,0},{28,4},{1,25},{... | collective-permute-start | bytes 12296 | tf_op jit(solution)/shard_map/ppermute | solution.py:501
  6.2 12.0 %collective-permute-start.4 = (s32[8,128]{1,0:T(8,128)}, s32[8,128]{1,0:T(8,128)S(1)}, u32[]{:S(2)}, u32[]{:S(2)}) collective-permute-start(s32[8,128]{1,0:T(8,128)} %bitcast.6), channel_id=1, source_target_pairs={{0,20},{4,16},{8,28},{12,24},{16,4},{20,0},{24,12},{28,8},{1,21},{... | collective-permute-start | bytes 12296 | tf_op jit(solution)/shard_map/ppermute | solution.py:501
  7.0 11.3 %collective-permute-start.3 = (s32[8,128]{1,0:T(8,128)}, s32[8,128]{1,0:T(8,128)S(1)}, u32[]{:S(2)}, u32[]{:S(2)}) collective-permute-start(s32[8,128]{1,0:T(8,128)} %bitcast.7), channel_id=1, source_target_pairs={{0,16},{4,20},{8,24},{12,28},{16,0},{20,4},{24,8},{28,12},{1,17},{... | collective-permute-start | bytes 12296 | tf_op jit(solution)/shard_map/ppermute | solution.py:501
  8.9 9.4 %collective-permute-start.2 = (s32[8,128]{1,0:T(8,128)}, s32[8,128]{1,0:T(8,128)S(1)}, u32[]{:S(2)}, u32[]{:S(2)}) collective-permute-start(s32[8,128]{1,0:T(8,128)} %bitcast.8), channel_id=1, source_target_pairs={{0,12},{4,8},{8,4},{12,0},{16,28},{20,24},{24,20},{28,16},{1,13},{... | collective-permute-start | bytes 12296 | tf_op jit(solution)/shard_map/ppermute | solution.py:501
  11.3 7.0 %copy-start = (s32[8,128]{1,0:T(8,128)}, s32[8,128]{1,0:T(8,128)S(1)}, u32[]{:S(2)}) copy-start(s32[8,128]{1,0:T(8,128)S(1)} %collective-permute-done.6.others_7_) | copy-start | bytes 12292
  11.3 7.0 %collective-permute-start.1 = (s32[8,128]{1,0:T(8,128)}, s32[8,128]{1,0:T(8,128)S(1)}, u32[]{:S(2)}, u32[]{:S(2)}) collective-permute-start(s32[8,128]{1,0:T(8,128)} %bitcast.9), channel_id=1, source_target_pairs={{0,8},{4,12},{8,0},{12,4},{16,24},{20,28},{24,16},{28,20},{1,9},{5... | collective-permute-start | bytes 12296 | tf_op jit(solution)/shard_map/ppermute | solution.py:501
  12.1 6.3 %copy-start.1 = (s32[8,128]{1,0:T(8,128)}, s32[8,128]{1,0:T(8,128)S(1)}, u32[]{:S(2)}) copy-start(s32[8,128]{1,0:T(8,128)S(1)} %collective-permute-done.5.others_6_) | copy-start | bytes 12292
  12.1 6.2 %collective-permute-start = (s32[8,128]{1,0:T(8,128)}, s32[8,128]{1,0:T(8,128)S(1)}, u32[]{:S(2)}, u32[]{:S(2)}) collective-permute-start(s32[8,128]{1,0:T(8,128)} %bitcast.10), channel_id=1, source_target_pairs={{0,4},{4,0},{8,12},{12,8},{16,20},{20,16},{24,28},{28,24},{1,5},{5... | collective-permute-start | bytes 12296 | tf_op jit(solution)/shard_map/ppermute | solution.py:501
  18.3 0.6 %copy-start.2 = (s32[8,128]{1,0:T(8,128)}, s32[8,128]{1,0:T(8,128)S(1)}, u32[]{:S(2)}) copy-start(s32[8,128]{1,0:T(8,128)S(1)} %collective-permute-done.4.others_5_) | copy-start | bytes 12292
  18.3 0.6 %copy-start.3 = (s32[8,128]{1,0:T(8,128)}, s32[8,128]{1,0:T(8,128)S(1)}, u32[]{:S(2)}) copy-start(s32[8,128]{1,0:T(8,128)S(1)} %collective-permute-done.3.others_4_) | copy-start | bytes 12292
  18.3 0.6 %copy-start.4 = (s32[8,128]{1,0:T(8,128)}, s32[8,128]{1,0:T(8,128)S(1)}, u32[]{:S(2)}) copy-start(s32[8,128]{1,0:T(8,128)S(1)} %collective-permute-done.2.others_3_) | copy-start | bytes 12292
  18.3 0.6 %copy-start.5 = (s32[8,128]{1,0:T(8,128)}, s32[8,128]{1,0:T(8,128)S(1)}, u32[]{:S(2)}) copy-start(s32[8,128]{1,0:T(8,128)S(1)} %collective-permute-done.1.others_2_) | copy-start | bytes 12292
  18.3 0.6 %copy-start.6 = (s32[8,128]{1,0:T(8,128)}, s32[8,128]{1,0:T(8,128)S(1)}, u32[]{:S(2)}) copy-start(s32[8,128]{1,0:T(8,128)S(1)} %collective-permute-done.others_1_) | copy-start | bytes 12292

commit v10 on v8

--- a/solution.py
+++ b/solution.py
@@ -426,7 +426,8 @@
         hot = jnp.concatenate(
             [jnp.where(row == sub, 1.0, 0.0), jnp.zeros((CH - 8, CH), F32)], axis=0
         ).T.astype(BF16)
-        parts = [mix[pl.ds(base + i, CH, stride=8), :].astype(BF16) for i in range(8)]
+        held_rows = mix.at[pl.ds(pl.multiple_of(base, CH * 8), CH * 8), :]
+        parts = [held_rows[pl.ds(i, CH, stride=8), :].astype(BF16) for i in range(8)]
         one = nn(jnp.concatenate(parts[0:4], axis=1), wout).astype(BF16).astype(F32)
         two = nn(jnp.concatenate(parts[4:8], axis=1), wflip).astype(BF16).astype(F32)
         out[pl.ds(pl.multiple_of(c * CH, CH), CH), :] = (nn(hot, emb_rows) + one + two).astype(BF16)
@@ -486,7 +487,10 @@
     low = max(rounds - 3, 0)
     for bit in range(low):
         gathered = jnp.concatenate([gathered, sent(gathered, 1 << bit)], axis=0)
-    blocks = [gathered] + [sent(gathered, m << low) for m in range(1, own >> low)]
+    blocks = [gathered] + [None] * ((own >> low) - 1)
+    for m in sorted(range(1, own >> low), key=lambda m: (bin(m).count("1"), m)):
+        top = 1 << (m.bit_length() - 1)
+        blocks[m] = sent(blocks[m ^ top], top << low)
     mine = lax.axis_index("seq").reshape(1).astype(jnp.int32)
     table = pltpu.VMEM((4 * SYM * CH, E), BF16)
     steps = pltpu.VMEM((length * 8, CH), F32)

time: 36.6 us -> 37.6 us (1.027)
  waiting for transfers between devices: 3.46 us -> 4.38 us
    ppermute x7, waiting for transfers between devices: 3.46 us -> 4.38 us  [sent(): return lax.ppermute(blocks, 'seq', [(i, i ^ mask) for i in range(own)])]
where the time goes in v10:
time: 37.6 us; the launch traced here: 37.4 us
  Pallas kernels  19.9 us (53%)
  starting transfers between devices  12.5 us (33%)
  waiting for transfers between devices  4.38 us (12%)
  local copies, waits for them, and re-layouts  0.57 us (2%)
    pallas_call x1, Pallas kernels, per_device(): pl.pallas_call(functools.partial(layer_kernel, len(blocks)), out_shape=sd...  19.9 us
    ppermute x7, starting transfers between devices, sent(): return lax.ppermute(blocks, 'seq', [(i, i ^ mask) for i in range(own)])  12.5 us
    ppermute x7, waiting for transfers between devices, sent(): return lax.ppermute(blocks, 'seq', [(i, i ^ mask) for i in range(own)])  4.38 us
  transfers between devices with their start and end apart: 7, of which 3 were waited for; matrix products, arithmetic and copies ran while one was open for 0% of the time, Pallas kernels for 0%

profile of v10, /device:TPU:0, one launch (start us, length us, event | category | flops | bytes accessed | tf_op | source)
XLA Modules:
  0.0 37.4 jit_solution(6827524806234425242)
XLA Ops:
  0.0 3.0 %collective-permute-start = (s32[8,128]{1,0:T(8,128)}, s32[8,128]{1,0:T(8,128)S(1)}, u32[]{:S(2)}, u32[]{:S(2)}) collective-permute-start(s32[8,128]{1,0:T(8,128)} %bitcast.4), channel_id=1, source_target_pairs={{0,4},{4,0},{8,12},{12,8},{16,20},{20,16},{24,28},{28,24},{1,5},{5... | collective-permute-start | bytes 12296 | tf_op jit(solution)/shard_map/ppermute | solution.py:484
  3.0 1.6 %collective-permute-start.1 = (s32[8,128]{1,0:T(8,128)}, s32[8,128]{1,0:T(8,128)S(1)}, u32[]{:S(2)}, u32[]{:S(2)}) collective-permute-start(s32[8,128]{1,0:T(8,128)} %bitcast.5), channel_id=1, source_target_pairs={{0,8},{4,12},{8,0},{12,4},{16,24},{20,28},{24,16},{28,20},{1,9},{5... | collective-permute-start | bytes 12296 | tf_op jit(solution)/shard_map/ppermute | solution.py:484
  4.5 0.2 collective-permute-done.others_1_
  4.8 0.0 copy-start
  4.8 2.1 %collective-permute-start.2 = (s32[8,128]{1,0:T(8,128)S(1)}, s32[8,128]{1,0:T(8,128)S(1)}, u32[]{:S(2)}, u32[]{:S(2)}) collective-permute-start(s32[8,128]{1,0:T(8,128)S(1)} %collective-permute-done.others_1_), channel_id=1, source_target_pairs={{0,8},{4,12},{8,0},{12,4},{16,24},{20,28},{24,16},{28,20},{1,9},{5... | collective-permute-start | bytes 12296 | tf_op jit(solution)/shard_map/ppermute | solution.py:484
  6.8 2.6 %collective-permute-start.3 = (s32[8,128]{1,0:T(8,128)}, s32[8,128]{1,0:T(8,128)S(1)}, u32[]{:S(2)}, u32[]{:S(2)}) collective-permute-start(s32[8,128]{1,0:T(8,128)} %bitcast.6), channel_id=1, source_target_pairs={{0,16},{4,20},{8,24},{12,28},{16,0},{20,4},{24,8},{28,12},{1,17},{... | collective-permute-start | bytes 12296 | tf_op jit(solution)/shard_map/ppermute | solution.py:484
  9.4 0.3 collective-permute-start.4
  9.8 0.0 collective-permute-done.1.others_2_
  9.8 0.0 copy-start.1
  9.8 2.6 %collective-permute-start.5 = (s32[8,128]{1,0:T(8,128)S(1)}, s32[8,128]{1,0:T(8,128)S(1)}, u32[]{:S(2)}, u32[]{:S(2)}) collective-permute-start(s32[8,128]{1,0:T(8,128)S(1)} %collective-permute-done.1.others_2_), channel_id=1, source_target_pairs={{0,16},{4,20},{8,24},{12,28},{16,0},{20,4},{24,8},{28,12},{1,17},{... | collective-permute-start | bytes 12296 | tf_op jit(solution)/shard_map/ppermute | solution.py:484
  12.4 0.0 collective-permute-done.2.others_3_
  12.4 0.0 copy-start.2
  12.4 0.3 collective-permute-start.6
  12.7 0.0 collective-permute-done.3.others_4_
  12.7 0.0 copy-start.3
  12.7 1.6 %collective-permute-done.5.others_6_ = s32[8,128]{1,0:T(8,128)S(1)} collective-permute-done((s32[8,128]{1,0:T(8,128)S(1)}, s32[8,128]{1,0:T(8,128)S(1)}, u32[]{:S(2)}, u32[]{:S(2)}) %collective-permute-start.5) | collective-permute-done | bytes 4128 | tf_op jit(solution)/shard_map/ppermute | solution.py:484
  14.3 0.0 copy-start.5
  14.3 0.0 collective-permute-done.4.others_5_
  14.3 0.0 copy-start.4
  14.3 2.6 %collective-permute-done.6.others_7_ = s32[8,128]{1,0:T(8,128)S(1)} collective-permute-done((s32[8,128]{1,0:T(8,128)S(1)}, s32[8,128]{1,0:T(8,128)S(1)}, u32[]{:S(2)}, u32[]{:S(2)}) %collective-permute-start.6) | collective-permute-done | bytes 4128 | tf_op jit(solution)/shard_map/ppermute | solution.py:484
  16.9 0.0 copy-start.6
  16.9 0.0 copy-done
  16.9 0.0 copy-done.1
  16.9 0.0 copy-done.2
  16.9 0.0 copy-done.3
  16.9 0.0 copy-done.5
  16.9 0.0 copy-done.4
  16.9 0.5 %copy-done.6 = s32[8,128]{1,0:T(8,128)} copy-done((s32[8,128]{1,0:T(8,128)}, s32[8,128]{1,0:T(8,128)S(1)}, u32[]{:S(2)}) %copy-start.6) | copy-done | bytes 4120
  17.5 19.9 %bidirectional_layer.1 = bf16[1024,256]{1,0:T(8,128)(2,1)} custom-call(s32[1]{0:T(128)} %bitcast.mine, s32[1024]{0:T(1024)} %tok_s.1, bf16[5,256]{1,0:T(8,128)(2,1)} %emb_h.1, bf16[1064,256]{1,0:T(8,128)(2,1)} %bitcast.3, f32[2,4,512]{2,1,0:T(4,128)} %cw_h.1, f32[2,8]{1,0:T(2,128)} %bias_h.1, f32[2,8]{1,0:T(2,128)} %rate_h.1, f32[2,8]{1,0:T(2,128)} %skip_h.1, ...), custom_call_target="tpu_custom_call" | custom-call | flops 8999999488 | bytes 4000000 | tf_op jit(solution)/shard_map/bidirectional_layer/pallas_call | solution.py:498
Async XLA Ops:
  0.0 4.8 %collective-permute-start = (s32[8,128]{1,0:T(8,128)}, s32[8,128]{1,0:T(8,128)S(1)}, u32[]{:S(2)}, u32[]{:S(2)}) collective-permute-start(s32[8,128]{1,0:T(8,128)} %bitcast.4), channel_id=1, source_target_pairs={{0,4},{4,0},{8,12},{12,8},{16,20},{20,16},{24,28},{28,24},{1,5},{5... | collective-permute-start | bytes 12296 | tf_op jit(solution)/shard_map/ppermute | solution.py:484
  3.0 6.8 %collective-permute-start.1 = (s32[8,128]{1,0:T(8,128)}, s32[8,128]{1,0:T(8,128)S(1)}, u32[]{:S(2)}, u32[]{:S(2)}) collective-permute-start(s32[8,128]{1,0:T(8,128)} %bitcast.5), channel_id=1, source_target_pairs={{0,8},{4,12},{8,0},{12,4},{16,24},{20,28},{24,16},{28,20},{1,9},{5... | collective-permute-start | bytes 12296 | tf_op jit(solution)/shard_map/ppermute | solution.py:484
  4.8 12.1 %copy-start = (s32[8,128]{1,0:T(8,128)}, s32[8,128]{1,0:T(8,128)S(1)}, u32[]{:S(2)}) copy-start(s32[8,128]{1,0:T(8,128)S(1)} %collective-permute-done.others_1_) | copy-start | bytes 12292
  4.8 7.6 %collective-permute-start.2 = (s32[8,128]{1,0:T(8,128)S(1)}, s32[8,128]{1,0:T(8,128)S(1)}, u32[]{:S(2)}, u32[]{:S(2)}) collective-permute-start(s32[8,128]{1,0:T(8,128)S(1)} %collective-permute-done.others_1_), channel_id=1, source_target_pairs={{0,8},{4,12},{8,0},{12,4},{16,24},{20,28},{24,16},{28,20},{1,9},{5... | collective-permute-start | bytes 12296 | tf_op jit(solution)/shard_map/ppermute | solution.py:484
  6.8 5.9 %collective-permute-start.3 = (s32[8,128]{1,0:T(8,128)}, s32[8,128]{1,0:T(8,128)S(1)}, u32[]{:S(2)}, u32[]{:S(2)}) collective-permute-start(s32[8,128]{1,0:T(8,128)} %bitcast.6), channel_id=1, source_target_pairs={{0,16},{4,20},{8,24},{12,28},{16,0},{20,4},{24,8},{28,12},{1,17},{... | collective-permute-start | bytes 12296 | tf_op jit(solution)/shard_map/ppermute | solution.py:484
  9.4 4.9 %collective-permute-start.4 = (s32[8,128]{1,0:T(8,128)S(1)}, s32[8,128]{1,0:T(8,128)S(1)}, u32[]{:S(2)}, u32[]{:S(2)}) collective-permute-start(s32[8,128]{1,0:T(8,128)S(1)} %collective-permute-done.others_1_), channel_id=1, source_target_pairs={{0,16},{4,20},{8,24},{12,28},{16,0},{20,4},{24,8},{28,12},{1,17},{... | collective-permute-start | bytes 12296 | tf_op jit(solution)/shard_map/ppermute | solution.py:484
  9.8 7.1 %copy-start.1 = (s32[8,128]{1,0:T(8,128)}, s32[8,128]{1,0:T(8,128)S(1)}, u32[]{:S(2)}) copy-start(s32[8,128]{1,0:T(8,128)S(1)} %collective-permute-done.1.others_2_) | copy-start | bytes 12292
  9.8 4.5 %collective-permute-start.5 = (s32[8,128]{1,0:T(8,128)S(1)}, s32[8,128]{1,0:T(8,128)S(1)}, u32[]{:S(2)}, u32[]{:S(2)}) collective-permute-start(s32[8,128]{1,0:T(8,128)S(1)} %collective-permute-done.1.others_2_), channel_id=1, source_target_pairs={{0,16},{4,20},{8,24},{12,28},{16,0},{20,4},{24,8},{28,12},{1,17},{... | collective-permute-start | bytes 12296 | tf_op jit(solution)/shard_map/ppermute | solution.py:484
  12.4 4.5 %copy-start.2 = (s32[8,128]{1,0:T(8,128)}, s32[8,128]{1,0:T(8,128)S(1)}, u32[]{:S(2)}) copy-start(s32[8,128]{1,0:T(8,128)S(1)} %collective-permute-done.2.others_3_) | copy-start | bytes 12292
  12.4 4.5 %collective-permute-start.6 = (s32[8,128]{1,0:T(8,128)S(1)}, s32[8,128]{1,0:T(8,128)S(1)}, u32[]{:S(2)}, u32[]{:S(2)}) collective-permute-start(s32[8,128]{1,0:T(8,128)S(1)} %collective-permute-done.2.others_3_), channel_id=1, source_target_pairs={{0,16},{4,20},{8,24},{12,28},{16,0},{20,4},{24,8},{28,12},{1,17},{... | collective-permute-start | bytes 12296 | tf_op jit(solution)/shard_map/ppermute | solution.py:484
  12.7 4.2 %copy-start.3 = (s32[8,128]{1,0:T(8,128)}, s32[8,128]{1,0:T(8,128)S(1)}, u32[]{:S(2)}) copy-start(s32[8,128]{1,0:T(8,128)S(1)} %collective-permute-done.3.others_4_) | copy-start | bytes 12292
  14.3 2.6 %copy-start.5 = (s32[8,128]{1,0:T(8,128)}, s32[8,128]{1,0:T(8,128)S(1)}, u32[]{:S(2)}) copy-start(s32[8,128]{1,0:T(8,128)S(1)} %collective-permute-done.5.others_6_) | copy-start | bytes 12292
  14.3 2.6 %copy-start.4 = (s32[8,128]{1,0:T(8,128)}, s32[8,128]{1,0:T(8,128)S(1)}, u32[]{:S(2)}) copy-start(s32[8,128]{1,0:T(8,128)S(1)} %collective-permute-done.4.others_5_) | copy-start | bytes 12292
  16.9 0.6 %copy-start.6 = (s32[8,128]{1,0:T(8,128)}, s32[8,128]{1,0:T(8,128)S(1)}, u32[]{:S(2)}) copy-start(s32[8,128]{1,0:T(8,128)S(1)} %collective-permute-done.6.others_7_) | copy-start | bytes 12292

commit v11 on v8

--- a/solution.py
+++ b/solution.py
@@ -374,7 +374,7 @@
     def rows8(ref, k):
         return ref[k * 8 : k * 8 + 8, :]
 
-    unroll = 128
+    unroll = CH
     held = 8
     rings = ((ring0, ring1), (ring2, ring3))
 
@@ -404,7 +404,6 @@
                 targets[d][local * 8 : local * 8 + 8, :] = y * rows8(part, 6)
         return tuple(states[0] + states[1])
 
-    lax.fori_loop(0, total // unroll, group, tuple(starts))
 
     flip = jnp.where(iota((D, D), 0) + iota((D, D), 1) == D - 1, 1.0, 0.0).astype(BF16)
     wout = w_out[...]
@@ -417,7 +416,6 @@
     ).astype(BF16)
     gains = (cst[16:24, :], cst[24:32, :])
     sub = iota((8, CH), 0).astype(F32)
-    mix[...] = jnp.zeros_like(mix)
     tiles = CH // SUB
 
     def project(c):
@@ -443,14 +441,26 @@
         at = (c & 1) * (CH * 8) + k * SUB * 8
         mix[pl.ds(pl.multiple_of(at, 8), SUB * 8), :] = normed.reshape(SUB * 8, CH)
 
-    def chunk(c, _):
-        project(jnp.maximum(c - 1, 0))
-        for k in range(tiles):
-            tile(c, k)
-        return 0
-
-    lax.fori_loop(0, nchunk, chunk, 0)
-    project(nchunk - 1)
+    def chunks(pair):
+        for c in pair:
+            for k in range(tiles):
+                tile(c, k)
+
+    def late_group(g, carry):
+        pair = (nchunk - g, g - 1)
+        chunks(pair)
+        carry = group(g, carry)
+        for c in pair:
+            project(c)
+        return carry
+
+    half = nchunk // 2 + 1
+    carry = lax.fori_loop(0, half, group, tuple(starts))
+    lax.fori_loop(half, nchunk, late_group, carry)
+    pair = (0, nchunk - 1)
+    chunks(pair)
+    for c in pair:
+        project(c)
 
 
 def per_device(

time: 36.6 us -> 36.3 us (level)
  no operation moved by 1% of the time
where the time goes in v11:
time: 36.3 us; the launch traced here: 36.1 us
  Pallas kernels  19.6 us (54%)
  starting transfers between devices  12.4 us (34%)
  waiting for transfers between devices  3.46 us (10%)
  local copies, waits for them, and re-layouts  0.57 us (2%)
    pallas_call x1, Pallas kernels, per_device(): pl.pallas_call(functools.partial(layer_kernel, len(blocks)), out_shape=sd...  19.6 us
    ppermute x7, starting transfers between devices, sent(): return lax.ppermute(blocks, 'seq', [(i, i ^ mask) for i in range(own)])  12.4 us
    ppermute x7, waiting for transfers between devices, sent(): return lax.ppermute(blocks, 'seq', [(i, i ^ mask) for i in range(own)])  3.46 us
  transfers between devices with their start and end apart: 7, of which 3 were waited for; matrix products, arithmetic and copies ran while one was open for 0% of the time, Pallas kernels for 0%

profile of v11, /device:TPU:0, one launch (start us, length us, event | category | flops | bytes accessed | tf_op | source)
XLA Modules:
  0.0 36.1 jit_solution(10875128285886811100)
XLA Ops:
  0.0 6.0 %collective-permute-start.6 = (s32[8,128]{1,0:T(8,128)}, s32[8,128]{1,0:T(8,128)S(1)}, u32[]{:S(2)}, u32[]{:S(2)}) collective-permute-start(s32[8,128]{1,0:T(8,128)} %bitcast.4), channel_id=1, source_target_pairs={{0,28},{4,24},{8,20},{12,16},{16,12},{20,8},{24,4},{28,0},{1,29},{... | collective-permute-start | bytes 12296 | tf_op jit(solution)/shard_map/ppermute | solution.py:493
  6.0 0.2 collective-permute-start.5
  6.2 0.7 %collective-permute-start.4 = (s32[8,128]{1,0:T(8,128)}, s32[8,128]{1,0:T(8,128)S(1)}, u32[]{:S(2)}, u32[]{:S(2)}) collective-permute-start(s32[8,128]{1,0:T(8,128)} %bitcast.6), channel_id=1, source_target_pairs={{0,20},{4,16},{8,28},{12,24},{16,4},{20,0},{24,12},{28,8},{1,21},{... | collective-permute-start | bytes 12296 | tf_op jit(solution)/shard_map/ppermute | solution.py:493
  7.0 2.0 %collective-permute-start.3 = (s32[8,128]{1,0:T(8,128)}, s32[8,128]{1,0:T(8,128)S(1)}, u32[]{:S(2)}, u32[]{:S(2)}) collective-permute-start(s32[8,128]{1,0:T(8,128)} %bitcast.7), channel_id=1, source_target_pairs={{0,16},{4,20},{8,24},{12,28},{16,0},{20,4},{24,8},{28,12},{1,17},{... | collective-permute-start | bytes 12296 | tf_op jit(solution)/shard_map/ppermute | solution.py:493
  8.9 2.4 %collective-permute-start.2 = (s32[8,128]{1,0:T(8,128)}, s32[8,128]{1,0:T(8,128)S(1)}, u32[]{:S(2)}, u32[]{:S(2)}) collective-permute-start(s32[8,128]{1,0:T(8,128)} %bitcast.8), channel_id=1, source_target_pairs={{0,12},{4,8},{8,4},{12,0},{16,28},{20,24},{24,20},{28,16},{1,13},{... | collective-permute-start | bytes 12296 | tf_op jit(solution)/shard_map/ppermute | solution.py:493
  11.3 0.0 collective-permute-done.6.others_7_
  11.3 0.0 copy-start
  11.3 0.8 %collective-permute-start.1 = (s32[8,128]{1,0:T(8,128)}, s32[8,128]{1,0:T(8,128)S(1)}, u32[]{:S(2)}, u32[]{:S(2)}) collective-permute-start(s32[8,128]{1,0:T(8,128)} %bitcast.9), channel_id=1, source_target_pairs={{0,8},{4,12},{8,0},{12,4},{16,24},{20,28},{24,16},{28,20},{1,9},{5... | collective-permute-start | bytes 12296 | tf_op jit(solution)/shard_map/ppermute | solution.py:493
  12.1 0.0 collective-permute-done.5.others_6_
  12.1 0.0 copy-start.1
  12.1 0.3 collective-permute-start
  12.4 0.0 collective-permute-done.4.others_5_
  12.4 0.0 copy-start.2
  12.4 0.0 collective-permute-done.3.others_4_
  12.4 0.0 copy-start.3
  12.5 1.2 %collective-permute-done.2.others_3_ = s32[8,128]{1,0:T(8,128)S(1)} collective-permute-done((s32[8,128]{1,0:T(8,128)}, s32[8,128]{1,0:T(8,128)S(1)}, u32[]{:S(2)}, u32[]{:S(2)}) %collective-permute-start.2) | collective-permute-done | bytes 4128 | tf_op jit(solution)/shard_map/ppermute | solution.py:493
  13.7 0.0 copy-start.4
  13.7 1.5 %collective-permute-done.1.others_2_ = s32[8,128]{1,0:T(8,128)S(1)} collective-permute-done((s32[8,128]{1,0:T(8,128)}, s32[8,128]{1,0:T(8,128)S(1)}, u32[]{:S(2)}, u32[]{:S(2)}) %collective-permute-start.1) | collective-permute-done | bytes 4128 | tf_op jit(solution)/shard_map/ppermute | solution.py:493
  15.1 0.0 copy-start.5
  15.1 0.8 %collective-permute-done.others_1_ = s32[8,128]{1,0:T(8,128)S(1)} collective-permute-done((s32[8,128]{1,0:T(8,128)}, s32[8,128]{1,0:T(8,128)S(1)}, u32[]{:S(2)}, u32[]{:S(2)}) %collective-permute-start) | collective-permute-done | bytes 4128 | tf_op jit(solution)/shard_map/ppermute | solution.py:493
  15.9 0.0 copy-start.6
  15.9 0.0 copy-done
  15.9 0.0 copy-done.1
  15.9 0.0 copy-done.2
  15.9 0.0 copy-done.3
  15.9 0.0 copy-done.4
  15.9 0.0 copy-done.5
  16.0 0.5 %copy-done.6 = s32[8,128]{1,0:T(8,128)} copy-done((s32[8,128]{1,0:T(8,128)}, s32[8,128]{1,0:T(8,128)S(1)}, u32[]{:S(2)}) %copy-start.6) | copy-done | bytes 4120
  16.5 19.6 %bidirectional_layer.1 = bf16[1024,256]{1,0:T(8,128)(2,1)} custom-call(s32[1]{0:T(128)} %bitcast.mine, s32[1024]{0:T(1024)} %tok_s.1, bf16[5,256]{1,0:T(8,128)(2,1)} %emb_h.1, bf16[1064,256]{1,0:T(8,128)(2,1)} %bitcast.3, f32[2,4,512]{2,1,0:T(4,128)} %cw_h.1, f32[2,8]{1,0:T(2,128)} %bias_h.1, f32[2,8]{1,0:T(2,128)} %rate_h.1, f32[2,8]{1,0:T(2,128)} %skip_h.1, ...), custom_call_target="tpu_custom_call" | custom-call | flops 8999999488 | bytes 4000000 | tf_op jit(solution)/shard_map/bidirectional_layer/pallas_call | solution.py:504
Async XLA Ops:
  0.0 11.3 %collective-permute-start.6 = (s32[8,128]{1,0:T(8,128)}, s32[8,128]{1,0:T(8,128)S(1)}, u32[]{:S(2)}, u32[]{:S(2)}) collective-permute-start(s32[8,128]{1,0:T(8,128)} %bitcast.4), channel_id=1, source_target_pairs={{0,28},{4,24},{8,20},{12,16},{16,12},{20,8},{24,4},{28,0},{1,29},{... | collective-permute-start | bytes 12296 | tf_op jit(solution)/shard_map/ppermute | solution.py:493
  6.0 6.1 %collective-permute-start.5 = (s32[8,128]{1,0:T(8,128)}, s32[8,128]{1,0:T(8,128)S(1)}, u32[]{:S(2)}, u32[]{:S(2)}) collective-permute-start(s32[8,128]{1,0:T(8,128)} %bitcast.5), channel_id=1, source_target_pairs={{0,24},{4,28},{8,16},{12,20},{16,8},{20,12},{24,0},{28,4},{1,25},{... | collective-permute-start | bytes 12296 | tf_op jit(solution)/shard_map/ppermute | solution.py:493
  6.2 6.2 %collective-permute-start.4 = (s32[8,128]{1,0:T(8,128)}, s32[8,128]{1,0:T(8,128)S(1)}, u32[]{:S(2)}, u32[]{:S(2)}) collective-permute-start(s32[8,128]{1,0:T(8,128)} %bitcast.6), channel_id=1, source_target_pairs={{0,20},{4,16},{8,28},{12,24},{16,4},{20,0},{24,12},{28,8},{1,21},{... | collective-permute-start | bytes 12296 | tf_op jit(solution)/shard_map/ppermute | solution.py:493
  7.0 5.5 %collective-permute-start.3 = (s32[8,128]{1,0:T(8,128)}, s32[8,128]{1,0:T(8,128)S(1)}, u32[]{:S(2)}, u32[]{:S(2)}) collective-permute-start(s32[8,128]{1,0:T(8,128)} %bitcast.7), channel_id=1, source_target_pairs={{0,16},{4,20},{8,24},{12,28},{16,0},{20,4},{24,8},{28,12},{1,17},{... | collective-permute-start | bytes 12296 | tf_op jit(solution)/shard_map/ppermute | solution.py:493
  8.9 4.7 %collective-permute-start.2 = (s32[8,128]{1,0:T(8,128)}, s32[8,128]{1,0:T(8,128)S(1)}, u32[]{:S(2)}, u32[]{:S(2)}) collective-permute-start(s32[8,128]{1,0:T(8,128)} %bitcast.8), channel_id=1, source_target_pairs={{0,12},{4,8},{8,4},{12,0},{16,28},{20,24},{24,20},{28,16},{1,13},{... | collective-permute-start | bytes 12296 | tf_op jit(solution)/shard_map/ppermute | solution.py:493
  11.3 4.6 %copy-start = (s32[8,128]{1,0:T(8,128)}, s32[8,128]{1,0:T(8,128)S(1)}, u32[]{:S(2)}) copy-start(s32[8,128]{1,0:T(8,128)S(1)} %collective-permute-done.6.others_7_) | copy-start | bytes 12292
  11.3 3.8 %collective-permute-start.1 = (s32[8,128]{1,0:T(8,128)}, s32[8,128]{1,0:T(8,128)S(1)}, u32[]{:S(2)}, u32[]{:S(2)}) collective-permute-start(s32[8,128]{1,0:T(8,128)} %bitcast.9), channel_id=1, source_target_pairs={{0,8},{4,12},{8,0},{12,4},{16,24},{20,28},{24,16},{28,20},{1,9},{5... | collective-permute-start | bytes 12296 | tf_op jit(solution)/shard_map/ppermute | solution.py:493
  12.1 3.8 %copy-start.1 = (s32[8,128]{1,0:T(8,128)}, s32[8,128]{1,0:T(8,128)S(1)}, u32[]{:S(2)}) copy-start(s32[8,128]{1,0:T(8,128)S(1)} %collective-permute-done.5.others_6_) | copy-start | bytes 12292
  12.1 3.8 %collective-permute-start = (s32[8,128]{1,0:T(8,128)}, s32[8,128]{1,0:T(8,128)S(1)}, u32[]{:S(2)}, u32[]{:S(2)}) collective-permute-start(s32[8,128]{1,0:T(8,128)} %bitcast.10), channel_id=1, source_target_pairs={{0,4},{4,0},{8,12},{12,8},{16,20},{20,16},{24,28},{28,24},{1,5},{5... | collective-permute-start | bytes 12296 | tf_op jit(solution)/shard_map/ppermute | solution.py:493
  12.4 3.5 %copy-start.2 = (s32[8,128]{1,0:T(8,128)}, s32[8,128]{1,0:T(8,128)S(1)}, u32[]{:S(2)}) copy-start(s32[8,128]{1,0:T(8,128)S(1)} %collective-permute-done.4.others_5_) | copy-start | bytes 12292
  12.4 3.5 %copy-start.3 = (s32[8,128]{1,0:T(8,128)}, s32[8,128]{1,0:T(8,128)S(1)}, u32[]{:S(2)}) copy-start(s32[8,128]{1,0:T(8,128)S(1)} %collective-permute-done.3.others_4_) | copy-start | bytes 12292
  13.7 2.3 %copy-start.4 = (s32[8,128]{1,0:T(8,128)}, s32[8,128]{1,0:T(8,128)S(1)}, u32[]{:S(2)}) copy-start(s32[8,128]{1,0:T(8,128)S(1)} %collective-permute-done.2.others_3_) | copy-start | bytes 12292
  15.1 0.8 %copy-start.5 = (s32[8,128]{1,0:T(8,128)}, s32[8,128]{1,0:T(8,128)S(1)}, u32[]{:S(2)}) copy-start(s32[8,128]{1,0:T(8,128)S(1)} %collective-permute-done.1.others_2_) | copy-start | bytes 12292
  15.9 0.6 %copy-start.6 = (s32[8,128]{1,0:T(8,128)}, s32[8,128]{1,0:T(8,128)S(1)}, u32[]{:S(2)}) copy-start(s32[8,128]{1,0:T(8,128)S(1)} %collective-permute-done.others_1_) | copy-start | bytes 12292

commit v12 on v11

--- a/solution.py
+++ b/solution.py
@@ -396,11 +396,17 @@
                     x = rows8(sources[d], local)
                     a = rows8(part, 0)
                     states[d] = [a * states[d][w] + rows8(part, 1 + w) * x for w in range(SYM)]
-                    for w in range(SYM):
-                        pair[d][(i * SYM + w) * 8 : (i * SYM + w) * 8 + 8, :] = states[d][w]
+                    odd = (u & 1) == 1
+                    kept = (
+                        jnp.where(odd, states[d][1], states[d][0]),
+                        jnp.where(odd, states[d][3], states[d][2]),
+                        states[d][4],
+                    )
+                    for w in range(3):
+                        pair[d][(i * 3 + w) * 8 : (i * 3 + w) * 8 + 8, :] = kept[w]
                     done.append((d, i, local, x, u, part))
             for d, i, local, x, u, part in done:
-                y = tile_at(pair[d], i * SYM * 8 + u * 8) + skips[d] * x
+                y = tile_at(pair[d], i * 24 + (u >> 1) * 8) + skips[d] * x
                 targets[d][local * 8 : local * 8 + 8, :] = y * rows8(part, 6)
         return tuple(states[0] + states[1])
 

time: 36.3 us -> 36.8 us (1.014)
  Pallas kernels: 19.6 us -> 20.1 us
    pallas_call x1, Pallas kernels: 19.6 us -> 20.1 us  [per_device(): pl.pallas_call(functools.partial(layer_kernel, len(blocks)), out_shape=sd...]
where the time goes in v12:
time: 36.8 us; the launch traced here: 36.6 us
  Pallas kernels  20.1 us (55%)
  starting transfers between devices  12.4 us (34%)
  waiting for transfers between devices  3.46 us (9%)
  local copies, waits for them, and re-layouts  0.57 us (2%)
    pallas_call x1, Pallas kernels, per_device(): pl.pallas_call(functools.partial(layer_kernel, len(blocks)), out_shape=sd...  20.1 us
    ppermute x7, starting transfers between devices, sent(): return lax.ppermute(blocks, 'seq', [(i, i ^ mask) for i in range(own)])  12.4 us
    ppermute x7, waiting for transfers between devices, sent(): return lax.ppermute(blocks, 'seq', [(i, i ^ mask) for i in range(own)])  3.46 us
  transfers between devices with their start and end apart: 7, of which 3 were waited for; matrix products, arithmetic and copies ran while one was open for 0% of the time, Pallas kernels for 0%

profile of v12, /device:TPU:0, one launch (start us, length us, event | category | flops | bytes accessed | tf_op | source)
XLA Modules:
  0.0 36.6 jit_solution(4591294492976110884)
XLA Ops:
  0.0 6.0 %collective-permute-start.6 = (s32[8,128]{1,0:T(8,128)}, s32[8,128]{1,0:T(8,128)S(1)}, u32[]{:S(2)}, u32[]{:S(2)}) collective-permute-start(s32[8,128]{1,0:T(8,128)} %bitcast.4), channel_id=1, source_target_pairs={{0,28},{4,24},{8,20},{12,16},{16,12},{20,8},{24,4},{28,0},{1,29},{... | collective-permute-start | bytes 12296 | tf_op jit(solution)/shard_map/ppermute | solution.py:499
  6.0 0.2 collective-permute-start.5
  6.2 0.7 %collective-permute-start.4 = (s32[8,128]{1,0:T(8,128)}, s32[8,128]{1,0:T(8,128)S(1)}, u32[]{:S(2)}, u32[]{:S(2)}) collective-permute-start(s32[8,128]{1,0:T(8,128)} %bitcast.6), channel_id=1, source_target_pairs={{0,20},{4,16},{8,28},{12,24},{16,4},{20,0},{24,12},{28,8},{1,21},{... | collective-permute-start | bytes 12296 | tf_op jit(solution)/shard_map/ppermute | solution.py:499
  7.0 2.0 %collective-permute-start.3 = (s32[8,128]{1,0:T(8,128)}, s32[8,128]{1,0:T(8,128)S(1)}, u32[]{:S(2)}, u32[]{:S(2)}) collective-permute-start(s32[8,128]{1,0:T(8,128)} %bitcast.7), channel_id=1, source_target_pairs={{0,16},{4,20},{8,24},{12,28},{16,0},{20,4},{24,8},{28,12},{1,17},{... | collective-permute-start | bytes 12296 | tf_op jit(solution)/shard_map/ppermute | solution.py:499
  8.9 2.4 %collective-permute-start.2 = (s32[8,128]{1,0:T(8,128)}, s32[8,128]{1,0:T(8,128)S(1)}, u32[]{:S(2)}, u32[]{:S(2)}) collective-permute-start(s32[8,128]{1,0:T(8,128)} %bitcast.8), channel_id=1, source_target_pairs={{0,12},{4,8},{8,4},{12,0},{16,28},{20,24},{24,20},{28,16},{1,13},{... | collective-permute-start | bytes 12296 | tf_op jit(solution)/shard_map/ppermute | solution.py:499
  11.3 0.0 collective-permute-done.6.others_7_
  11.3 0.0 copy-start
  11.3 0.8 %collective-permute-start.1 = (s32[8,128]{1,0:T(8,128)}, s32[8,128]{1,0:T(8,128)S(1)}, u32[]{:S(2)}, u32[]{:S(2)}) collective-permute-start(s32[8,128]{1,0:T(8,128)} %bitcast.9), channel_id=1, source_target_pairs={{0,8},{4,12},{8,0},{12,4},{16,24},{20,28},{24,16},{28,20},{1,9},{5... | collective-permute-start | bytes 12296 | tf_op jit(solution)/shard_map/ppermute | solution.py:499
  12.1 0.0 collective-permute-done.5.others_6_
  12.1 0.0 copy-start.1
  12.1 0.3 collective-permute-start
  12.4 0.0 collective-permute-done.4.others_5_
  12.4 0.0 copy-start.2
  12.4 0.0 collective-permute-done.3.others_4_
  12.4 0.0 copy-start.3
  12.5 1.2 %collective-permute-done.2.others_3_ = s32[8,128]{1,0:T(8,128)S(1)} collective-permute-done((s32[8,128]{1,0:T(8,128)}, s32[8,128]{1,0:T(8,128)S(1)}, u32[]{:S(2)}, u32[]{:S(2)}) %collective-permute-start.2) | collective-permute-done | bytes 4128 | tf_op jit(solution)/shard_map/ppermute | solution.py:499
  13.7 0.0 copy-start.4
  13.7 1.5 %collective-permute-done.1.others_2_ = s32[8,128]{1,0:T(8,128)S(1)} collective-permute-done((s32[8,128]{1,0:T(8,128)}, s32[8,128]{1,0:T(8,128)S(1)}, u32[]{:S(2)}, u32[]{:S(2)}) %collective-permute-start.1) | collective-permute-done | bytes 4128 | tf_op jit(solution)/shard_map/ppermute | solution.py:499
  15.1 0.0 copy-start.5
  15.1 0.8 %collective-permute-done.others_1_ = s32[8,128]{1,0:T(8,128)S(1)} collective-permute-done((s32[8,128]{1,0:T(8,128)}, s32[8,128]{1,0:T(8,128)S(1)}, u32[]{:S(2)}, u32[]{:S(2)}) %collective-permute-start) | collective-permute-done | bytes 4128 | tf_op jit(solution)/shard_map/ppermute | solution.py:499
  15.9 0.0 copy-start.6
  15.9 0.0 copy-done
  15.9 0.0 copy-done.1
  15.9 0.0 copy-done.2
  15.9 0.0 copy-done.3
  15.9 0.0 copy-done.4
  15.9 0.0 copy-done.5
  16.0 0.5 %copy-done.6 = s32[8,128]{1,0:T(8,128)} copy-done((s32[8,128]{1,0:T(8,128)}, s32[8,128]{1,0:T(8,128)S(1)}, u32[]{:S(2)}) %copy-start.6) | copy-done | bytes 4120
  16.5 20.1 %bidirectional_layer.1 = bf16[1024,256]{1,0:T(8,128)(2,1)} custom-call(s32[1]{0:T(128)} %bitcast.mine, s32[1024]{0:T(1024)} %tok_s.1, bf16[5,256]{1,0:T(8,128)(2,1)} %emb_h.1, bf16[1064,256]{1,0:T(8,128)(2,1)} %bitcast.3, f32[2,4,512]{2,1,0:T(4,128)} %cw_h.1, f32[2,8]{1,0:T(2,128)} %bias_h.1, f32[2,8]{1,0:T(2,128)} %rate_h.1, f32[2,8]{1,0:T(2,128)} %skip_h.1, ...), custom_call_target="tpu_custom_call" | custom-call | flops 8999999488 | bytes 4000000 | tf_op jit(solution)/shard_map/bidirectional_layer/pallas_call | solution.py:510
Async XLA Ops:
  0.0 11.3 %collective-permute-start.6 = (s32[8,128]{1,0:T(8,128)}, s32[8,128]{1,0:T(8,128)S(1)}, u32[]{:S(2)}, u32[]{:S(2)}) collective-permute-start(s32[8,128]{1,0:T(8,128)} %bitcast.4), channel_id=1, source_target_pairs={{0,28},{4,24},{8,20},{12,16},{16,12},{20,8},{24,4},{28,0},{1,29},{... | collective-permute-start | bytes 12296 | tf_op jit(solution)/shard_map/ppermute | solution.py:499
  6.0 6.1 %collective-permute-start.5 = (s32[8,128]{1,0:T(8,128)}, s32[8,128]{1,0:T(8,128)S(1)}, u32[]{:S(2)}, u32[]{:S(2)}) collective-permute-start(s32[8,128]{1,0:T(8,128)} %bitcast.5), channel_id=1, source_target_pairs={{0,24},{4,28},{8,16},{12,20},{16,8},{20,12},{24,0},{28,4},{1,25},{... | collective-permute-start | bytes 12296 | tf_op jit(solution)/shard_map/ppermute | solution.py:499
  6.2 6.2 %collective-permute-start.4 = (s32[8,128]{1,0:T(8,128)}, s32[8,128]{1,0:T(8,128)S(1)}, u32[]{:S(2)}, u32[]{:S(2)}) collective-permute-start(s32[8,128]{1,0:T(8,128)} %bitcast.6), channel_id=1, source_target_pairs={{0,20},{4,16},{8,28},{12,24},{16,4},{20,0},{24,12},{28,8},{1,21},{... | collective-permute-start | bytes 12296 | tf_op jit(solution)/shard_map/ppermute | solution.py:499
  7.0 5.5 %collective-permute-start.3 = (s32[8,128]{1,0:T(8,128)}, s32[8,128]{1,0:T(8,128)S(1)}, u32[]{:S(2)}, u32[]{:S(2)}) collective-permute-start(s32[8,128]{1,0:T(8,128)} %bitcast.7), channel_id=1, source_target_pairs={{0,16},{4,20},{8,24},{12,28},{16,0},{20,4},{24,8},{28,12},{1,17},{... | collective-permute-start | bytes 12296 | tf_op jit(solution)/shard_map/ppermute | solution.py:499
  8.9 4.7 %collective-permute-start.2 = (s32[8,128]{1,0:T(8,128)}, s32[8,128]{1,0:T(8,128)S(1)}, u32[]{:S(2)}, u32[]{:S(2)}) collective-permute-start(s32[8,128]{1,0:T(8,128)} %bitcast.8), channel_id=1, source_target_pairs={{0,12},{4,8},{8,4},{12,0},{16,28},{20,24},{24,20},{28,16},{1,13},{... | collective-permute-start | bytes 12296 | tf_op jit(solution)/shard_map/ppermute | solution.py:499
  11.3 4.6 %copy-start = (s32[8,128]{1,0:T(8,128)}, s32[8,128]{1,0:T(8,128)S(1)}, u32[]{:S(2)}) copy-start(s32[8,128]{1,0:T(8,128)S(1)} %collective-permute-done.6.others_7_) | copy-start | bytes 12292
  11.3 3.8 %collective-permute-start.1 = (s32[8,128]{1,0:T(8,128)}, s32[8,128]{1,0:T(8,128)S(1)}, u32[]{:S(2)}, u32[]{:S(2)}) collective-permute-start(s32[8,128]{1,0:T(8,128)} %bitcast.9), channel_id=1, source_target_pairs={{0,8},{4,12},{8,0},{12,4},{16,24},{20,28},{24,16},{28,20},{1,9},{5... | collective-permute-start | bytes 12296 | tf_op jit(solution)/shard_map/ppermute | solution.py:499
  12.1 3.8 %copy-start.1 = (s32[8,128]{1,0:T(8,128)}, s32[8,128]{1,0:T(8,128)S(1)}, u32[]{:S(2)}) copy-start(s32[8,128]{1,0:T(8,128)S(1)} %collective-permute-done.5.others_6_) | copy-start | bytes 12292
  12.1 3.8 %collective-permute-start = (s32[8,128]{1,0:T(8,128)}, s32[8,128]{1,0:T(8,128)S(1)}, u32[]{:S(2)}, u32[]{:S(2)}) collective-permute-start(s32[8,128]{1,0:T(8,128)} %bitcast.10), channel_id=1, source_target_pairs={{0,4},{4,0},{8,12},{12,8},{16,20},{20,16},{24,28},{28,24},{1,5},{5... | collective-permute-start | bytes 12296 | tf_op jit(solution)/shard_map/ppermute | solution.py:499
  12.4 3.5 %copy-start.2 = (s32[8,128]{1,0:T(8,128)}, s32[8,128]{1,0:T(8,128)S(1)}, u32[]{:S(2)}) copy-start(s32[8,128]{1,0:T(8,128)S(1)} %collective-permute-done.4.others_5_) | copy-start | bytes 12292
  12.4 3.5 %copy-start.3 = (s32[8,128]{1,0:T(8,128)}, s32[8,128]{1,0:T(8,128)S(1)}, u32[]{:S(2)}) copy-start(s32[8,128]{1,0:T(8,128)S(1)} %collective-permute-done.3.others_4_) | copy-start | bytes 12292
  13.7 2.3 %copy-start.4 = (s32[8,128]{1,0:T(8,128)}, s32[8,128]{1,0:T(8,128)S(1)}, u32[]{:S(2)}) copy-start(s32[8,128]{1,0:T(8,128)S(1)} %collective-permute-done.2.others_3_) | copy-start | bytes 12292
  15.1 0.8 %copy-start.5 = (s32[8,128]{1,0:T(8,128)}, s32[8,128]{1,0:T(8,128)S(1)}, u32[]{:S(2)}) copy-start(s32[8,128]{1,0:T(8,128)S(1)} %collective-permute-done.1.others_2_) | copy-start | bytes 12292
  15.9 0.6 %copy-start.6 = (s32[8,128]{1,0:T(8,128)}, s32[8,128]{1,0:T(8,128)S(1)}, u32[]{:S(2)}) copy-start(s32[8,128]{1,0:T(8,128)S(1)} %collective-permute-done.others_1_) | copy-start | bytes 12292
